TPU v7x, 32 devices: a whole 2x2x4 slice. The times are simulated.
32 devices in a mesh: ctx: 8 (over y, x, core), fsdp: 4 (over z).
Axes of the slice: x: 2, y: 2, z: 4, core: 2. Of those that a mesh axis runs over, the one named last changes fastest.
Arguments:
- tokens: bfloat16 [4, 1024, 1024], P('fsdp', 'ctx'), may hold values from -6 to 6
- encoder_states: bfloat16 [4, 256, 1024], P('fsdp', 'ctx'), may hold values from -6 to 6
- grad_out: bfloat16 [4, 1024, 1024], P('fsdp', 'ctx'), may hold values from -8 to 8
- doc_starts: int32 [4, 8], P('fsdp'), may hold values from 0 to 1023, as said below
- source_doc: int32 [4, 8], P('fsdp'), may hold values from 0 to 7, as said below
- source_offsets: int32 [4, 8], P('fsdp'), may hold values from 0 to 255, as said below
- self_qkv: bfloat16 [2, 1024, 3072], P(None, 'fsdp'), may hold values from -0.1875 to 0.1875
- self_out: bfloat16 [2, 1024, 1024], P(None, 'fsdp'), may hold values from -1.5 to 1.5
- cross_q: bfloat16 [2, 1024, 1024], P(None, 'fsdp'), may hold values from -0.1875 to 0.1875
- cross_kv: bfloat16 [2, 1024, 2048], P(None, 'fsdp'), may hold values from -0.1875 to 0.1875
- cross_out: bfloat16 [2, 1024, 1024], P(None, 'fsdp'), may hold values from -1.5 to 1.5
- ffn_in: bfloat16 [2, 1024, 8192], P(None, 'fsdp'), may hold values from -0.1875 to 0.1875
- ffn_out: bfloat16 [2, 8192, 1024], P(None, 'fsdp'), may hold values from -0.0625 to 0.0625
- norm_gains: bfloat16 [2, 3, 1024], P(None, None, 'fsdp'), may hold values from 0.5 to 1.5
- vec_biases: bfloat16 [2, 10, 1024], P(None, None, 'fsdp'), may hold values from -1.25 to 1.25
- fc1_bias: bfloat16 [2, 8192], P(None, 'fsdp'), may hold values from -1.25 to 1.25
Outputs:
- output: bfloat16 [4, 1024, 1024], P('fsdp', 'ctx')
- tokens_grad: float32 [4, 1024, 1024], P('fsdp', 'ctx')
- encoder_grad: float32 [4, 256, 1024], P('fsdp', 'ctx')
- self_qkv_grad: float32 [2, 1024, 3072], P(None, ('ctx', 'fsdp'))
- self_out_grad: float32 [2, 1024, 1024], P(None, ('ctx', 'fsdp'))
- cross_q_grad: float32 [2, 1024, 1024], P(None, ('ctx', 'fsdp'))
- cross_kv_grad: float32 [2, 1024, 2048], P(None, ('ctx', 'fsdp'))
- cross_out_grad: float32 [2, 1024, 1024], P(None, ('ctx', 'fsdp'))
- ffn_in_grad: float32 [2, 1024, 8192], P(None, ('ctx', 'fsdp'))
- ffn_out_grad: float32 [2, 8192, 1024], P(None, ('ctx', 'fsdp'))
- norm_gains_grad: float32 [2, 3, 1024], P(None, None, ('ctx', 'fsdp'))
- vec_biases_grad: float32 [2, 10, 1024], P(None, None, ('ctx', 'fsdp'))
- fc1_bias_grad: float32 [2, 8192], P(None, ('ctx', 'fsdp'))
Inputs may be any that keep to these rules, and one draw needn't show every extreme that they name: `doc_starts`: each stream's 8 starts rise strictly from 0; a document runs to the next start or to the stream's end. Exactly one document of each stream has 896 tokens, and it is the first or the last; the others are shorter. `source_doc`: the document of 896 tokens reads the source document that starts within the first 32 states. `source_offsets`: each stream's 8 starts rise strictly from 0; a source document runs to the next start or to the end of the 256 states. Exactly one starts within the first 32 states and ends within the last 32; the others are shorter than 32.
All inputs are finite; a program needn't handle non-finite values.
Results may differ from a plain program's by a relative error of at most 0.017.
Values may be sent and summed in bfloat16 or wider, within the bound.
No kernel may reach another device: no remote copies, remote signals or barrier semaphores. Data moves between devices by JAX's collectives and lax.ppermute only.
A program may use at most 512 MiB of HBM per device.

v0:
```python
from functools import partial

import jax
import jax.numpy as jnp
from jax import lax
from jax.sharding import PartitionSpec as P

HEADS = 16


EPSILON = 1e-05
NEGATIVE = -1e30


def layer_norm(values, gain_row, offset_row):
    center = values - jnp.mean(values, axis=-1, keepdims=True)
    spread = jnp.mean(center * center, axis=-1, keepdims=True)
    return center * lax.rsqrt(spread + EPSILON) * gain_row + offset_row


def stored_positions(row_index, row_count, dev_count):
    device = row_index // row_count
    offset = row_index % row_count
    half_rows = row_count // 2
    return jnp.where(
        offset < half_rows,
        device * half_rows + offset,
        (2 * dev_count - 1 - device) * half_rows + offset - half_rows,
    )


def group_of(places, starts):
    return jnp.sum((starts[None, :] <= places[:, None]).astype(jnp.int32), axis=1) - 1


def split_heads(values):
    return values.reshape(values.shape[0], HEADS, values.shape[1] // HEADS)


def allowed(geometry, group_block, place_block):
    return (geometry[0][:, None] == group_block[None, :]) & (
        place_block[None, :] <= geometry[2][:, None]
    )


def key_blocks(keyvals, geometry, blocks):
    block_span = keyvals.shape[0] // blocks
    return (
        keyvals.reshape(blocks, block_span, keyvals.shape[1]),
        geometry[1].reshape(blocks, block_span),
        geometry[3].reshape(blocks, block_span),
    )


def attend_forward(queries, keyvals, geometry, blocks):
    feature_width = queries.shape[1]
    row_count = queries.shape[0]
    query_heads = split_heads(queries)
    block_items = key_blocks(keyvals, geometry, blocks)

    def running(state_pair, block_item):
        highest, row_mass = state_pair
        keyval_block, group_block, place_block = block_item
        allowed_mask = allowed(geometry, group_block, place_block)
        scores = jnp.einsum(
            "qhd,khd->hqk",
            query_heads,
            split_heads(keyval_block[:, :feature_width]),
            preferred_element_type=jnp.float32,
        )
        top_new = jnp.maximum(highest, jnp.max(jnp.where(allowed_mask, scores, NEGATIVE), axis=-1))
        row_mass = row_mass * jnp.exp(highest - top_new) + jnp.sum(
            jnp.where(allowed_mask, jnp.exp(scores - top_new[..., None]), 0.0), axis=-1
        )
        return ((top_new, row_mass), None)

    initial = (
        jnp.full((HEADS, row_count), NEGATIVE, jnp.float32),
        jnp.zeros((HEADS, row_count), jnp.float32),
    )
    (highest, row_mass), unused = lax.scan(running, initial, block_items)
    log_mass = highest + jnp.log(row_mass)

    def collect(running_sum, block_item):
        keyval_block, group_block, place_block = block_item
        allowed_mask = allowed(geometry, group_block, place_block)
        scores = jnp.einsum(
            "qhd,khd->hqk",
            query_heads,
            split_heads(keyval_block[:, :feature_width]),
            preferred_element_type=jnp.float32,
        )
        weights_low = jnp.where(allowed_mask, jnp.exp(scores - log_mass[..., None]), 0.0).astype(
            jnp.bfloat16
        )
        added = jnp.einsum(
            "hqk,khd->qhd",
            weights_low,
            split_heads(keyval_block[:, feature_width:]),
            preferred_element_type=jnp.float32,
        )
        return (running_sum + added, None)

    mixed_out, unused = lax.scan(collect, jnp.zeros(query_heads.shape, jnp.float32), block_items)
    return (mixed_out.reshape(row_count, feature_width), log_mass)


def attend_backward(queries, keyvals, geometry, blocks, mixed_out, log_mass, grad_low):
    feature_width = queries.shape[1]
    query_heads = split_heads(queries)
    grad_heads = split_heads(grad_low)
    row_delta = jnp.transpose(
        jnp.sum(split_heads(mixed_out) * grad_heads.astype(jnp.float32), axis=-1)
    )
    block_items = key_blocks(keyvals, geometry, blocks)

    def backward_step(query_grad, block_item):
        keyval_block, group_block, place_block = block_item
        allowed_mask = allowed(geometry, group_block, place_block)
        key_heads = split_heads(keyval_block[:, :feature_width])
        value_heads = split_heads(keyval_block[:, feature_width:])
        scores = jnp.einsum(
            "qhd,khd->hqk", query_heads, key_heads, preferred_element_type=jnp.float32
        )
        weights = jnp.where(allowed_mask, jnp.exp(scores - log_mass[..., None]), 0.0)
        weight_grad = jnp.einsum(
            "qhd,khd->hqk", grad_heads, value_heads, preferred_element_type=jnp.float32
        )
        score_grad = (weights * (weight_grad - row_delta[..., None])).astype(jnp.bfloat16)
        key_grad = jnp.einsum(
            "hqk,qhd->khd", score_grad, query_heads, preferred_element_type=jnp.float32
        )
        value_grad = jnp.einsum(
            "hqk,qhd->khd",
            weights.astype(jnp.bfloat16),
            grad_heads,
            preferred_element_type=jnp.float32,
        )
        query_grad = query_grad + jnp.einsum(
            "hqk,khd->qhd", score_grad, key_heads, preferred_element_type=jnp.float32
        )
        span_rows = keyval_block.shape[0]
        joined = jnp.concatenate(
            [
                key_grad.reshape(span_rows, feature_width),
                value_grad.reshape(span_rows, feature_width),
            ],
            axis=1,
        )
        return (query_grad, joined)

    query_grad, keyval_grad = lax.scan(
        backward_step, jnp.zeros(query_heads.shape, jnp.float32), block_items
    )
    return (
        query_grad.reshape(queries.shape[0], feature_width),
        keyval_grad.reshape(keyvals.shape[0], 2 * feature_width),
    )


def fetch_layer(
    layer_index,
    self_qkv,
    self_out,
    cross_q,
    cross_kv,
    cross_out,
    ffn_in,
    ffn_out,
    norm_gains,
    vec_biases,
    fc1_bias,
):
    fetched = (
        lax.all_gather(self_qkv[layer_index], "fsdp", axis=0, tiled=True),
        lax.all_gather(self_out[layer_index], "fsdp", axis=0, tiled=True),
        lax.all_gather(cross_q[layer_index], "fsdp", axis=0, tiled=True),
        lax.all_gather(cross_kv[layer_index], "fsdp", axis=0, tiled=True),
        lax.all_gather(cross_out[layer_index], "fsdp", axis=0, tiled=True),
        lax.all_gather(ffn_in[layer_index], "fsdp", axis=0, tiled=True),
        lax.all_gather(ffn_out[layer_index], "fsdp", axis=0, tiled=True),
        lax.all_gather(norm_gains[layer_index], "fsdp", axis=1, tiled=True),
        lax.all_gather(vec_biases[layer_index], "fsdp", axis=1, tiled=True),
        lax.all_gather(fc1_bias[layer_index], "fsdp", axis=0, tiled=True),
    )
    return tuple(fetched[:7]) + tuple((piece.astype(jnp.float32) for piece in fetched[7:]))


def run_layer(
    layer_input, enc_rows, weights, self_geometry, cross_geometry, blocks, gathered, attn_saved
):
    w_qkv, w_out, w_cross_q, w_cross_kv, w_cross_out, w_up, w_down, gains, biases, up_bias = weights
    feature_width = layer_input.shape[1]
    zero_half = jnp.zeros_like(biases[4])
    normed_one = layer_norm(layer_input, gains[0], biases[0]).astype(jnp.bfloat16)
    qkv_rows = jnp.dot(normed_one, w_qkv, preferred_element_type=jnp.float32)
    queries = ((qkv_rows[:, :feature_width] + biases[3]) * 0.125).astype(jnp.bfloat16)
    keyvals = (qkv_rows[:, feature_width:] + jnp.concatenate([zero_half, biases[4]])).astype(
        jnp.bfloat16
    )
    enc_proj = jnp.dot(enc_rows, w_cross_kv, preferred_element_type=jnp.float32)
    enc_keyvals = (enc_proj + jnp.concatenate([zero_half, biases[7]])).astype(jnp.bfloat16)
    gathered = (
        lax.all_gather(keyvals, "ctx", axis=0, tiled=True),
        lax.all_gather(enc_keyvals, "ctx", axis=0, tiled=True),
    )
    all_keyvals, all_enc = gathered
    if attn_saved is None:
        self_att, self_lse = attend_forward(queries, all_keyvals, self_geometry, blocks)
    else:
        self_att, self_lse = (attn_saved[0], attn_saved[1])
    self_low = self_att.astype(jnp.bfloat16)
    after_self = (
        layer_input + jnp.dot(self_low, w_out, preferred_element_type=jnp.float32) + biases[5]
    )
    normed_two = layer_norm(after_self, gains[1], biases[1]).astype(jnp.bfloat16)
    cross_queries = (
        (jnp.dot(normed_two, w_cross_q, preferred_element_type=jnp.float32) + biases[6]) * 0.125
    ).astype(jnp.bfloat16)
    if attn_saved is None:
        cross_att, cross_lse = attend_forward(cross_queries, all_enc, cross_geometry, blocks)
    else:
        cross_att, cross_lse = (attn_saved[2], attn_saved[3])
    cross_low = cross_att.astype(jnp.bfloat16)
    after_cross = (
        after_self + jnp.dot(cross_low, w_cross_out, preferred_element_type=jnp.float32) + biases[8]
    )
    normed_three = layer_norm(after_cross, gains[2], biases[2]).astype(jnp.bfloat16)
    hidden_pre = jnp.dot(normed_three, w_up, preferred_element_type=jnp.float32) + up_bias
    hidden_act = jax.nn.gelu(hidden_pre, approximate=False).astype(jnp.bfloat16)
    output = (
        after_cross + jnp.dot(hidden_act, w_down, preferred_element_type=jnp.float32) + biases[9]
    )
    return {
        "normed_one": normed_one,
        "queries": queries,
        "gathered": gathered,
        "all_keyvals": all_keyvals,
        "all_enc": all_enc,
        "self_att": self_att,
        "self_lse": self_lse,
        "self_low": self_low,
        "after_self": after_self,
        "normed_two": normed_two,
        "cross_queries": cross_queries,
        "cross_att": cross_att,
        "cross_lse": cross_lse,
        "cross_low": cross_low,
        "after_cross": after_cross,
        "normed_three": normed_three,
        "hidden_pre": hidden_pre,
        "hidden_act": hidden_act,
        "output": output,
    }


def layer_backward(
    state, grad_next, layer_input, enc_rows, weights, self_geometry, cross_geometry, blocks
):
    w_qkv, w_out, w_cross_q, w_cross_kv, w_cross_out, w_up, w_down, gains, biases, up_bias = weights
    feature_width = layer_input.shape[1]
    ffn_grad = grad_next.astype(jnp.bfloat16)
    grad_down = jnp.einsum(
        "tf,td->fd", state["hidden_act"], ffn_grad, preferred_element_type=jnp.float32
    )
    bias_nine = jnp.sum(ffn_grad.astype(jnp.float32), axis=0)
    act_grad = jnp.einsum("td,fd->tf", ffn_grad, w_down, preferred_element_type=jnp.float32)
    gelu_value, gelu_back = jax.vjp(partial(jax.nn.gelu, approximate=False), state["hidden_pre"])
    pre_grad = gelu_back(act_grad)[0].astype(jnp.bfloat16)
    grad_up = jnp.einsum(
        "td,tf->df", state["normed_three"], pre_grad, preferred_element_type=jnp.float32
    )
    grad_up_bias = jnp.sum(pre_grad.astype(jnp.float32), axis=0)
    normed_grad = jnp.einsum("tf,df->td", pre_grad, w_up, preferred_element_type=jnp.float32)
    norm_value, norm_back = jax.vjp(layer_norm, state["after_cross"], gains[2], biases[2])
    input_grad, gain_two, shift_two = norm_back(normed_grad)
    cross_total = grad_next + input_grad
    cross_grad = cross_total.astype(jnp.bfloat16)
    grad_cross_out = jnp.einsum(
        "td,te->de", state["cross_low"], cross_grad, preferred_element_type=jnp.float32
    )
    bias_eight = jnp.sum(cross_grad.astype(jnp.float32), axis=0)
    cross_att_grad = jnp.einsum(
        "te,de->td", cross_grad, w_cross_out, preferred_element_type=jnp.float32
    ).astype(jnp.bfloat16)
    cq_grad, enc_kv_grad = attend_backward(
        state["cross_queries"],
        state["all_enc"],
        cross_geometry,
        blocks,
        state["cross_att"],
        state["cross_lse"],
        cross_att_grad,
    )
    cq_low = cq_grad.astype(jnp.bfloat16) * 0.125
    grad_cross_q = jnp.einsum(
        "td,te->de", state["normed_two"], cq_low, preferred_element_type=jnp.float32
    )
    bias_six = jnp.sum(cq_low.astype(jnp.float32), axis=0)
    normed_grad = jnp.einsum("te,de->td", cq_low, w_cross_q, preferred_element_type=jnp.float32)
    norm_value, norm_back = jax.vjp(layer_norm, state["after_self"], gains[1], biases[1])
    input_grad, gain_one, shift_one = norm_back(normed_grad)
    self_total = cross_total + input_grad
    self_grad = self_total.astype(jnp.bfloat16)
    grad_out_proj = jnp.einsum(
        "td,te->de", state["self_low"], self_grad, preferred_element_type=jnp.float32
    )
    bias_five = jnp.sum(self_grad.astype(jnp.float32), axis=0)
    self_att_grad = jnp.einsum(
        "te,de->td", self_grad, w_out, preferred_element_type=jnp.float32
    ).astype(jnp.bfloat16)
    query_grad, keyval_grad = attend_backward(
        state["queries"],
        state["all_keyvals"],
        self_geometry,
        blocks,
        state["self_att"],
        state["self_lse"],
        self_att_grad,
    )
    keyval_local, enc_local = (
        lax.psum_scatter(
            keyval_grad.astype(jnp.bfloat16), "ctx", scatter_dimension=0, tiled=True
        ).astype(jnp.float32),
        lax.psum_scatter(
            enc_kv_grad.astype(jnp.bfloat16), "ctx", scatter_dimension=0, tiled=True
        ).astype(jnp.float32),
    )
    keyval_low = keyval_local.astype(jnp.bfloat16)
    enc_low = enc_local.astype(jnp.bfloat16)
    query_low = query_grad.astype(jnp.bfloat16) * 0.125
    qkv_grad = jnp.concatenate([query_low, keyval_low], axis=1)
    grad_qkv = jnp.einsum(
        "td,te->de", state["normed_one"], qkv_grad, preferred_element_type=jnp.float32
    )
    bias_three = jnp.sum(query_low.astype(jnp.float32), axis=0)
    bias_four = jnp.sum(keyval_low[:, feature_width:].astype(jnp.float32), axis=0)
    normed_grad = jnp.einsum("te,de->td", qkv_grad, w_qkv, preferred_element_type=jnp.float32)
    norm_value, norm_back = jax.vjp(layer_norm, layer_input, gains[0], biases[0])
    input_grad, gain_zero, shift_zero = norm_back(normed_grad)
    layer_grad = self_total + input_grad
    grad_cross_kv = jnp.einsum("sd,se->de", enc_rows, enc_low, preferred_element_type=jnp.float32)
    bias_seven = jnp.sum(enc_low[:, feature_width:].astype(jnp.float32), axis=0)
    enc_grad = jnp.einsum("se,de->sd", enc_low, w_cross_kv, preferred_element_type=jnp.float32)
    gain_grads = jnp.stack([gain_zero, gain_one, gain_two])
    bias_grads = jnp.stack(
        [
            shift_zero,
            shift_one,
            shift_two,
            bias_three,
            bias_four,
            bias_five,
            bias_six,
            bias_seven,
            bias_eight,
            bias_nine,
        ]
    )
    grads = (
        grad_qkv,
        grad_out_proj,
        grad_cross_q,
        grad_cross_kv,
        grad_cross_out,
        grad_up,
        grad_down,
        gain_grads,
        bias_grads,
        grad_up_bias,
    )
    return (layer_grad, enc_grad, grads)


def spread_grads(grads):
    (
        grad_qkv,
        grad_out_proj,
        grad_cross_q,
        grad_cross_kv,
        grad_cross_out,
        grad_up,
        grad_down,
        gain_grads,
        bias_grads,
        grad_up_bias,
    ) = grads
    owned = (
        lax.psum_scatter(grad_qkv, ("ctx", "fsdp"), scatter_dimension=0, tiled=True),
        lax.psum_scatter(grad_out_proj, ("ctx", "fsdp"), scatter_dimension=0, tiled=True),
        lax.psum_scatter(grad_cross_q, ("ctx", "fsdp"), scatter_dimension=0, tiled=True),
        lax.psum_scatter(grad_cross_kv, ("ctx", "fsdp"), scatter_dimension=0, tiled=True),
        lax.psum_scatter(grad_cross_out, ("ctx", "fsdp"), scatter_dimension=0, tiled=True),
        lax.psum_scatter(grad_up, ("ctx", "fsdp"), scatter_dimension=0, tiled=True),
        lax.psum_scatter(grad_down, ("ctx", "fsdp"), scatter_dimension=0, tiled=True),
        lax.psum_scatter(gain_grads, ("ctx", "fsdp"), scatter_dimension=1, tiled=True),
        lax.psum_scatter(bias_grads, ("ctx", "fsdp"), scatter_dimension=1, tiled=True),
        lax.psum_scatter(grad_up_bias, ("ctx", "fsdp"), scatter_dimension=0, tiled=True),
    )
    return tuple(owned)


def on_device(
    tokens,
    encoder_states,
    grad_out,
    doc_starts,
    source_doc,
    source_offsets,
    self_qkv,
    self_out,
    cross_q,
    cross_kv,
    cross_out,
    ffn_in,
    ffn_out,
    norm_gains,
    vec_biases,
    fc1_bias,
):
    row_count = tokens.shape[1]
    source_rows = encoder_states.shape[1]
    dev_count = lax.axis_size("ctx")
    device = lax.axis_index("ctx")
    blocks = dev_count // 4
    local_place = stored_positions(
        device * row_count + jnp.arange(row_count, dtype=jnp.int32), row_count, dev_count
    )
    key_place = stored_positions(
        jnp.arange(dev_count * row_count, dtype=jnp.int32), row_count, dev_count
    )
    starts = doc_starts[0]
    query_doc = group_of(local_place, starts)
    key_doc = group_of(key_place, starts)
    doc_slots = jnp.arange(starts.shape[0], dtype=jnp.int32)
    cross_group = jnp.sum(
        jnp.where(query_doc[:, None] == doc_slots[None, :], source_doc[0][None, :], 0), axis=1
    )
    source_group = group_of(jnp.arange(dev_count * source_rows, dtype=jnp.int32), source_offsets[0])
    self_geometry = (query_doc, key_doc, local_place, key_place)
    cross_geometry = (
        cross_group,
        source_group,
        jnp.zeros((row_count,), jnp.int32),
        jnp.zeros((dev_count * source_rows,), jnp.int32),
    )
    enc_rows = encoder_states[0]
    layers = self_qkv.shape[0]
    layer_input = tokens[0].astype(jnp.float32)
    inputs_kept = []
    keys_kept = []
    attn_kept = []
    for layer_index in range(layers):
        weights = fetch_layer(
            layer_index,
            self_qkv,
            self_out,
            cross_q,
            cross_kv,
            cross_out,
            ffn_in,
            ffn_out,
            norm_gains,
            vec_biases,
            fc1_bias,
        )
        state = run_layer(
            layer_input, enc_rows, weights, self_geometry, cross_geometry, blocks, None, None
        )
        inputs_kept.append(layer_input)
        attn_kept.append(
            (state["self_att"], state["self_lse"], state["cross_att"], state["cross_lse"])
        )
        keys_kept.append(None)
        layer_input = state["output"]
    result = layer_input.astype(jnp.bfloat16)
    grad_next = grad_out[0].astype(jnp.float32)
    enc_total = jnp.zeros(enc_rows.shape, jnp.float32)
    collected = [None] * layers
    for layer_index in reversed(range(layers)):
        weights = fetch_layer(
            layer_index,
            self_qkv,
            self_out,
            cross_q,
            cross_kv,
            cross_out,
            ffn_in,
            ffn_out,
            norm_gains,
            vec_biases,
            fc1_bias,
        )
        state = run_layer(
            inputs_kept[layer_index],
            enc_rows,
            weights,
            self_geometry,
            cross_geometry,
            blocks,
            keys_kept[layer_index],
            attn_kept[layer_index],
        )
        grad_next, enc_part, grads = layer_backward(
            state,
            grad_next,
            inputs_kept[layer_index],
            enc_rows,
            weights,
            self_geometry,
            cross_geometry,
            blocks,
        )
        enc_total = enc_total + enc_part
        collected[layer_index] = spread_grads(grads)
    stacked = tuple(
        (
            jnp.stack([collected[layer_index][slot] for layer_index in range(layers)])
            for slot in range(10)
        )
    )
    return (result[None], grad_next[None], enc_total[None]) + stacked


def solution(mesh):
    placed = (
        P("fsdp", "ctx", None),
        P("fsdp", "ctx", None),
        P("fsdp", "ctx", None),
        P("fsdp", None),
        P("fsdp", None),
        P("fsdp", None),
        P(None, "fsdp", None),
        P(None, "fsdp", None),
        P(None, "fsdp", None),
        P(None, "fsdp", None),
        P(None, "fsdp", None),
        P(None, "fsdp", None),
        P(None, "fsdp", None),
        P(None, None, "fsdp"),
        P(None, None, "fsdp"),
        P(None, "fsdp"),
    )
    return jax.shard_map(
        on_device,
        mesh=mesh,
        in_specs=placed,
        out_specs=(
            P("fsdp", "ctx", None),
            P("fsdp", "ctx", None),
            P("fsdp", "ctx", None),
            P(None, ("ctx", "fsdp"), None),
            P(None, ("ctx", "fsdp"), None),
            P(None, ("ctx", "fsdp"), None),
            P(None, ("ctx", "fsdp"), None),
            P(None, ("ctx", "fsdp"), None),
            P(None, ("ctx", "fsdp"), None),
            P(None, ("ctx", "fsdp"), None),
            P(None, None, ("ctx", "fsdp")),
            P(None, None, ("ctx", "fsdp")),
            P(None, ("ctx", "fsdp")),
        ),
        check_vma=False,
    )
```

profile of v0, /device:TPU:0, one launch (start us, length us, event | category | flops | bytes accessed | tf_op | source)
XLA Modules:
  0.0 7382.1 jit_solution(13294190374873054676)
XLA Ops:
  98.5 111.9 %all-gather.47.cloned.1.call-done = bf16[1,1024,3072]{2,1,0:T(8,128)(2,1)} async-done(((bf16[1,256,3072]{2,1,0:T(8,128)(2,1)}), bf16[1,1024,3072]{2,1,0:T(8,128)(2,1)}) %all-gather.47.cloned.1.call-update) | async-done | bytes 6291472 | tf_op jit(solution)/shard_map/all_gather | solution.py:175
  498.0 284.6 %all-gather.57.cloned.1.call-done = bf16[1,1024,8192]{2,1,0:T(8,128)(2,1)} async-done(((bf16[1,256,8192]{2,1,0:T(8,128)(2,1)}), bf16[1,1024,8192]{2,1,0:T(8,128)(2,1)}) %all-gather.57.cloned.1.call-update) | async-done | bytes 16777232 | tf_op jit(solution)/shard_map/all_gather | solution.py:180
  799.6 269.4 %all-gather.59.cloned.1.call-done = bf16[1,8192,1024]{2,1,0:T(8,128)(2,1)} async-done(((bf16[1,2048,1024]{2,1,0:T(8,128)(2,1)}), bf16[1,8192,1024]{2,1,0:T(8,128)(2,1)}) %all-gather.59.cloned.1.call-update) | async-done | bytes 16777232 | tf_op jit(solution)/shard_map/all_gather | solution.py:181
  1078.1 106.6 %all-gather.61.cloned.1.call-done = bf16[1,1024,3072]{2,1,0:T(8,128)(2,1)} async-done(((bf16[1,256,3072]{2,1,0:T(8,128)(2,1)}), bf16[1,1024,3072]{2,1,0:T(8,128)(2,1)}) %all-gather.61.cloned.1.call-update) | async-done | bytes 6291472 | tf_op jit(solution)/shard_map/all_gather | solution.py:175
  1390.1 284.9 %all-gather.71.cloned.1.call-done = bf16[1,1024,8192]{2,1,0:T(8,128)(2,1)} async-done(((bf16[1,256,8192]{2,1,0:T(8,128)(2,1)}), bf16[1,1024,8192]{2,1,0:T(8,128)(2,1)}) %all-gather.71.cloned.1.call-update) | async-done | bytes 16777232 | tf_op jit(solution)/shard_map/all_gather | solution.py:180
  1685.5 275.9 %all-gather.73.cloned.1.call-done = bf16[1,8192,1024]{2,1,0:T(8,128)(2,1)} async-done(((bf16[1,2048,1024]{2,1,0:T(8,128)(2,1)}), bf16[1,8192,1024]{2,1,0:T(8,128)(2,1)}) %all-gather.73.cloned.1.call-update) | async-done | bytes 16777232 | tf_op jit(solution)/shard_map/all_gather | solution.py:181
  2425.5 104.3 %all-reduce.9.cloned.1.call-done = (f32[8192]{0:T(1024)}, f32[8192]{0:T(1024)}) async-done(((f32[8192]{0:T(1024)}, f32[8192]{0:T(1024)}), (f32[8192]{0:T(1024)}, f32[8192]{0:T(1024)})) %all-reduce.9.cloned.1.call-update) | async-done | bytes 65552
  2531.9 135.5 %reduce-scatter.77.cloned.1.call-done = f32[32,10]{1,0:T(8,128)} async-done(((f32[1024,10]{1,0:T(8,128)}), f32[32,10]{1,0:T(8,128)}) %reduce-scatter.77.cloned.1.call-update) | async-done | bytes 1296
  2673.5 126.4 %reduce-scatter.71.cloned.1.call-done = f32[32,3]{1,0:T(8,128)} async-done(((f32[1024,3]{1,0:T(8,128)}), f32[32,3]{1,0:T(8,128)}) %reduce-scatter.71.cloned.1.call-update) | async-done | bytes 400
  2801.2 131.3 %reduce-scatter.75.cloned.1.call-done = f32[32,10]{1,0:T(8,128)} async-done(((f32[1024,10]{1,0:T(8,128)}), f32[32,10]{1,0:T(8,128)}) %reduce-scatter.75.cloned.1.call-update) | async-done | bytes 1296
  2933.9 144.6 %reduce-scatter.57.cloned.1.call-done = f32[32,1024]{1,0:T(8,128)} async-done(((f32[1024,1024]{1,0:T(8,128)}), f32[32,1024]{1,0:T(8,128)}) %reduce-scatter.57.cloned.1.call-update) | async-done | bytes 131088 | tf_op jit(solution)/shard_map/reduce_scatter | solution.py:393
  3078.4 148.6 %reduce-scatter.55.cloned.1.call-done = f32[32,1024]{1,0:T(8,128)} async-done(((f32[1024,1024]{1,0:T(8,128)}), f32[32,1024]{1,0:T(8,128)}) %reduce-scatter.55.cloned.1.call-update) | async-done | bytes 131088 | tf_op jit(solution)/shard_map/reduce_scatter | solution.py:393
  3228.7 147.3 %reduce-scatter.53.cloned.1.call-done = f32[32,1024]{1,0:T(8,128)} async-done(((f32[1024,1024]{1,0:T(8,128)}), f32[32,1024]{1,0:T(8,128)}) %reduce-scatter.53.cloned.1.call-update) | async-done | bytes 131088 | tf_op jit(solution)/shard_map/reduce_scatter | solution.py:391
  3376.1 149.4 %reduce-scatter.51.cloned.1.call-done = f32[32,1024]{1,0:T(8,128)} async-done(((f32[1024,1024]{1,0:T(8,128)}), f32[32,1024]{1,0:T(8,128)}) %reduce-scatter.51.cloned.1.call-update) | async-done | bytes 131088 | tf_op jit(solution)/shard_map/reduce_scatter | solution.py:391
  3527.1 148.0 %reduce-scatter.49.cloned.1.call-done = f32[32,1024]{1,0:T(8,128)} async-done(((f32[1024,1024]{1,0:T(8,128)}), f32[32,1024]{1,0:T(8,128)}) %reduce-scatter.49.cloned.1.call-update) | async-done | bytes 131088 | tf_op jit(solution)/shard_map/reduce_scatter | solution.py:390
  3675.2 148.8 %reduce-scatter.47.cloned.1.call-done = f32[32,1024]{1,0:T(8,128)} async-done(((f32[1024,1024]{1,0:T(8,128)}), f32[32,1024]{1,0:T(8,128)}) %reduce-scatter.47.cloned.1.call-update) | async-done | bytes 131088 | tf_op jit(solution)/shard_map/reduce_scatter | solution.py:390
  3825.7 185.2 %reduce-scatter.69.cloned.1.call-done = f32[32,2048]{1,0:T(8,128)} async-done(((f32[1024,2048]{1,0:T(8,128)}), f32[32,2048]{1,0:T(8,128)}) %reduce-scatter.69.cloned.1.call-update) | async-done | bytes 262160
  4012.5 184.2 %reduce-scatter.67.cloned.1.call-done = f32[32,2048]{1,0:T(8,128)} async-done(((f32[1024,2048]{1,0:T(8,128)}), f32[32,2048]{1,0:T(8,128)}) %reduce-scatter.67.cloned.1.call-update) | async-done | bytes 262160
  4199.1 156.8 %reduce-scatter.45.cloned.1.call-done = f32[32,3072]{1,0:T(8,128)} async-done(((f32[1024,3072]{1,0:T(8,128)}), f32[32,3072]{1,0:T(8,128)}) %reduce-scatter.45.cloned.1.call-update) | async-done | bytes 393232 | tf_op jit(solution)/shard_map/reduce_scatter | solution.py:389
  4355.9 161.8 %reduce-scatter.43.cloned.1.call-done = f32[32,3072]{1,0:T(8,128)} async-done(((f32[1024,3072]{1,0:T(8,128)}), f32[32,3072]{1,0:T(8,128)}) %reduce-scatter.43.cloned.1.call-update) | async-done | bytes 393232 | tf_op jit(solution)/shard_map/reduce_scatter | solution.py:389
  4519.8 711.3 %reduce-scatter.61.cloned.1.call-done = f32[32,8192]{1,0:T(8,128)} async-done(((f32[1024,8192]{1,0:T(8,128)}), f32[32,8192]{1,0:T(8,128)}) %reduce-scatter.61.cloned.1.call-update) | async-done | bytes 1048592 | tf_op jit(solution)/shard_map/reduce_scatter | solution.py:394
  5231.0 713.4 %reduce-scatter.59.cloned.1.call-done = f32[32,8192]{1,0:T(8,128)} async-done(((f32[1024,8192]{1,0:T(8,128)}), f32[32,8192]{1,0:T(8,128)}) %reduce-scatter.59.cloned.1.call-update) | async-done | bytes 1048592 | tf_op jit(solution)/shard_map/reduce_scatter | solution.py:394
  5947.5 710.6 %reduce-scatter.65.cloned.1.call-done = f32[256,1024]{1,0:T(8,128)} async-done(((f32[8192,1024]{1,0:T(8,128)}), f32[256,1024]{1,0:T(8,128)}) %reduce-scatter.65.cloned.1.call-update) | async-done | bytes 1048592 | tf_op jit(solution)/shard_map/reduce_scatter | solution.py:395
  6658.1 713.6 %reduce-scatter.63.cloned.1.call-done = f32[256,1024]{1,0:T(8,128)} async-done(((f32[8192,1024]{1,0:T(8,128)}), f32[256,1024]{1,0:T(8,128)}) %reduce-scatter.63.cloned.1.call-update) | async-done | bytes 1048592 | tf_op jit(solution)/shard_map/reduce_scatter | solution.py:395
  (945 shorter events, 1284.2 us)
Async XLA Ops:
  221.2 561.4 %all-gather.57.cloned.1.call-start = ((), (), s32[]{:S(2)}) async-start(), calls=%async_computation.47 | async-start | bytes 20971520 | tf_op jit(solution)/shard_map/all_gather | solution.py:180
  227.3 841.8 %all-gather.59.cloned.1.call-start = ((), (), s32[]{:S(2)}) async-start(), calls=%async_computation.48 | async-start | bytes 20971520 | tf_op jit(solution)/shard_map/all_gather | solution.py:181
  233.3 951.4 %all-gather.61.cloned.1.call-start = ((), (), s32[]{:S(2)}) async-start(), calls=%async_computation.49 | async-start | bytes 7864320 | tf_op jit(solution)/shard_map/all_gather | solution.py:175
  234.1 974.8 %all-gather.45.cloned.1.call-start = ((), (), s32[]{:S(2)}) async-start(), calls=%async_computation.25 | async-start | bytes 1179648 | tf_op jit(solution)/shard_map/all_gather | solution.py:205
  295.9 951.6 %all-gather.43.cloned.1.call-start = ((), (), s32[]{:S(2)}) async-start(), calls=%async_computation.24 | async-start | bytes 4718592 | tf_op jit(solution)/shard_map/all_gather | solution.py:204
  1192.5 482.4 %all-gather.71.cloned.1.call-start = ((), (), s32[]{:S(2)}) async-start(), calls=%async_computation.54 | async-start | bytes 20971520 | tf_op jit(solution)/shard_map/all_gather | solution.py:180
  1193.1 768.2 %all-gather.73.cloned.1.call-start = ((), (), s32[]{:S(2)}) async-start(), calls=%async_computation.55 | async-start | bytes 20971520 | tf_op jit(solution)/shard_map/all_gather | solution.py:181
  1193.7 922.5 %reduce-scatter.35.cloned.1.call-start = ((), (), s32[]{:S(2)}) async-start(), calls=%async_computation.26 | async-start | bytes 4718592 | tf_op jit(solution)/shard_map/reduce_scatter | solution.py:322
  2224.8 575.0 %reduce-scatter.71.cloned.1.call-start = ((), (), s32[]{:S(2)}) async-start(), calls=%async_computation.58 | async-start | bytes 540672
  2278.8 653.6 %reduce-scatter.75.cloned.1.call-start = ((), (), s32[]{:S(2)}) async-start(), calls=%async_computation.60 | async-start | bytes 540672
  2280.1 798.3 %reduce-scatter.57.cloned.1.call-start = ((), (), s32[]{:S(2)}) async-start(), calls=%async_computation.37 | async-start | bytes 4325376 | tf_op jit(solution)/shard_map/reduce_scatter | solution.py:393
  2282.9 944.1 %reduce-scatter.55.cloned.1.call-start = ((), (), s32[]{:S(2)}) async-start(), calls=%async_computation.36 | async-start | bytes 4325376 | tf_op jit(solution)/shard_map/reduce_scatter | solution.py:393
  2286.1 1090.0 %reduce-scatter.53.cloned.1.call-start = ((), (), s32[]{:S(2)}) async-start(), calls=%async_computation.35 | async-start | bytes 4325376 | tf_op jit(solution)/shard_map/reduce_scatter | solution.py:391
  2289.0 1236.4 %reduce-scatter.51.cloned.1.call-start = ((), (), s32[]{:S(2)}) async-start(), calls=%async_computation.34 | async-start | bytes 4325376 | tf_op jit(solution)/shard_map/reduce_scatter | solution.py:391
  2292.1 1383.1 %reduce-scatter.49.cloned.1.call-start = ((), (), s32[]{:S(2)}) async-start(), calls=%async_computation.33 | async-start | bytes 4325376 | tf_op jit(solution)/shard_map/reduce_scatter | solution.py:390
  2294.9 1529.2 %reduce-scatter.47.cloned.1.call-start = ((), (), s32[]{:S(2)}) async-start(), calls=%async_computation.32 | async-start | bytes 4325376 | tf_op jit(solution)/shard_map/reduce_scatter | solution.py:390
  2297.7 1713.1 %reduce-scatter.69.cloned.1.call-start = ((), (), s32[]{:S(2)}) async-start(), calls=%async_computation.57 | async-start | bytes 8650752
  2311.6 1885.1 %reduce-scatter.67.cloned.1.call-start = ((), (), s32[]{:S(2)}) async-start(), calls=%async_computation.56 | async-start | bytes 8650752
  2326.3 2029.6 %reduce-scatter.45.cloned.1.call-start = ((), (), s32[]{:S(2)}) async-start(), calls=%async_computation.31 | async-start | bytes 12976128 | tf_op jit(solution)/shard_map/reduce_scatter | solution.py:389
  2333.9 2183.8 %reduce-scatter.43.cloned.1.call-start = ((), (), s32[]{:S(2)}) async-start(), calls=%async_computation.30 | async-start | bytes 12976128 | tf_op jit(solution)/shard_map/reduce_scatter | solution.py:389
  2341.4 2889.6 %reduce-scatter.61.cloned.1.call-start = ((), (), s32[]{:S(2)}) async-start(), calls=%async_computation.39 | async-start | bytes 34603008 | tf_op jit(solution)/shard_map/reduce_scatter | solution.py:394
  2356.5 3587.9 %reduce-scatter.59.cloned.1.call-start = ((), (), s32[]{:S(2)}) async-start(), calls=%async_computation.38 | async-start | bytes 34603008 | tf_op jit(solution)/shard_map/reduce_scatter | solution.py:394
  2371.6 4286.5 %reduce-scatter.65.cloned.1.call-start = ((), (), s32[]{:S(2)}) async-start(), calls=%async_computation.41 | async-start | bytes 34603008 | tf_op jit(solution)/shard_map/reduce_scatter | solution.py:395
  2392.5 4979.2 %reduce-scatter.63.cloned.1.call-start = ((), (), s32[]{:S(2)}) async-start(), calls=%async_computation.40 | async-start | bytes 34603008 | tf_op jit(solution)/shard_map/reduce_scatter | solution.py:395
  (216 other events, 20288.6 us)
Sparse Core Ops, SparseCore 0:
  96.5 113.9 all-gather.46
  497.2 285.4 all-gather.56
  784.0 284.9 all-gather.58
  1389.1 285.7 all-gather.70
  1676.3 284.9 all-gather.72
  2273.7 134.0 reduce-scatter.72
  2414.9 114.8 all-reduce.8
  2532.1 135.2 reduce-scatter.76
  2669.4 130.3 reduce-scatter.70
  2802.0 130.4 reduce-scatter.74
  2934.7 143.6 reduce-scatter.56
  3080.7 146.2 reduce-scatter.54
  3229.2 146.8 reduce-scatter.52
  3378.3 147.0 reduce-scatter.50
  3527.7 147.4 reduce-scatter.48
  3677.3 146.6 reduce-scatter.46
  3826.3 184.5 reduce-scatter.68
  4013.2 183.4 reduce-scatter.66
  4202.6 153.3 reduce-scatter.44
  4362.8 154.8 reduce-scatter.42
  4520.0 711.0 reduce-scatter.60
  5233.2 711.2 reduce-scatter.58
  5946.8 711.2 reduce-scatter.64
  6660.4 711.2 reduce-scatter.62
  (17 shorter events, 836.8 us)
where the time goes:
time: 7390 us; the launch traced here: 7380 us
  waiting for transfers between devices  6710 us (91%)
  matrix products  344 us (5%)
  local copies, waits for them, and re-layouts  171 us (2%)
    reduce_scatter x2, waiting for transfers between devices, spread_grads(): lax.psum_scatter(grad_up, ('ctx', 'fsdp'), scatter_dimension=0, tiled=True)  1420 us
    reduce_scatter x2, waiting for transfers between devices, spread_grads(): lax.psum_scatter(grad_down, ('ctx', 'fsdp'), scatter_dimension=0, tiled=T...  1420 us
    unnamed x48, waiting for transfers between devices  872 us
    all_gather x2, waiting for transfers between devices, fetch_layer(): lax.all_gather(ffn_in[layer_index], 'fsdp', axis=0, tiled=True)  569 us
    all_gather x2, waiting for transfers between devices, fetch_layer(): lax.all_gather(ffn_out[layer_index], 'fsdp', axis=0, tiled=True)  545 us
    reduce_scatter x2, waiting for transfers between devices, spread_grads(): lax.psum_scatter(grad_qkv, ('ctx', 'fsdp'), scatter_dimension=0, tiled=True)  319 us
    reduce_scatter x2, waiting for transfers between devices, spread_grads(): lax.psum_scatter(grad_out_proj, ('ctx', 'fsdp'), scatter_dimension=0, til...  297 us
    reduce_scatter x2, waiting for transfers between devices, spread_grads(): lax.psum_scatter(grad_cross_q, ('ctx', 'fsdp'), scatter_dimension=0, tile...  297 us
  transfers between devices with their start and end apart: 41, of which 38 were waited for; matrix products, arithmetic and copies ran while one was open for 6% of the time, Pallas kernels for 0%

commit v1 on v0

v1 whole, which is shorter than its diff:
```python
from functools import partial

import jax
import jax.numpy as jnp
from jax import lax
from jax.experimental import pallas as pl
from jax.experimental.pallas import tpu as pltpu
from jax.sharding import PartitionSpec as P

HEADS = 16
EPSILON = 1e-05
NEGATIVE = -1e30
F32 = jnp.float32
LOW = jnp.bfloat16


def swap(values, bits):
    count = lax.axis_size("ctx")
    return lax.ppermute(values, "ctx", [(i, i ^ bits) for i in range(count)])


def gather_slots(rows):
    count = lax.axis_size("ctx")
    if count == 8:
        near_x, near_y = swap(rows, 2), swap(rows, 4)
        half = rows.shape[0] // 2
        far = jnp.concatenate([swap(near_x[:half], 4), swap(near_y[half:], 2)])
        blocks = []
        for block in (rows, near_x, near_y, far):
            blocks += [block, swap(block, 1)]
        return jnp.stack(blocks)
    stack = rows[None]
    bit = 1
    while bit < count:
        stack = jnp.concatenate([stack, swap(stack, bit)])
        bit *= 2
    return stack


def reduce_slots(parts, kind=LOW):
    count = lax.axis_size("ctx")
    if count == 8 and parts.shape[1] % 32 == 0:
        other = swap(parts[1::2].astype(kind), 1)
        chip = parts[0::2].astype(F32) + other.astype(F32)
        half = parts.shape[1] // 2
        far = chip[3].astype(kind)
        far_x, far_y = swap(far[:half], 2), swap(far[half:], 4)
        to_x = jnp.concatenate([chip[1][:half], chip[1][half:] + far_y.astype(F32)]).astype(kind)
        to_y = jnp.concatenate([chip[2][:half] + far_x.astype(F32), chip[2][half:]]).astype(kind)
        return chip[0] + swap(to_x, 2).astype(F32) + swap(to_y, 4).astype(F32)
    total = parts.astype(F32)
    bit = count // 2
    while bit:
        total = total[:bit] + swap(total[bit : 2 * bit].astype(kind), bit).astype(F32)
        bit //= 2
    return total[0]


def exchange_slots(parts):
    return jnp.stack([parts[0]] + [swap(parts[k], k) for k in range(1, parts.shape[0])])


def turn(values, axis):
    count = lax.axis_size("ctx")
    here = lax.axis_index("ctx")
    width = values.shape[axis] // count
    return jnp.concatenate(
        [
            lax.dynamic_slice_in_dim(values, (here ^ k) * width, width, axis)
            for k in range(count)
        ],
        axis=axis,
    )


def gather_planes(values):
    return lax.all_gather(values, "fsdp", axis=0, tiled=True)


def reduce_planes(parts):
    return lax.psum_scatter(parts, "fsdp", scatter_dimension=0, tiled=False)


def attend_forward_kernel(head_width, q_ref, k_ref, v_ref, low_ref, high_ref, place_ref, o_ref, lse_ref):
    place = place_ref[...]
    mask = (place >= low_ref[...]) & (place <= high_ref[...])
    outs, masses = [], []
    for start in range(0, q_ref.shape[1], head_width):
        span = slice(start, start + head_width)
        scores = lax.dot_general(
            q_ref[:, span], k_ref[:, span], (((1,), (1,)), ((), ())), preferred_element_type=F32
        )
        scores = jnp.where(mask, scores, NEGATIVE)
        top = jnp.max(scores, axis=1, keepdims=True)
        raised = jnp.exp(scores - top)
        mass = jnp.sum(raised, axis=1, keepdims=True)
        weights = (raised * (1.0 / mass)).astype(LOW)
        outs.append(jnp.dot(weights, v_ref[:, span], preferred_element_type=F32))
        masses.append(top + jnp.log(mass))
    o_ref[...] = jnp.concatenate(outs, axis=1).astype(LOW)
    lse_ref[0] = jnp.concatenate(masses, axis=1)


def attend_backward_kernel(
    head_width, q_ref, k_ref, v_ref, d_ref, lse_ref, low_ref, high_ref, place_ref, dq_ref, dk_ref, dv_ref
):
    @pl.when(pl.program_id(1) == 0)
    def _():
        dk_ref[...] = jnp.zeros_like(dk_ref)
        dv_ref[...] = jnp.zeros_like(dv_ref)

    place = place_ref[...]
    mask = (place >= low_ref[...]) & (place <= high_ref[...])
    dqs, dks, dvs = [], [], []
    for index, start in enumerate(range(0, q_ref.shape[1], head_width)):
        span = slice(start, start + head_width)
        q, k, v, d = q_ref[:, span], k_ref[:, span], v_ref[:, span], d_ref[:, span]
        across = (((1,), (1,)), ((), ()))
        down = (((0,), (0,)), ((), ()))
        scores = lax.dot_general(q, k, across, preferred_element_type=F32)
        weights = jnp.where(mask, jnp.exp(scores - lse_ref[0][:, index : index + 1]), 0.0)
        weight_grad = lax.dot_general(d, v, across, preferred_element_type=F32)
        delta = jnp.sum(weights * weight_grad, axis=1, keepdims=True)
        score_grad = (weights * (weight_grad - delta)).astype(LOW)
        dqs.append(jnp.dot(score_grad, k, preferred_element_type=F32))
        dks.append(lax.dot_general(score_grad, q, down, preferred_element_type=F32))
        dvs.append(lax.dot_general(weights.astype(LOW), d, down, preferred_element_type=F32))
    dq_ref[...] = (jnp.concatenate(dqs, axis=1).astype(LOW).astype(F32) * 0.125).astype(LOW)
    dk_ref[...] += jnp.concatenate(dks, axis=1)
    dv_ref[...] += jnp.concatenate(dvs, axis=1)


def attention_specs(rows, keys, width, head_width):
    block = min(128, width)
    step = min(rows, 256 if keys <= 1024 else 128)
    grid = (width // block, rows // step)
    q_spec = pl.BlockSpec((step, block), lambda j, i: (i, j))
    k_spec = pl.BlockSpec((keys, block), lambda j, i: (0, j))
    edge_spec = pl.BlockSpec((step, 1), lambda j, i: (i, 0))
    place_spec = pl.BlockSpec((1, keys), lambda j, i: (0, 0))
    lse_spec = pl.BlockSpec((1, step, block // head_width), lambda j, i: (j, i, 0))
    lse_shape = jax.ShapeDtypeStruct((width // block, rows, block // head_width), F32)
    params = pltpu.CompilerParams(vmem_limit_bytes=48 * 2**20)
    return grid, q_spec, k_spec, edge_spec, place_spec, lse_spec, lse_shape, params


def attend_forward(q, k, v, bounds, head_width):
    rows, width = q.shape
    keys = k.shape[0]
    grid, q_spec, k_spec, edge_spec, place_spec, lse_spec, lse_shape, params = attention_specs(
        rows, keys, width, head_width
    )
    return pl.pallas_call(
        partial(attend_forward_kernel, head_width),
        grid=grid,
        in_specs=[q_spec, k_spec, k_spec, edge_spec, edge_spec, place_spec],
        out_specs=[q_spec, lse_spec],
        out_shape=[jax.ShapeDtypeStruct((rows, width), LOW), lse_shape],
        compiler_params=params,
        cost_estimate=pl.CostEstimate(
            flops=4 * rows * keys * width,
            bytes_accessed=4 * (rows + keys) * width,
            transcendentals=rows * keys * width // head_width,
        ),
    )(q, k, v, *bounds)


def attend_backward(q, k, v, d, lse, bounds, head_width):
    rows, width = q.shape
    keys = k.shape[0]
    grid, q_spec, k_spec, edge_spec, place_spec, lse_spec, lse_shape, params = attention_specs(
        rows, keys, width, head_width
    )
    return pl.pallas_call(
        partial(attend_backward_kernel, head_width),
        grid=grid,
        in_specs=[q_spec, k_spec, k_spec, q_spec, lse_spec, edge_spec, edge_spec, place_spec],
        out_specs=[q_spec, k_spec, k_spec],
        out_shape=[
            jax.ShapeDtypeStruct((rows, width), LOW),
            jax.ShapeDtypeStruct((keys, width), F32),
            jax.ShapeDtypeStruct((keys, width), F32),
        ],
        compiler_params=params,
        cost_estimate=pl.CostEstimate(
            flops=10 * rows * keys * width,
            bytes_accessed=6 * (rows + 2 * keys) * width,
            transcendentals=rows * keys * width // head_width,
        ),
    )(q, k, v, d, lse, *bounds)


def layer_norm(values, gain_row, offset_row):
    center = values - jnp.mean(values, axis=-1, keepdims=True)
    spread = jnp.mean(center * center, axis=-1, keepdims=True)
    return center * lax.rsqrt(spread + EPSILON) * gain_row + offset_row


def layer_norm_back(values, gain_row, grad):
    center = values - jnp.mean(values, axis=-1, keepdims=True)
    inverse = lax.rsqrt(jnp.mean(center * center, axis=-1, keepdims=True) + EPSILON)
    normed = center * inverse
    scaled = grad * gain_row
    back = inverse * (
        scaled
        - jnp.mean(scaled, axis=-1, keepdims=True)
        - normed * jnp.mean(scaled * normed, axis=-1, keepdims=True)
    )
    return back, jnp.sum(grad * normed, axis=0), jnp.sum(grad, axis=0)


def dot(left, right):
    return jnp.dot(left, right, preferred_element_type=F32)


def dot_t(left, right):
    return lax.dot_general(left, right, (((1,), (1,)), ((), ())), preferred_element_type=F32)


def t_dot(left, right):
    return lax.dot_general(left, right, (((0,), (0,)), ((), ())), preferred_element_type=F32)


def column_sum(values):
    return jnp.sum(values.astype(F32), axis=0)


def stored_positions(row_index, row_count, dev_count):
    device = row_index // row_count
    offset = row_index % row_count
    half_rows = row_count // 2
    return jnp.where(
        offset < half_rows,
        device * half_rows + offset,
        (2 * dev_count - 1 - device) * half_rows + offset - half_rows,
    )


def ranges_of(starts, length):
    return starts, jnp.concatenate([starts[1:], jnp.full((1,), length, jnp.int32)]) - 1


def group_of(places, starts):
    return jnp.sum((starts[None, :] <= places[:, None]).astype(jnp.int32), axis=1) - 1


def pick(table, index):
    slots = jnp.arange(table.shape[0], dtype=jnp.int32)
    return jnp.sum(jnp.where(index[:, None] == slots[None, :], table[None, :], 0), axis=1)


def on_device(
    tokens,
    encoder_states,
    grad_out,
    doc_starts,
    source_doc,
    source_offsets,
    self_qkv,
    self_out,
    cross_q,
    cross_kv,
    cross_out,
    ffn_in,
    ffn_out,
    norm_gains,
    vec_biases,
    fc1_bias,
):
    n, m = lax.axis_size("ctx"), lax.axis_size("fsdp")
    c, f = lax.axis_index("ctx"), lax.axis_index("fsdp")
    layers = self_qkv.shape[0]
    rows, width = tokens.shape[1:]
    source_rows = encoder_states.shape[1]
    length, source_length = n * rows, n * source_rows
    hidden = ffn_out.shape[1] * m
    head_width = width // HEADS
    groups = min(n, HEADS)
    split = n // groups
    group, part = c // split, c % split
    own = width // groups
    col = width // n
    piece = hidden // (n * m)
    high_c, low_c = c // m, c % m

    slot_rows = ((c ^ jnp.arange(n, dtype=jnp.int32)) * rows)[:, None] + jnp.arange(
        rows, dtype=jnp.int32
    )[None, :]
    places = stored_positions(slot_rows.reshape(-1), rows, n)
    own_places = places.reshape(n // split, split, rows)[:, 0].reshape(-1)
    doc_low, doc_high = ranges_of(doc_starts[0], length)
    self_bounds = (
        pick(doc_low, group_of(own_places, doc_starts[0]))[:, None],
        own_places[:, None],
        places[None, :],
    )
    source_low, source_high = ranges_of(source_offsets[0], source_length)
    read_doc = pick(source_doc[0], group_of(places[:rows], doc_starts[0]))
    cross_bounds = (
        pick(source_low, read_doc)[:, None],
        pick(source_high, read_doc)[:, None],
        jnp.arange(source_length, dtype=jnp.int32)[None, :],
    )

    def columns(array, start, count):
        return lax.dynamic_slice_in_dim(array, start, count, 1)

    def fetch_self(layer):
        blocks = [columns(self_qkv[layer], i * width + group * own, own) for i in range(3)]
        return gather_planes(jnp.concatenate(blocks, axis=1))

    def fetch_cross(layer):
        kv = [columns(cross_kv[layer], i * width + c * col, col) for i in range(2)]
        got = gather_planes(
            jnp.concatenate(
                kv + [columns(cross_q[layer], c * col, col), columns(cross_out[layer], c * col, col)],
                axis=1,
            )
        )
        return got[:, : 2 * col], got[:, 2 * col :]

    def fetch_ffn(layer):
        up = ffn_in[layer].reshape(ffn_in.shape[1], m, n, piece)
        blocks = [
            lax.dynamic_index_in_dim(up[:, j], m * high_c + (j + low_c) % m, 1, False)
            for j in range(m)
        ]
        up = jnp.concatenate(blocks, axis=1)
        start = (m * high_c + (f + low_c) % m) * piece
        down = lax.dynamic_slice_in_dim(ffn_out[layer], start, piece, 0)
        return gather_planes(up), gather_planes(down)

    def fetch_out():
        here = self_out.shape[1]
        start = group * own
        source = start // here
        got = lax.dynamic_slice_in_dim(self_out, start % here, own, 1)
        bit = 1
        while bit < m:
            pairs = []
            for device in range(n):
                at = (device // split) * own // here
                for near in range(bit):
                    pairs.append((device * m + (at ^ near), device * m + (at ^ near ^ bit)))
            arrived = lax.ppermute(got, ("ctx", "fsdp"), pairs)
            got = jnp.where((f ^ source) // bit == 1, arrived, got)
            bit *= 2
        return got

    vectors = jnp.concatenate([norm_gains, vec_biases], axis=1).astype(LOW)
    vectors = lax.all_gather(vectors, "fsdp", axis=2, tiled=True).astype(F32)
    gains, biases = vectors[:, :3], vectors[:, 3:]
    up_bias = lax.dynamic_slice_in_dim(
        fc1_bias, (m * high_c + (f + low_c) % m) * piece, piece, 1
    )
    up_bias = lax.all_gather(up_bias, "fsdp", axis=1, tiled=True).astype(F32)
    w_out = fetch_out()
    weights = []
    for layer in range(layers):
        w_qkv = fetch_self(layer)
        w_kv, w_cross = fetch_cross(layer)
        w_up, w_down = fetch_ffn(layer)
        weights.append((w_qkv, w_out[layer], w_kv, w_cross, w_up, w_down))

    def own_slots(values):
        if split == 1:
            return values
        shaped = values.reshape((n // split, split, rows) + values.shape[1:])
        return shaped[:, 0].reshape((-1,) + values.shape[1:])

    def slots_of(values):
        shaped = values.reshape(n // split, 1, rows, values.shape[1])
        if split > 1:
            shaped = jnp.pad(shaped, ((0, 0), (0, split - 1), (0, 0), (0, 0)))
        return shaped.reshape(n, rows, values.shape[1])

    def share(parts):
        if split == 1:
            return parts[0]
        total = lax.dynamic_index_in_dim(parts, part, 0, False).astype(F32)
        for other in range(1, split):
            term = lax.dynamic_index_in_dim(parts, part ^ other, 0, False)
            total = total + swap(term, other).astype(F32)
        return total

    encoder_all = gather_slots(encoder_states[0]).reshape(source_length, width)
    grad_low = grad_out[0]

    x = tokens[0].astype(F32)
    kept = []
    for layer in range(layers):
        w_qkv, w_self_out, w_kv, w_cross, w_up, w_down = weights[layer]
        gain, bias = gains[layer], biases[layer]
        enc = dot(encoder_all, w_kv)
        enc = enc + jnp.concatenate([jnp.zeros((col,), F32), lax.dynamic_slice_in_dim(bias[7], c * col, col)])
        enc = turn(enc.astype(LOW), 0)
        enc_all = gather_slots(enc)
        ek = turn(jnp.concatenate([enc_all[k][:, :col] for k in range(n)], axis=1), 1)
        ev = turn(jnp.concatenate([enc_all[k][:, col:] for k in range(n)], axis=1), 1)
        cross_full = gather_slots(w_cross.T)
        cross_q_t = turn(cross_full[:, :col].reshape(width, width), 0)
        cross_out_t = turn(cross_full[:, col:].reshape(width, width), 0)

        h1 = layer_norm(x, gain[0], bias[0]).astype(LOW)
        h1_all = gather_slots(h1).reshape(length, width)
        z = dot(h1_all, w_qkv)
        q = own_slots((z[:, :own] + lax.dynamic_slice_in_dim(bias[3], group * own, own)) * 0.125)
        q = q.astype(LOW)
        k = z[:, own : 2 * own].astype(LOW)
        v = (z[:, 2 * own :] + lax.dynamic_slice_in_dim(bias[4], group * own, own)).astype(LOW)
        a, self_lse = attend_forward(q, k, v, self_bounds, head_width)
        x1 = x + reduce_slots(slots_of(dot(a, w_self_out))) + bias[5]
        h2 = layer_norm(x1, gain[1], bias[1]).astype(LOW)
        cq = ((dot_t(h2, cross_q_t) + bias[6]) * 0.125).astype(LOW)
        mixed, cross_lse = attend_forward(cq, ek, ev, cross_bounds, head_width)
        x2 = x1 + dot_t(mixed, cross_out_t) + bias[8]
        h3 = layer_norm(x2, gain[2], bias[2]).astype(LOW)
        h3_all = gather_slots(h3).reshape(length, width)
        u = dot(h3_all, w_up) + up_bias[layer]
        g = jax.nn.gelu(u, approximate=False).astype(LOW)
        y = x2 + reduce_slots(dot(g, w_down).reshape(n, rows, width)) + bias[9]
        kept.append(
            (x, x1, x2, h1_all, q, k, v, a, self_lse, h2, cq, ek, ev, mixed, cross_lse)
            + (h3_all, u, g, cross_q_t, cross_out_t)
        )
        x = y
    result = x.astype(LOW)

    grad_x = grad_low.astype(F32)
    enc_total = jnp.zeros((source_length, width), F32)
    grads = [None] * layers
    vec_rows = [None] * layers
    for layer in reversed(range(layers)):
        w_qkv, w_self_out, w_kv, w_cross, w_up, w_down = weights[layer]
        x, x1, x2, h1_all, q, k, v, a, self_lse, h2, cq, ek, ev, mixed, cross_lse = kept[layer][:15]
        h3_all, u, g, cross_q_t, cross_out_t = kept[layer][15:]
        gain = gains[layer]
        e3 = grad_x.astype(LOW)
        e3_all = gather_slots(e3).reshape(length, width)
        act_grad = dot_t(e3_all, w_down)
        unused, gelu_back = jax.vjp(partial(jax.nn.gelu, approximate=False), u)
        du = gelu_back(act_grad)[0].astype(LOW)
        dh3 = reduce_slots(dot_t(du, w_up).reshape(n, rows, width))
        down_grad = t_dot(g, e3_all).astype(LOW).reshape(m, piece, width)
        to_plane = [
            lax.dynamic_index_in_dim(down_grad, (p - low_c) % m, 0, False) for p in range(m)
        ]
        down_grad = jnp.stack(to_plane)
        up_grad = t_dot(h3_all, du).astype(LOW)
        up_grad = up_grad.reshape(n, m, width // (n * m), m * piece).transpose(1, 0, 2, 3)
        up_grad = up_grad.reshape(m, width // m, m * piece)
        fc1_grad = column_sum(du).reshape(m, piece)
        fc1_grad = jnp.stack(
            [lax.dynamic_index_in_dim(fc1_grad, (p - low_c) % m, 0, False) for p in range(m)]
        )
        back, gain_two, shift_two = layer_norm_back(x2, gain[2], dh3)
        dx2 = grad_x + back
        e2 = dx2.astype(LOW)
        d_mixed = dot(e2, cross_out_t).astype(LOW)
        dcq, dek, dev = attend_backward(cq, ek, ev, d_mixed, cross_lse, cross_bounds, head_width)
        dh2 = dot(dcq, cross_q_t)
        back, gain_one, shift_one = layer_norm_back(x1, gain[1], dh2)
        dx1 = dx2 + back
        e1 = dx1.astype(LOW)
        e1_all = gather_slots(e1).reshape(length, width)
        e1_own = own_slots(e1_all)
        d_a = dot_t(e1_own, w_self_out).astype(LOW)
        dq, dk, dv = attend_backward(q, k, v, d_a, self_lse, self_bounds, head_width)
        dkv = jnp.concatenate([dk, dv], axis=1).astype(LOW)
        if split > 1:
            shaped = dkv.reshape(n // split, split, rows, 2 * own)
            total = shaped[:, 0].astype(F32)
            for other in range(1, split):
                total = total + swap(shaped[:, other], other).astype(F32)
            dkv = total.astype(LOW).reshape(-1, 2 * own)
        dqkv = jnp.concatenate([dq, dkv], axis=1)
        dh1 = reduce_slots(slots_of(dot_t(dqkv, w_qkv)))
        back, gain_zero, shift_zero = layer_norm_back(x, gain[0], dh1)
        grad_x = dx1 + back

        dek_slots = turn(dek.astype(LOW), 1).reshape(source_length, n, col)
        dev_slots = turn(dev.astype(LOW), 1).reshape(source_length, n, col)
        dkv_cross = jnp.concatenate([dek_slots, dev_slots], axis=2).transpose(1, 0, 2)
        dkv_cross = reduce_slots(dkv_cross).astype(LOW)
        dkv_cross = turn(dkv_cross, 0)
        enc_total = enc_total + dot_t(dkv_cross, w_kv)
        kv_grad = t_dot(encoder_all, dkv_cross).astype(LOW)

        q_grad = t_dot(turn(h2, 1), dcq).reshape(n, col, width)
        out_grad = t_dot(turn(mixed, 1), e2).reshape(n, col, width)
        cross_grad = reduce_slots(jnp.concatenate([q_grad, out_grad], axis=1))
        cross_grad = cross_grad.reshape(2, m, col // m, width).transpose(1, 0, 2, 3)
        cross_grad = cross_grad.reshape(m, 2 * col // m, width).astype(LOW)

        qkv_grad = t_dot(own_slots(h1_all), dqkv).astype(LOW)
        qkv_grad = share(qkv_grad.reshape(width, 3, split, own // split).transpose(2, 0, 1, 3))
        qkv_grad = qkv_grad.astype(LOW).reshape(width, 3 * col)
        o_grad = share(t_dot(a, e1_own).astype(LOW).reshape(split, own // split, width))
        o_grad = o_grad.reshape(m, col // m, width).astype(LOW)

        def by_rows(grad):
            shaped = grad.reshape(n, m, width // (n * m), grad.shape[1]).transpose(1, 0, 2, 3)
            return shaped.reshape(m, width // m, grad.shape[1])

        def to_rows(summed):
            r = width // (n * m)
            return turn(exchange_slots(turn(summed, 0).reshape(n, r, summed.shape[1])).reshape(n * r, -1), 0).reshape(n, r, -1).transpose(1, 0, 2)

        down_sum = reduce_planes(down_grad)
        up_sum = reduce_planes(up_grad)
        cross_sum = reduce_planes(cross_grad)
        kv_sum = reduce_planes(by_rows(kv_grad))
        o_sum = reduce_planes(o_grad)
        qkv_sum = reduce_planes(by_rows(qkv_grad))
        fc1_sum = lax.psum_scatter(fc1_grad, "fsdp", scatter_dimension=0, tiled=False)
        moves = [
            (i * m + p, ((n // m) * ((p - i % m) % m) + i // m) * m + p)
            for i in range(n)
            for p in range(m)
        ]
        down_own = lax.ppermute(down_sum, ("ctx", "fsdp"), moves).astype(F32)
        fc1_own = lax.ppermute(fc1_sum, ("ctx", "fsdp"), moves)
        r = width // (n * m)
        up_own = to_rows(up_sum).astype(F32)
        up_own = up_own.reshape(r, n // m, m, m, piece)
        up_blocks = [
            jnp.stack([up_own[:, :, (s - j) % m, j] for s in range(m)], axis=2) for j in range(m)
        ]
        up_own = jnp.stack(up_blocks, axis=1).reshape(r, hidden)
        kv_own = to_rows(kv_sum).astype(F32).reshape(r, n, 2, col).transpose(0, 2, 1, 3)
        kv_own = kv_own.reshape(r, 2 * width)
        qkv_own = to_rows(qkv_sum).astype(F32).reshape(r, n, 3, col).transpose(0, 2, 1, 3)
        qkv_own = qkv_own.reshape(r, 3 * width)
        cross_own = cross_sum.reshape(2, col // m, width).astype(F32)
        grads[layer] = (
            qkv_own,
            o_sum.astype(F32),
            cross_own[0],
            kv_own,
            cross_own[1],
            up_own,
            down_own,
            fc1_own,
        )
        zero = jnp.zeros((width,), F32)
        summed = jnp.stack(
            [gain_zero, gain_one, gain_two, shift_zero, shift_one, shift_two]
            + [zero, zero, column_sum(e1), column_sum(dcq), zero, column_sum(e2), column_sum(e3)]
        )
        owned_q = share(column_sum(dq).reshape(split, col))
        owned_v = share(column_sum(dkv[:, own:]).reshape(split, col))
        owned_ev = column_sum(dkv_cross[:, col:])
        blank = jnp.zeros((col,), F32)
        owned = jnp.stack([blank] * 6 + [owned_q, owned_v, blank, blank, owned_ev, blank, blank])
        vec_rows[layer] = (summed, owned)

    enc_grad = reduce_slots(enc_total.reshape(n, source_rows, width), F32)
    summed = jnp.concatenate([pair[0] for pair in vec_rows])
    owned = jnp.concatenate([pair[1] for pair in vec_rows])
    summed = turn(summed, 1).reshape(-1, n, col).transpose(1, 0, 2)
    vec = reduce_slots(summed, F32) + owned
    vec = vec.reshape(-1, m, col // m).transpose(1, 0, 2)
    vec = lax.psum_scatter(vec, "fsdp", scatter_dimension=0, tiled=False)
    vec = vec.reshape(layers, -1, col // m)
    stacked = [jnp.stack([grads[layer][i] for layer in range(layers)]) for i in range(8)]
    return (
        (result[None], grad_x[None], enc_grad[None])
        + tuple(stacked[:7])
        + (vec[:, :3], vec[:, 3:], stacked[7])
    )


def solution(mesh):
    tokens = P("fsdp", "ctx", None)
    per_stream = P("fsdp", None)
    weight = P(None, "fsdp", None)
    vector = P(None, None, "fsdp")
    grad = P(None, ("ctx", "fsdp"), None)
    vector_grad = P(None, None, ("ctx", "fsdp"))
    return jax.shard_map(
        on_device,
        mesh=mesh,
        in_specs=(tokens,) * 3 + (per_stream,) * 3 + (weight,) * 7 + (vector,) * 2 + (P(None, "fsdp"),),
        out_specs=(tokens,) * 3 + (grad,) * 7 + (vector_grad,) * 2 + (P(None, ("ctx", "fsdp")),),
        check_vma=False,
    )
```

time: 7390 us -> 1110 us (0.15)
  waiting for transfers between devices: 6710 us -> 273 us
  matrix products: 344 us -> 116 us
  starting transfers between devices: 2.84 us -> 227 us
  Pallas kernels: 0 us -> 77.1 us
    reduce_scatter x16 -> x12, waiting for transfers between devices: 4150 us -> 14.6 us  [reduce_planes(): return lax.psum_scatter(parts, 'fsdp', scatter_dimension=0, tiled=False)]
    all_gather x18 -> x6, waiting for transfers between devices: 1690 us -> 0.03 us  [gather_planes(): return lax.all_gather(values, 'fsdp', axis=0, tiled=True)]
    unnamed x48 -> x18, waiting for transfers between devices: 872 us -> 0.3 us
    ppermute x0 -> x220, waiting for transfers between devices: none -> 258 us  [the longest x214 242 us: swap(): return lax.ppermute(values, 'ctx', [(i, i ^ bits) for i in range(count)])]
    dot_general x98 -> x42, matrix products: 344 us -> 116 us  [the longest x14 48.7 us: dot(): return jnp.dot(left, right, preferred_element_type=F32)]
    ppermute x0 -> x220, starting transfers between devices: none -> 225 us  [the longest x214 209 us: swap(): return lax.ppermute(values, 'ctx', [(i, i ^ bits) for i in range(count)])]
    pallas_call x0 -> x8, Pallas kernels: none -> 77.1 us  [the longest x4 42 us: attend_forward(): pl.pallas_call(partial(attend_forward_kernel, head_width), grid=grid, in_...]
  transfers between devices with their start and end apart: 41 -> 238, of which waited for: 38 -> 108; matrix products, arithmetic and copies ran while one was open for 6% -> 33% of each run, Pallas kernels for 0% -> 6%
where the time goes in v1:
time: 1110 us; the launch traced here: 1100 us
  waiting for transfers between devices  273 us (25%)
  starting transfers between devices  227 us (20%)
  local copies, waits for them, and re-layouts  201 us (18%)
  matrix products  116 us (10%)
  blocking collectives  95.4 us (9%)
  other arithmetic  92 us (8%)
  Pallas kernels  77.1 us (7%)
  between operations  21.4 us (2%)
    ppermute x214, waiting for transfers between devices, swap(): return lax.ppermute(values, 'ctx', [(i, i ^ bits) for i in range(count)])  242 us
    ppermute x214, starting transfers between devices, swap(): return lax.ppermute(values, 'ctx', [(i, i ^ bits) for i in range(count)])  209 us
    unnamed x785, local copies, waits for them, and re-layouts  100 us
    all_gather x2, blocking collectives, gather_planes(): return lax.all_gather(values, 'fsdp', axis=0, tiled=True)  55.2 us
    dot_general x14, matrix products, dot(): return jnp.dot(left, right, preferred_element_type=F32)  48.7 us
    pallas_call x4, Pallas kernels, attend_forward(): pl.pallas_call(partial(attend_forward_kernel, head_width), grid=grid, in_...  42 us
    dot_general x14, matrix products, dot_t(): lax.dot_general(left, right, (((1,), (1,)), ((), ())), preferred_element_...  37.1 us
    pallas_call x4, Pallas kernels, attend_backward(): pl.pallas_call(partial(attend_backward_kernel, head_width), grid=grid, in...  35 us
  transfers between devices with their start and end apart: 238, of which 108 were waited for; matrix products, arithmetic and copies ran while one was open for 33% of the time, Pallas kernels for 6%

profile of v1, /device:TPU:0, one launch (start us, length us, event | category | flops | bytes accessed | tf_op | source)
XLA Modules:
  0.0 1102.7 jit_solution(2534136294450294130)
XLA Ops:
  23.4 6.4 copy.600
  40.0 6.4 copy.601
  55.1 12.4 %all_gather.30 = bf16[2,13,1024]{2,0,1:T(2,128)(2,1)S(1)} all-gather(bf16[2,13,256]{2,0,1:T(2,128)(2,1)S(1)} %pad_maximum_fusion.47), channel_id=1, replica_groups=mesh['ctx'=8,'fsdp'=4] {'fsdp'}, dimensions={2}, use_global_device_ids=true | all-gather | bytes 66560 | tf_op jit(solution)/shard_map/all_gather | solution.py:351
  76.0 9.2 all_gather.34
  94.9 29.5 %all_gather.36 = bf16[1024,384]{1,0:T(8,128)(2,1)} all-gather(bf16[256,384]{1,0:T(8,128)(2,1)S(1)} %pad_maximum_fusion.40), channel_id=1, replica_groups=mesh['ctx'=8,'fsdp'=4] {'fsdp'}, dimensions={0}, use_global_device_ids=true | all-gather | bytes 983040 | tf_op jit(solution)/shard_map/all_gather | solution.py:77
  124.5 25.7 %all_gather.31 = bf16[1024,384]{1,0:T(8,128)(2,1)S(1)} all-gather(bf16[256,384]{1,0:T(8,128)(2,1)S(1)} %pad_maximum_fusion.39), channel_id=1, replica_groups=mesh['ctx'=8,'fsdp'=4] {'fsdp'}, dimensions={0}, use_global_device_ids=true | all-gather | bytes 983040 | tf_op jit(solution)/shard_map/all_gather | solution.py:77
  161.5 6.3 collective-permute-done.29
  187.9 10.4 collective-permute-done.8
  201.7 6.8 shard_map.255
  219.4 43.8 %collective-permute-start.34 = (bf16[256,256]{1,0:T(8,128)(2,1)S(1)}, bf16[256,256]{1,0:T(8,128)(2,1)S(1)}, u32[]{:S(2)}, u32[]{:S(2)}) collective-permute-start(bf16[256,256]{1,0:T(8,128)(2,1)S(1)} %constant_dynamic-update-slice_fusion.38), channel_id=1, source_target_pairs={{0,16},{4,20},{8,24},{12,28},{16,0},{20,4},{24,8},{28,12},{1,17},{... | collective-permute-start | bytes 393224 | tf_op jit(solution)/shard_map/ppermute | solution.py:19
  313.2 14.3 %collective-permute-done.13 = bf16[64,1024]{1,0:T(8,128)(2,1)S(1)} collective-permute-done((bf16[64,1024]{1,0:T(8,128)(2,1)S(1)}, bf16[64,1024]{1,0:T(8,128)(2,1)S(1)}, u32[]{:S(2)}, u32[]{:S(2)}) %collective-permute-start.13) | collective-permute-done | bytes 131104 | tf_op jit(solution)/shard_map/ppermute | solution.py:19
  343.0 20.0 %shard_map.256 = (bf16[128,1024]{1,0:T(8,128)(2,1)S(1)}, f32[8,128,2]{2,1,0:T(8,128)S(1)}) custom-call(bf16[128,1024]{1,0:T(8,128)(2,1)S(1)} %fusion.28.q_ref, bf16[256,1024]{1,0:T(8,128)(2,1)S(1)} %constant_dynamic-update-slice_fusion.56.k_ref, bf16[256,1024]{1,0:T(8,128)(2,1)S(1)} %constant_dynamic-update-slice_fusion.72.v_ref, ...), custom_call_target="tpu_custom_call" | custom-call | flops 134217728 | bytes 1572864 | tf_op jit(solution)/shard_map/pallas_call | solution.py:153
  388.8 14.9 %multiply_convert_fusion.1 = (bf16[1024,1024]{1,0:T(8,128)(2,1)}, f32[1024,1024]{1,0:T(8,128)}, f32[1024,1024]{1,0:T(8,128)}) fusion(f32[1024]{0:T(1024)S(1)} %bitcast.1517, bf16[1024,1024]{1,0:T(8,128)(2,1)} %bitcast.76, bf16[1024,1024]{1,0:T(8,128)(2,1)} %all-gather.11.cloned.1.call-done), kind=kOutput, calls=%fused_computation.25 | convolution fusion | flops 2216689664 | bytes 14684160 | tf_op jit(solution)/shard_map/dot_general | solution.py:213
  451.1 6.8 shard_map.257
  478.8 8.4 shard_map.258
  508.8 14.9 %multiply_convert_fusion = (bf16[1024,1024]{1,0:T(8,128)(2,1)}, f32[1024,1024]{1,0:T(8,128)}, f32[1024,1024]{1,0:T(8,128)}) fusion(f32[1024]{0:T(1024)} %bitcast.1519, bf16[1024,1024]{1,0:T(8,128)(2,1)} %bitcast.150, bf16[1024,1024]{1,0:T(8,128)(2,1)} %all-gather.15.cloned.1.call-done), kind=kOutput, calls=%fused_computation.12 | convolution fusion | flops 2216689664 | bytes 14684160 | tf_op jit(solution)/shard_map/dot_general | solution.py:213
  523.6 9.0 convert_reduce_fusion
  566.5 8.3 shard_map.259
  610.1 9.3 shard_map.260
  747.2 8.1 shard_map.261
  792.8 9.3 shard_map.262
  969.5 18.7 %all-reduce.5 = (f32[4,26,32]{2,0,1:T(4,128)S(1)}, f32[4,256]{1,0:T(4,128)S(1)}, f32[4,256]{1,0:T(4,128)S(1)}) all-reduce(f32[4,26,32]{2,0,1:T(4,128)S(1)} %add_bitcast_fusion, f32[4,256]{1,0:T(4,128)S(1)} %copy-done.153, f32[4,256]{1,0:T(4,128)S(1)} %copy-done.154), channel_id=16, replica_groups=mesh['ctx'=8,'fsdp'=4] {'fsdp'}, use_global_device_ids=true, to_apply=%region_68.69.clone | all-reduce | flops 5376 | bytes 43008
  1029.8 13.8 %collective-permute-done.200 = bf16[32,1024]{1,0:T(8,128)(2,1)S(1)} collective-permute-done((bf16[32,1024]{1,0:T(8,128)(2,1)S(1)}, bf16[32,1024]{1,0:T(8,128)(2,1)S(1)}, u32[]{:S(2)}, u32[]{:S(2)}) %collective-permute-start.200) | collective-permute-done | bytes 65568 | tf_op jit(solution)/shard_map/ppermute | solution.py:19
  1078.5 14.6 %reduce-scatter.22.cloned.1.call-done = bf16[1,64,1024]{2,1,0:T(8,128)(2,1)} async-done(((bf16[4,64,1024]{2,1,0:T(8,128)(2,1)}), bf16[1,64,1024]{2,1,0:T(8,128)(2,1)}) %reduce-scatter.22.cloned.1.call-update) | async-done | bytes 131088 | tf_op jit(solution)/shard_map/reduce_scatter | solution.py:81
  (1731 shorter events, 754.0 us)
Async XLA Ops:
  7.2 210.7 %all-gather.9.cloned.1.call-start = ((), (), s32[]{:S(2)}) async-start(), calls=%async_computation.12 | async-start | bytes 1310720 | tf_op jit(solution)/shard_map/all_gather | solution.py:77
  14.4 249.2 %all-gather.13.cloned.1.call-start = ((), (), s32[]{:S(2)}) async-start(), calls=%async_computation.14 | async-start | bytes 1310720 | tf_op jit(solution)/shard_map/all_gather | solution.py:77
  17.4 371.4 %all-gather.11.cloned.1.call-start = ((), (), s32[]{:S(2)}) async-start(), calls=%async_computation.13 | async-start | bytes 2621440 | tf_op jit(solution)/shard_map/all_gather | solution.py:77
  33.7 370.0 %all-gather.17.cloned.1.call-start = ((), (), s32[]{:S(2)}) async-start(), calls=%async_computation.28 | async-start | bytes 2621440 | tf_op jit(solution)/shard_map/all_gather | solution.py:77
  39.9 468.8 %all-gather.15.cloned.1.call-start = ((), (), s32[]{:S(2)}) async-start(), calls=%async_computation.15 | async-start | bytes 2621440 | tf_op jit(solution)/shard_map/all_gather | solution.py:77
  50.4 473.3 %all-gather.19.cloned.1.call-start = ((), (), s32[]{:S(2)}) async-start(), calls=%async_computation.29 | async-start | bytes 2621440 | tf_op jit(solution)/shard_map/all_gather | solution.py:77
  50.4 108.3 %collective-permute-start.26 = (bf16[32,1024]{1,0:T(8,128)(2,1)}, bf16[32,1024]{1,0:T(8,128)(2,1)}, u32[]{:S(2)}, u32[]{:S(2)}) collective-permute-start(bf16[32,1024]{1,0:T(8,128)(2,1)} %bitcast.49), channel_id=1, source_target_pairs={{0,16},{4,20},{8,24},{12,28},{16,0},{20,4},{24,8},{28,12},{1,17},{... | collective-permute-start | bytes 196616 | tf_op jit(solution)/shard_map/ppermute | solution.py:19
  53.6 101.1 %collective-permute-start.24 = (bf16[32,1024]{1,0:T(8,128)(2,1)}, bf16[32,1024]{1,0:T(8,128)(2,1)}, u32[]{:S(2)}, u32[]{:S(2)}) collective-permute-start(bf16[32,1024]{1,0:T(8,128)(2,1)} %bitcast.49), channel_id=1, source_target_pairs={{0,8},{4,12},{8,0},{12,4},{16,24},{20,28},{24,16},{28,20},{1,9},{5... | collective-permute-start | bytes 196616 | tf_op jit(solution)/shard_map/ppermute | solution.py:19
  55.1 100.4 %collective-permute-start.23 = (bf16[32,1024]{1,0:T(8,128)(2,1)}, bf16[32,1024]{1,0:T(8,128)(2,1)}, u32[]{:S(2)}, u32[]{:S(2)}) collective-permute-start(bf16[32,1024]{1,0:T(8,128)(2,1)} %bitcast.49), channel_id=1, source_target_pairs={{0,4},{4,0},{8,12},{12,8},{16,20},{20,16},{24,28},{28,24},{1,5},{5... | collective-permute-start | bytes 196616 | tf_op jit(solution)/shard_map/ppermute | solution.py:19
  69.4 103.3 %collective-permute-start.3 = (bf16[128,1024]{1,0:T(8,128)(2,1)}, bf16[128,1024]{1,0:T(8,128)(2,1)S(1)}, u32[]{:S(2)}, u32[]{:S(2)}) collective-permute-start(bf16[128,1024]{1,0:T(8,128)(2,1)} %fusion.47), channel_id=1, source_target_pairs={{0,16},{4,20},{8,24},{12,28},{16,0},{20,4},{24,8},{28,12},{1,17},{... | collective-permute-start | bytes 786440 | tf_op jit(solution)/shard_map/ppermute | solution.py:19
  70.1 104.9 %collective-permute-start.1 = (bf16[128,1024]{1,0:T(8,128)(2,1)}, bf16[128,1024]{1,0:T(8,128)(2,1)S(1)}, u32[]{:S(2)}, u32[]{:S(2)}) collective-permute-start(bf16[128,1024]{1,0:T(8,128)(2,1)} %fusion.47), channel_id=1, source_target_pairs={{0,8},{4,12},{8,0},{12,4},{16,24},{20,28},{24,16},{28,20},{1,9},{5... | collective-permute-start | bytes 786440 | tf_op jit(solution)/shard_map/ppermute | solution.py:19
  72.5 648.0 %reduce-scatter.28.cloned.1.call-start = ((), (), s32[]{:S(2)}) async-start(), calls=%async_computation.23 | async-start | bytes 655360 | tf_op jit(solution)/shard_map/reduce_scatter | solution.py:81
  604.9 215.5 %reduce-scatter.16.cloned.1.call-start = ((), (), s32[]{:S(2)}) async-start(), calls=%async_computation.17 | async-start | bytes 983040 | tf_op jit(solution)/shard_map/reduce_scatter | solution.py:81
  623.1 212.4 %reduce-scatter.32.cloned.1.call-start = ((), (), s32[]{:S(2)}) async-start(), calls=%async_computation.25 | async-start | bytes 2621440 | tf_op jit(solution)/shard_map/reduce_scatter | solution.py:81
  633.1 221.6 %reduce-scatter.36.cloned.1.call-start = ((), (), s32[]{:S(2)}) async-start(), calls=%async_computation.27 | async-start | bytes 2621440 | tf_op jit(solution)/shard_map/reduce_scatter | solution.py:81
  659.9 213.8 %reduce-scatter.24.cloned.1.call-start = ((), (), s32[]{:S(2)}) async-start(), calls=%async_computation.21 | async-start | bytes 655360 | tf_op jit(solution)/shard_map/reduce_scatter | solution.py:81
  704.1 205.4 %reduce-scatter.20.cloned.1.call-start = ((), (), s32[]{:S(2)}) async-start(), calls=%async_computation.19 | async-start | bytes 327680 | tf_op jit(solution)/shard_map/reduce_scatter | solution.py:81
  716.8 192.6 %reduce-scatter.18.cloned.1.call-start = ((), (), s32[]{:S(2)}) async-start(), calls=%async_computation.18 | async-start | bytes 327680 | tf_op jit(solution)/shard_map/reduce_scatter | solution.py:81
  783.1 131.9 %reduce-scatter.26.cloned.1.call-start = ((), (), s32[]{:S(2)}) async-start(), calls=%async_computation.22 | async-start | bytes 655360 | tf_op jit(solution)/shard_map/reduce_scatter | solution.py:81
  788.5 204.1 %reduce-scatter.14.cloned.1.call-start = ((), (), s32[]{:S(2)}) async-start(), calls=%async_computation.16 | async-start | bytes 983040 | tf_op jit(solution)/shard_map/reduce_scatter | solution.py:81
  805.2 219.0 %reduce-scatter.30.cloned.1.call-start = ((), (), s32[]{:S(2)}) async-start(), calls=%async_computation.24 | async-start | bytes 2621440 | tf_op jit(solution)/shard_map/reduce_scatter | solution.py:81
  818.2 239.9 %reduce-scatter.34.cloned.1.call-start = ((), (), s32[]{:S(2)}) async-start(), calls=%async_computation.26 | async-start | bytes 2621440 | tf_op jit(solution)/shard_map/reduce_scatter | solution.py:81
  848.8 244.2 %reduce-scatter.22.cloned.1.call-start = ((), (), s32[]{:S(2)}) async-start(), calls=%async_computation.20 | async-start | bytes 655360 | tf_op jit(solution)/shard_map/reduce_scatter | solution.py:81
  858.8 216.9 %collective-permute-start.214 = (bf16[256,1024]{1,0:T(8,128)(2,1)}, bf16[256,1024]{1,0:T(8,128)(2,1)}, u32[]{:S(2)}, u32[]{:S(2)}) collective-permute-start(bf16[256,1024]{1,0:T(8,128)(2,1)} %bitcast.1531), channel_id=1, source_target_pairs={{0,0},{1,9},{2,18},{3,27},{4,24},{5,1},{6,10},{7,19},{8,16},{9,25}... | collective-permute-start | bytes 1572872 | tf_op jit(solution)/shard_map/ppermute | solution.py:521
  (420 other events, 5030.5 us)
Sparse Core Ops, SparseCore 0:
  14.5 32.8 all-gather.8
  49.5 29.6 all-gather.12
  81.4 67.3 all-gather.10
  150.2 54.7 all-gather.16
  206.5 48.1 all-gather.14
  256.1 54.5 all-gather.18
  605.0 20.0 reduce-scatter.27
  627.5 21.5 reduce-scatter.15
  651.4 43.0 reduce-scatter.31
  696.8 43.1 reduce-scatter.35
  742.3 20.9 reduce-scatter.23
  765.9 17.9 reduce-scatter.19
  786.8 17.9 reduce-scatter.17
  807.5 19.8 reduce-scatter.25
  829.5 21.5 reduce-scatter.13
  853.3 43.0 reduce-scatter.29
  899.2 43.1 reduce-scatter.33
  1074.3 18.6 reduce-scatter.21

commit v2 on v1

v2 whole, which is shorter than its diff:
```python
from functools import partial

import jax
import jax.numpy as jnp
from jax import lax
from jax.experimental import pallas as pl
from jax.experimental.pallas import tpu as pltpu
from jax.sharding import PartitionSpec as P

HEADS = 16
EPSILON = 1e-05
NEGATIVE = -1e30
F32 = jnp.float32
LOW = jnp.bfloat16
VMEM = pl.BlockSpec(memory_space=pltpu.VMEM)
SMEM = pl.BlockSpec(memory_space=pltpu.SMEM)
FAR = pl.BlockSpec(memory_space=pl.ANY)
VMEM_BYTES = 56 * 2**20


def swap(values, bits):
    count = lax.axis_size("ctx")
    return lax.ppermute(values, "ctx", [(i, i ^ bits) for i in range(count)])


def gather_near(rows):
    if lax.axis_size("ctx") == 8:
        return swap(rows, 2), swap(rows, 4)
    return ()


def gather_slots(rows, near=None):
    count = lax.axis_size("ctx")
    if count == 8:
        near_x, near_y = near or gather_near(rows)
        half = rows.shape[0] // 2
        far = jnp.concatenate([swap(near_x[:half], 4), swap(near_y[half:], 2)])
        blocks = []
        for block in (rows, near_x, near_y, far):
            blocks += [block, swap(block, 1)]
        return blocks
    blocks = [rows]
    bit = 1
    while bit < count:
        blocks = blocks + [swap(block, bit) for block in blocks]
        bit *= 2
    return blocks


def gather_joined(rows, near):
    count = lax.axis_size("ctx")
    size = rows.shape[0]
    if count == 8:
        half = size // 2
        joined = swap(jnp.concatenate([rows, *near]), 1)
        far = jnp.concatenate([swap(near[0][:half], 4), swap(near[1][half:], 2)])
        arrays = [rows, *near, far, joined, swap(far, 1)]
        where = [(0, 0), (4, 0), (1, 0), (4, size), (2, 0), (4, 2 * size), (3, 0), (5, 0)]
        return arrays, where
    return gather_slots(rows), [(k, 0) for k in range(count)]


def send_chip(chip, kind):
    count = lax.axis_size("ctx")
    if count == 8:
        return [chip[0]] + [swap(chip[i].astype(kind), 2 * i) for i in (1, 2, 3)]
    bit = count // 4
    while bit:
        chip = chip[:bit] + swap(chip[bit : 2 * bit].astype(kind), 2 * bit).astype(F32)
        bit //= 2
    return [chip[0]]


def reduce_slots(even, odd, kind=LOW, hold=None):
    count = lax.axis_size("ctx")
    if isinstance(odd, list):
        odd = jnp.concatenate([swap(block, 1) for block in odd])
    else:
        odd = swap(odd.astype(kind), 1)
    chip = even.astype(F32) + odd.astype(F32)
    if count == 8:
        sent = [chip[i].astype(kind) for i in (1, 2, 3)]
        if hold is not None:
            sent = after(sent, hold)
        return [chip[0]] + [swap(sent[i], 2 * i + 2) for i in range(3)]
    bit = count // 4
    while bit:
        chip = chip[:bit] + swap(chip[bit : 2 * bit].astype(kind), 2 * bit).astype(F32)
        bit //= 2
    return [chip[0]]


def total_of(terms):
    total = terms[0].astype(F32)
    for term in terms[1:]:
        total = total + term.astype(F32)
    return total


def turn(values, axis):
    count = lax.axis_size("ctx")
    here = lax.axis_index("ctx")
    width = values.shape[axis] // count
    return jnp.concatenate(
        [
            lax.dynamic_slice_in_dim(values, (here ^ k) * width, width, axis)
            for k in range(count)
        ],
        axis=axis,
    )


def sum_planes(parts):
    count = lax.axis_size("fsdp")
    here = lax.axis_index("fsdp")
    total = lax.dynamic_index_in_dim(parts, here, 0, False)
    for step in range(1, count):
        term = lax.dynamic_index_in_dim(parts, (here + step) % count, 0, False)
        total = total + lax.ppermute(term, "fsdp", [(i, (i + step) % count) for i in range(count)])
    return total


def after(values, other):
    return lax.optimization_barrier((values, other))[0]


def gather_planes(values):
    return lax.all_gather(values, "fsdp", axis=0, tiled=True)


def reduce_planes(parts):
    return lax.psum_scatter(parts, "fsdp", scatter_dimension=0, tiled=False)


def layer_norm(values, gain_row, offset_row):
    center = values - jnp.mean(values, axis=-1, keepdims=True)
    spread = jnp.mean(center * center, axis=-1, keepdims=True)
    return center * lax.rsqrt(spread + EPSILON) * gain_row + offset_row


def layer_norm_back(values, gain_row, grad):
    center = values - jnp.mean(values, axis=-1, keepdims=True)
    inverse = lax.rsqrt(jnp.mean(center * center, axis=-1, keepdims=True) + EPSILON)
    normed = center * inverse
    scaled = grad * gain_row
    back = inverse * (
        scaled
        - jnp.mean(scaled, axis=-1, keepdims=True)
        - normed * jnp.mean(scaled * normed, axis=-1, keepdims=True)
    )
    return back, row_sum(grad * normed), row_sum(grad)


def row_sum(values):
    return jnp.sum(values.astype(F32), axis=0, keepdims=True)


def dot(left, right):
    return jnp.dot(left, right, preferred_element_type=F32)


def dot_t(left, right):
    return lax.dot_general(left, right, (((1,), (1,)), ((), ())), preferred_element_type=F32)


def t_dot(left, right):
    return lax.dot_general(left, right, (((0,), (0,)), ((), ())), preferred_element_type=F32)


def call(kernel, ins, outs, flops, scratch=(), smem=0, far=0, wait=()):
    count, extra = len(ins), len(wait)

    def body(*refs):
        kernel(*refs[:count], *refs[count + extra :])

    moved = sum(a.size * a.dtype.itemsize for a in ins)
    moved += sum(a.size * a.dtype.itemsize for a in outs)
    return pl.pallas_call(
        body,
        in_specs=[SMEM] * smem + [VMEM] * (count - smem - far) + [FAR] * (far + extra),
        out_specs=[VMEM] * len(outs),
        out_shape=outs,
        scratch_shapes=list(scratch),
        compiler_params=pltpu.CompilerParams(vmem_limit_bytes=VMEM_BYTES),
        cost_estimate=pl.CostEstimate(flops=int(flops), bytes_accessed=int(moved), transcendentals=0),
    )(*ins, *wait)


def like(shape, kind):
    return jax.ShapeDtypeStruct(tuple(shape), kind)


def tile_rows(rows, size):
    return pl.ds(pl.multiple_of(rows * size, size), size)


def put_slots(even_ref, odd_ref, index, values):
    rows = even_ref.shape[1]
    even_ref[index] = values[:rows].astype(LOW)
    odd_ref[index] = values[rows:].astype(LOW)


def self_forward_kernel(n, rows, split, raw, joined, head_width, *refs):
    blocks, refs = refs[:n], refs[n:]
    vec_ref, bias_ref, w_ref, low_ref, high_ref, place_ref = refs[:6]
    (wo_ref, *refs) = refs[6:] if joined else (None, *refs[6:])
    h_ref, q_ref, k_ref, v_ref, a_ref, lse_ref, *out_refs = refs
    own = k_ref.shape[1]
    for k in range(n):
        block = blocks[k][:rows]
        if raw:
            block = layer_norm(block.astype(F32), vec_ref[0:1], vec_ref[3:4]).astype(LOW)
        h_ref[k * rows : (k + 1) * rows] = block

    @pl.loop(0, n // 2)
    def _(i):
        at = tile_rows(i, 2 * rows)
        z = dot(h_ref[at], w_ref[:, : 3 * own])
        q = ((z[:, :own] + bias_ref[0:1]) * 0.125).astype(LOW)
        if split == 1:
            q_ref[at] = q
        else:
            q_ref[tile_rows(i, rows)] = q[:rows]
        k_ref[at] = z[:, own : 2 * own].astype(LOW)
        v_ref[at] = (z[:, 2 * own :] + bias_ref[1:2]).astype(LOW)

    step = 2 * rows // split

    @pl.loop(0, n // 2)
    def _(i):
        at = tile_rows(i, step)
        mask = (place_ref[...] >= low_ref[at]) & (place_ref[...] <= high_ref[at])
        outs, masses = [], []
        for start in range(0, own, head_width):
            span = slice(start, start + head_width)
            scores = jnp.where(mask, dot_t(q_ref[at, span], k_ref[:, span]), NEGATIVE)
            top = jnp.max(scores, axis=1, keepdims=True)
            raised = jnp.exp(scores - top)
            mass = jnp.sum(raised, axis=1, keepdims=True)
            outs.append(dot((raised * (1.0 / mass)).astype(LOW), v_ref[:, span]))
            masses.append(top + jnp.log(mass))
        a = jnp.concatenate(outs, axis=1).astype(LOW)
        a_ref[at] = a
        lse_ref[at] = jnp.concatenate(masses, axis=1)
        if joined:
            put_product(split, a, wo_ref, *out_refs, i)


def put_product(split, a, wo_ref, even_ref, odd_ref, i):
    y = dot(a, wo_ref[...])
    if split > 1:
        y = jnp.concatenate([y, jnp.zeros_like(y)])
    put_slots(even_ref, odd_ref, i, y)


def self_out_kernel(n, rows, split, a_ref, wo_ref, even_ref, odd_ref):
    step = 2 * rows // split

    @pl.loop(0, n // 2)
    def _(i):
        put_product(split, a_ref[tile_rows(i, step)], wo_ref, even_ref, odd_ref, i)


def mid_forward_kernel(n, terms, arrays, where, head_width, here_ref, *refs):
    x_ref, refs = refs[0], refs[1:]
    term_refs, refs = refs[:terms], refs[terms:]
    w_refs, refs = refs[:arrays], refs[arrays:]
    vec_ref, low_ref, high_ref, place_ref = refs[:4]
    x1_ref, x2_ref, h2_ref, cq_ref, c_ref, lse_ref, h3_ref = refs[4:11]
    wq_ref, wo_ref, ek_ref, ev_ref = refs[11:]
    col = w_refs[0].shape[0] // 2
    width = wq_ref.shape[1]
    here = here_ref[0]
    for k in range(n):
        at = tile_rows(here ^ k, col)
        array, first = where[k]
        top, bottom = pl.ds(first, col), pl.ds(first + col, col)
        wq_ref[at] = w_refs[array][top, :width]
        wo_ref[at] = w_refs[array][bottom, :width]
        ek_ref[at] = w_refs[array][top, width:]
        ev_ref[at] = w_refs[array][bottom, width:]
    x1 = x_ref[...].astype(F32) + total_of([t[...] for t in term_refs]) + vec_ref[8:9]
    x1_ref[...] = x1
    h2 = layer_norm(x1, vec_ref[1:2], vec_ref[4:5]).astype(LOW)
    h2_ref[...] = h2
    cq_ref[...] = ((dot_t(h2, wq_ref[...]) + vec_ref[9:10]) * 0.125).astype(LOW)
    mask = (place_ref[...] >= low_ref[...]) & (place_ref[...] <= high_ref[...])
    outs, masses = [], []
    for start in range(0, cq_ref.shape[1], head_width):
        span = slice(start, start + head_width)
        scores = jnp.where(mask, dot(cq_ref[:, span], ek_ref[span]), NEGATIVE)
        top = jnp.max(scores, axis=1, keepdims=True)
        raised = jnp.exp(scores - top)
        mass = jnp.sum(raised, axis=1, keepdims=True)
        outs.append(dot_t((raised * (1.0 / mass)).astype(LOW), ev_ref[span]))
        masses.append(top + jnp.log(mass))
    c_ref[...] = jnp.concatenate(outs, axis=1).astype(LOW)
    lse_ref[...] = jnp.concatenate(masses, axis=1)
    x2 = x1 + dot_t(c_ref[...], wo_ref[...]) + vec_ref[11:12]
    x2_ref[...] = x2
    h3_ref[...] = layer_norm(x2, vec_ref[2:3], vec_ref[5:6]).astype(LOW)


def copies_of(sources, up_ref, down_ref, sems):
    if len(sources) == 2:
        pairs = [(sources[0], up_ref), (sources[1], down_ref)]
    else:
        planes, both = sources[0].shape[:2]
        size = up_ref.shape[0] // planes
        pairs = []
        for j in range(planes):
            at = pl.ds(j * size, size)
            pairs.append((sources[0].at[j, pl.ds(0, size)], up_ref.at[at]))
            pairs.append((sources[0].at[j, pl.ds(size, size)], down_ref.at[at]))
    return [pltpu.make_async_copy(a, b, sems.at[i]) for i, (a, b) in enumerate(pairs)]


def ffn_forward_kernel(n, sources, *refs):
    blocks, refs = refs[:n], refs[n:]
    bias_ref, refs = refs[0], refs[1:]
    sources, refs = refs[:sources], refs[sources:]
    h_ref, g_ref, slope_ref, even_ref, odd_ref, up_ref, down_ref, sems = refs
    rows = blocks[0].shape[0]
    copies = copies_of(sources, up_ref, down_ref, sems)
    for copy in copies:
        copy.start()
    for k in range(n):
        h_ref[k * rows : (k + 1) * rows] = blocks[k][...]
    for copy in copies:
        copy.wait()

    @pl.loop(0, n // 2)
    def _(i):
        at = tile_rows(i, 2 * rows)
        u = dot(h_ref[at], up_ref[...]) + bias_ref[...]
        share = 0.5 + 0.5 * lax.erf(u * 0.7071067811865476)
        g = (u * share).astype(LOW)
        g_ref[at] = g
        slope_ref[at] = (share + u * (jnp.exp(-0.5 * u * u) * 0.3989422804014327)).astype(LOW)
        put_slots(even_ref, odd_ref, i, dot(g, down_ref[...]))


def ffn_backward_kernel(n, sources, *refs):
    blocks, refs = refs[:n], refs[n:]
    slope_ref, refs = refs[0], refs[1:]
    sources, refs = refs[:sources], refs[sources:]
    e_ref, du_ref, sum_ref, even_ref, odd_ref, up_ref, down_ref, sems = refs
    rows = blocks[0].shape[0]
    copies = copies_of(sources, up_ref, down_ref, sems)
    for copy in copies:
        copy.start()
    for k in range(n):
        e_ref[k * rows : (k + 1) * rows] = blocks[k][...]
    sum_ref[...] = jnp.zeros_like(sum_ref)
    for copy in copies:
        copy.wait()

    @pl.loop(0, n // 2)
    def _(i):
        at = tile_rows(i, 2 * rows)
        du = (dot_t(e_ref[at], down_ref[...]) * slope_ref[at].astype(F32)).astype(LOW)
        du_ref[at] = du
        sum_ref[...] += row_sum(du)
        put_slots(even_ref, odd_ref, i, dot_t(du, up_ref[...]))


def pack_kernel(m, n, jobs, where_ref, *refs):
    count = sum(len(FED[kind]) for kind, layer in jobs)
    sources, packed, sems = refs[:count], refs[count:-1], refs[-1]
    c, f = where_ref[0], where_ref[1]
    high, low = c // m, c % m
    copies = []

    def add(source, target):
        copies.append(pltpu.make_async_copy(source, target, sems.at[len(copies)]))

    def columns(start, size):
        return pl.ds(pl.multiple_of(start, 128), size)

    for (kind, layer), target in zip(jobs, packed):
        fed, sources = sources[: len(FED[kind])], sources[len(FED[kind]) :]
        at = 0
        if kind == "ffn":
            up, down = fed
            rows, piece = up.shape[1], down.shape[1] // n
            for j in range(m):
                start = (n * j + m * high + (j + low) % m) * piece
                add(up.at[layer, :, columns(start, piece)], target.at[pl.ds(0, rows), pl.ds(j * piece, piece)])
            start = (m * high + (f + low) % m) * piece
            add(down.at[layer, pl.ds(pl.multiple_of(start, piece), piece)], target.at[pl.ds(rows, piece)])
            continue
        for source, (name, parts) in zip(fed, FED[kind].items()):
            if parts == 0:
                add(source, target.at[:, pl.ds(at, source.shape[1])])
                continue
            width = source.shape[2] // parts
            col = width // n
            if name == "self_out":
                for l in range(source.shape[0]):
                    add(source.at[l, :, columns(c * col, col)], target.at[:, pl.ds(at, col)])
                    at += col
                continue
            for i in range(parts):
                add(source.at[layer, :, columns(i * width + c * col, col)], target.at[:, pl.ds(at, col)])
                at += col
    for copy in copies:
        copy.start()
    for copy in copies:
        copy.wait()


FED = {
    "first": {"qkv": 3, "kv": 2, "q": 1, "out": 1, "self_out": 1, "vec": 0},
    "attention": {"qkv": 3, "kv": 2, "q": 1, "out": 1},
    "ffn": {"up": 1, "down": 1},
}


def late_kernel(*refs):
    out_ref = refs[-1]
    size = out_ref.shape[1] // (len(refs) - 1)
    for layer, ref in enumerate(refs[:-1]):
        out_ref[:, layer * size : (layer + 1) * size] = ref[:, :size]


def copy_kernel(in_ref, out_ref):
    out_ref[...] = in_ref[...]


def assemble_kernel(n, skip, here_ref, *refs):
    out_ref = refs[n]
    size = refs[0].shape[0] - skip
    for k in range(n):
        out_ref[tile_rows(here_ref[0] ^ k, size)] = refs[k][skip:]


def cross_prepare_kernel(col, skip, w_ref, enc_ref, bias_ref, out_ref):
    kv = dot(enc_ref[...], w_ref[:, skip : skip + 2 * col]) + bias_ref[...]
    width = w_ref.shape[0]
    out_ref[:, width:] = kv.T.astype(LOW)
    out_ref[:, :width] = w_ref[:, skip + 2 * col : skip + 4 * col].astype(F32).T.astype(LOW)


def between_kernel(terms, last, *refs):
    x2_ref, refs = refs[0], refs[1:]
    term_refs, refs = refs[:terms], refs[terms:]
    y = x2_ref[...] + total_of([t[...] for t in term_refs]) + refs[0][12:13]
    if last:
        refs[1][...] = y.astype(LOW)
    else:
        next_ref, y_ref, h_ref = refs[1:]
        y_ref[...] = y
        h_ref[...] = layer_norm(y, next_ref[0:1], next_ref[3:4]).astype(LOW)


def put_folded(out_ref, grad, at, n, m):
    size, width = grad.shape[0] // m, grad.shape[1] // n
    for p in range(m):
        for i in range(n):
            block = grad[p * size : (p + 1) * size, i * width : (i + 1) * width]
            out_ref[p, i * size : (i + 1) * size, at : at + width] = block


def attention_weights_kernel(n, m, skip, terms, full, here_ref, *refs):
    w_refs, refs = refs[:terms], refs[terms:]
    own_refs, refs = (refs[:5], refs[5:]) if full else ((), refs)
    enc_ref, w_kv_ref, before_ref, out_ref, total_ref, sum_ref, even_ref, odd_ref = refs
    col = w_refs[0].shape[0] // 2
    width = w_kv_ref.shape[0]
    grad = total_of([t[:, :width] for t in w_refs]).astype(LOW)
    for i in range(2):
        at = (5 + i if full else 2 + i) * col
        put_folded(out_ref, grad[i * col : (i + 1) * col], at, n, m)
    dkv_t = total_of([t[:, width:] for t in w_refs])
    sum_ref[...] = jnp.sum(dkv_t.astype(LOW).astype(F32), axis=1, keepdims=True)
    dkv = dkv_t.T.astype(LOW)
    total_ref[...] = before_ref[...] + dot_t(dkv, w_kv_ref[:, skip : skip + 2 * col])
    put_by_rows(out_ref, t_dot(enc_ref[...], dkv).astype(LOW), 0, width, n, m)
    for k in range(n):
        part = total_ref[tile_rows(here_ref[0] ^ k, even_ref.shape[1])]
        (odd_ref if k % 2 else even_ref)[k // 2] = part
    if not full:
        return
    h_ref, dq_ref, dkv_ref, a_ref, e_ref = own_refs
    own = dq_ref.shape[1]
    step = min(256, width)
    for first in range(0, width, step):
        part = h_ref[:, first : first + step]
        grad = jnp.concatenate([t_dot(part, dq_ref[...]), t_dot(part, dkv_ref[...])], axis=1)
        put_by_rows(out_ref, grad.astype(LOW), first, width, n, m, 2 * own)
    put_folded(out_ref, t_dot(a_ref[...], e_ref[...]).astype(LOW), 7 * own, n, m)


def put_by_rows(out_ref, grad, first, total, n, m, at=0):
    size = total // (n * m)
    for i in range(grad.shape[0] // size):
        block = first // size + i
        device, plane = block // m, block % m
        part = grad[i * size : (i + 1) * size]
        out_ref[plane, device * size : (device + 1) * size, at : at + grad.shape[1]] = part


def ffn_weights_kernel(n, m, here_ref, h_ref, du_ref, g_ref, e_ref, sum_ref, up_ref, down_ref=None):
    piece = g_ref.shape[1] // m
    low = here_ref[0] % m
    first = h_ref.shape[1] // m if down_ref is None else 0
    down_ref = up_ref if down_ref is None else down_ref
    for j in range(m):
        plane = (low + j) % m
        grad = t_dot(g_ref[:, j * piece : (j + 1) * piece], e_ref[...]).astype(LOW)
        down_ref[plane, first : first + piece] = grad
        part = sum_ref[:, j * piece : (j + 1) * piece].astype(LOW)
        down_ref[plane, first + piece :] = jnp.zeros((16, down_ref.shape[2]), LOW)
        down_ref[plane, first + piece : first + piece + 1, :piece] = part
    step = min(256, h_ref.shape[1])
    for first in range(0, h_ref.shape[1], step):
        grad = t_dot(h_ref[:, first : first + step], du_ref[...]).astype(LOW)
        put_by_rows(up_ref, grad, first, h_ref.shape[1], n, m)


def mid_backward_kernel(n, terms, head_width, here_ref, *refs):
    dy_ref, refs = refs[0], refs[1:]
    term_refs, refs = refs[:terms], refs[terms:]
    x1_ref, x2_ref, vec_ref, wq_ref, wo_ref, ek_ref, ev_ref, cq_ref, lse_ref = refs[:9]
    low_ref, high_ref, place_ref = refs[9:12]
    dx1_ref, e1_ref, e2_ref, dcq_ref, even_ref, odd_ref, sum_ref = refs[12:19]
    dek_ref, dev_ref = refs[19:]
    col = even_ref.shape[1] // 2
    dy = dy_ref[...].astype(F32)
    back, gain_two, shift_two = layer_norm_back(
        x2_ref[...], vec_ref[2:3], total_of([t[...] for t in term_refs])
    )
    dx2 = dy + back
    e2 = dx2.astype(LOW)
    e2_ref[...] = e2
    d_all = dot(e2, wo_ref[...]).astype(LOW)
    mask = (place_ref[...] >= low_ref[...]) & (place_ref[...] <= high_ref[...])
    dqs = []
    for index, start in enumerate(range(0, cq_ref.shape[1], head_width)):
        span = slice(start, start + head_width)
        q, d, ek, ev = cq_ref[:, span], d_all[:, span], ek_ref[span], ev_ref[span]
        weights = jnp.where(mask, jnp.exp(dot(q, ek) - lse_ref[:, index : index + 1]), 0.0)
        weight_grad = dot(d, ev)
        delta = jnp.sum(weights * weight_grad, axis=1, keepdims=True)
        score_grad = (weights * (weight_grad - delta)).astype(LOW)
        dqs.append(dot_t(score_grad, ek))
        dek_ref[span] = t_dot(q, score_grad).astype(LOW)
        dev_ref[span] = t_dot(d, weights.astype(LOW)).astype(LOW)
    dcq = (jnp.concatenate(dqs, axis=1).astype(LOW).astype(F32) * 0.125).astype(LOW)
    dcq_ref[...] = dcq
    here = here_ref[0]
    for k in range(n):
        at = tile_rows(here ^ k, col)
        out = odd_ref if k % 2 else even_ref
        out[k // 2, :col] = dek_ref[at]
        out[k // 2, col:] = dev_ref[at]
    back, gain_one, shift_one = layer_norm_back(x1_ref[...], vec_ref[1:2], dot(dcq, wq_ref[...]))
    dx1 = dx2 + back
    dx1_ref[...] = dx1
    e1 = dx1.astype(LOW)
    e1_ref[...] = e1
    sums = [gain_one, gain_two, shift_one, shift_two]
    sums += [row_sum(e1), row_sum(dcq), row_sum(e2), row_sum(dy)]
    sum_ref[...] = jnp.concatenate(sums, axis=0)


def cross_weights_kernel(n, here_ref, h_ref, dcq_ref, c_ref, e_ref, kv_even, kv_odd, even_ref, *refs):
    odd_refs, (q_ref, o_ref) = refs[:2], refs[2:]
    col = even_ref.shape[1] // 2
    width = q_ref.shape[1]
    q_ref[...] = t_dot(h_ref[...], dcq_ref[...]).astype(LOW)
    o_ref[...] = t_dot(c_ref[...], e_ref[...]).astype(LOW)
    here = here_ref[0]
    for k in range(n):
        at = tile_rows(here ^ k, col)
        out, i = (odd_refs[2 * k // n], k // 2 % (n // 4)) if k % 2 else (even_ref, k // 2)
        out[i, :col, :width] = q_ref[at]
        out[i, col:, :width] = o_ref[at]
    even_ref[:, :, width:] = kv_even[...]
    for i in range(2):
        odd_refs[i][:, :, width:] = kv_odd[i * n // 4 : (i + 1) * n // 4]


def self_backward_kernel(n, split, head_width, *refs):
    blocks, refs = refs[:n], refs[n:]
    wo_ref, w_ref, q_ref, k_ref, v_ref, lse_ref, low_ref, high_ref, place_ref = refs[:9]
    e_ref, dq_ref, dkv_ref, even_ref, odd_ref, dk_ref, dv_ref = refs[9:]
    rows = blocks[0].shape[0]
    own = wo_ref.shape[0]
    for i, k in enumerate(range(0, n, split)):
        e_ref[i * rows : (i + 1) * rows] = blocks[k][...]
    dk_ref[...] = jnp.zeros_like(dk_ref)
    dv_ref[...] = jnp.zeros_like(dv_ref)
    step = 2 * rows // split

    @pl.loop(0, n // 2)
    def _(i):
        at = tile_rows(i, step)
        mask = (place_ref[...] >= low_ref[at]) & (place_ref[...] <= high_ref[at])
        d_all = dot_t(e_ref[at], wo_ref[...]).astype(LOW)
        dqs, dks, dvs = [], [], []
        for index, start in enumerate(range(0, own, head_width)):
            span = slice(start, start + head_width)
            q, k, v, d = q_ref[at, span], k_ref[:, span], v_ref[:, span], d_all[:, span]
            weights = jnp.where(mask, jnp.exp(dot_t(q, k) - lse_ref[at, index : index + 1]), 0.0)
            weight_grad = dot_t(d, v)
            delta = jnp.sum(weights * weight_grad, axis=1, keepdims=True)
            score_grad = (weights * (weight_grad - delta)).astype(LOW)
            dqs.append(dot(score_grad, k))
            dks.append(t_dot(score_grad, q))
            dvs.append(t_dot(weights.astype(LOW), d))
        dq = jnp.concatenate(dqs, axis=1).astype(LOW).astype(F32) * 0.125
        dq_ref[at] = dq.astype(LOW)
        dk_ref[...] += jnp.concatenate(dks, axis=1)
        dv_ref[...] += jnp.concatenate(dvs, axis=1)

    dkv_ref[:, :own] = dk_ref[...].astype(LOW)
    dkv_ref[:, own:] = dv_ref[...].astype(LOW)
    if split > 1:
        return

    @pl.loop(0, n // 2)
    def _(i):
        at = tile_rows(i, 2 * rows)
        put_slots(
            even_ref, odd_ref, i, dot_t(dq_ref[at], w_ref[:, :own]) + dot_t(dkv_ref[at], w_ref[:, own : 3 * own])
        )


def place_ffn_kernel(n, m, layers, *refs):
    up_refs, down_refs = refs[:layers], refs[layers : 2 * layers]
    up_out, down_out, fc1_out = refs[2 * layers :]
    piece = fc1_out.shape[1]
    for layer in range(layers):
        down_out[layer] = down_refs[layer][:piece].astype(F32)
        fc1_out[layer : layer + 1] = down_refs[layer][piece : piece + 16, :piece].astype(F32)[:1]
        for device in range(n):
            high, low = device // m, device % m
            for j in range(m):
                at = (n * j + m * high + (j + low) % m) * piece
                block = up_refs[layer][device, :, j * piece : (j + 1) * piece]
                up_out[layer, :, at : at + piece] = block.astype(F32)


def place_attention_kernel(n, layers, *refs):
    late, both, outs = refs[0], refs[1 : layers + 1], refs[layers + 1 :]
    qkv_out, o_out, q_out, kv_out, cross_out = outs
    col = both[0].shape[1] // 8
    rows = both[0].shape[0] // n
    for layer in range(layers):
        for i in range(n):
            for part in range(5):
                out, at = (kv_out, part) if part < 2 else (qkv_out, part - 2)
                start = (5 * layer + part) * col
                block = late[i, :, start : start + col]
                out[layer, :, (at * n + i) * col : (at * n + i + 1) * col] = block.astype(F32)
            for out, part in ((q_out, 5), (cross_out, 6), (o_out, 7)):
                block = both[layer][i * rows : (i + 1) * rows, part * col : (part + 1) * col]
                out[layer, :, i * col : (i + 1) * col] = block.astype(F32)


def last_backward_kernel(terms, *refs):
    dx1_ref, refs = refs[0], refs[1:]
    term_refs, refs = refs[:terms], refs[terms:]
    x_ref, vec_ref, dx_ref, e_ref, sum_ref = refs
    back, gain, shift = layer_norm_back(
        x_ref[...].astype(F32), vec_ref[0:1], total_of([t[...] for t in term_refs])
    )
    dx = dx1_ref[...] + back
    dx_ref[...] = dx
    e_ref[...] = dx.astype(LOW)
    sum_ref[...] = jnp.concatenate([gain, shift], axis=0)


def stored_positions(row_index, row_count, dev_count):
    device = row_index // row_count
    offset = row_index % row_count
    half_rows = row_count // 2
    return jnp.where(
        offset < half_rows,
        device * half_rows + offset,
        (2 * dev_count - 1 - device) * half_rows + offset - half_rows,
    )


def ranges_of(starts, length):
    return starts, jnp.concatenate([starts[1:], jnp.full((1,), length, jnp.int32)]) - 1


def group_of(places, starts):
    return jnp.sum((starts[None, :] <= places[:, None]).astype(jnp.int32), axis=1) - 1


def pick(table, index):
    slots = jnp.arange(table.shape[0], dtype=jnp.int32)
    return jnp.sum(jnp.where(index[:, None] == slots[None, :], table[None, :], 0), axis=1)


def on_device(
    tokens,
    encoder_states,
    grad_out,
    doc_starts,
    source_doc,
    source_offsets,
    self_qkv,
    self_out,
    cross_q,
    cross_kv,
    cross_out,
    ffn_in,
    ffn_out,
    norm_gains,
    vec_biases,
    fc1_bias,
):
    n, m = lax.axis_size("ctx"), lax.axis_size("fsdp")
    c, f = lax.axis_index("ctx"), lax.axis_index("fsdp")
    layers = self_qkv.shape[0]
    rows, width = tokens.shape[1:]
    source_rows = encoder_states.shape[1]
    length, source_length = n * rows, n * source_rows
    held = self_out.shape[1]
    hidden = ffn_out.shape[1] * m
    head_width = width // HEADS
    groups = min(n, HEADS)
    split = n // groups
    group, part = c // split, c % split
    own = width // groups
    col = width // n
    piece = hidden // (n * m)
    units = m * piece
    high_c, low_c = c // m, c % m
    here = jnp.stack([c, f]).astype(jnp.int32)
    queries = length // split
    packs = split == 1 and col % 128 == 0 and units == width and piece == held

    slot_rows = ((c ^ jnp.arange(n, dtype=jnp.int32)) * rows)[:, None] + jnp.arange(
        rows, dtype=jnp.int32
    )[None, :]
    places = stored_positions(slot_rows.reshape(-1), rows, n)
    own_places = places.reshape(n // split, split, rows)[:, 0].reshape(-1)
    doc_low, doc_high = ranges_of(doc_starts[0], length)
    self_bounds = [
        pick(doc_low, group_of(own_places, doc_starts[0]))[:, None],
        own_places[:, None],
        places[None, :],
    ]
    source_low, source_high = ranges_of(source_offsets[0], source_length)
    read_doc = pick(source_doc[0], group_of(places[:rows], doc_starts[0]))
    cross_bounds = [
        pick(source_low, read_doc)[:, None],
        pick(source_high, read_doc)[:, None],
        jnp.arange(source_length, dtype=jnp.int32)[None, :],
    ]

    def fetch_out():
        start = group * own
        got = lax.dynamic_slice(self_out, (0, start % held, 0), (layers, own, width))
        got = jnp.where(f == start // held, got, jnp.zeros_like(got))
        covered = [{(device // split) * own // held} for device in range(n)]
        while any(len(planes) < m for planes in covered):
            pairs = []
            for device, planes in enumerate(covered):
                reached = set()
                for plane in sorted(planes):
                    free = [p for p in (plane + 1, plane - 1) if 0 <= p < m and p not in planes | reached]
                    if free:
                        reached.add(free[0])
                        pairs.append((device * m + plane, device * m + free[0]))
                planes |= reached
            got = got + lax.ppermute(got, ("ctx", "fsdp"), pairs)
        return got

    def columns(array, layer, start, count):
        return lax.dynamic_slice(array, (layer, 0, start), (1, array.shape[1], count))[0]

    first_rows = jnp.concatenate([tokens[0], encoder_states[0]])
    first_slots = gather_slots(first_rows)
    unit_start = (m * high_c + (f + low_c) % m) * piece
    last_slots = gather_slots(after(grad_out[0], first_slots))
    vec_rows = jnp.concatenate([norm_gains, vec_biases], axis=1)
    fc1_rows = lax.dynamic_slice(fc1_bias, (0, unit_start), (layers, piece))
    fc1_rows = jnp.pad(fc1_rows, ((0, 0), (0, held - piece)))
    vec_rows = jnp.concatenate([vec_rows.reshape(-1, held), fc1_rows])
    if packs:
        arrays = dict(qkv=self_qkv, kv=cross_kv, q=cross_q, out=cross_out, up=ffn_in, down=ffn_out)
        arrays["self_out"] = self_out
        arrays["vec"] = jnp.pad(vec_rows.T, ((0, 0), (0, 128 - vec_rows.shape[0])))
        first_size = (7 + layers) * col
        sizes = {
            "first": (held, first_size + 128),
            "attention": (held, 7 * col),
            "ffn": (held + piece, units),
        }

        def pack(jobs, wait=()):
            fed = [arrays[name] for kind, layer in jobs for name in FED[kind]]
            return call(
                partial(pack_kernel, m, n, jobs),
                [here] + fed,
                [like(sizes[kind], LOW) for kind, layer in jobs],
                0,
                scratch=[pltpu.SemaphoreType.DMA((8 * len(jobs) + 8,))],
                smem=1,
                far=len(fed),
                wait=wait,
            )

        packed = pack([("first", 0)])
        packed += pack([("ffn", 0)], [first_slots[-1], last_slots[-1]])
        for layer in range(1, layers):
            packed += pack([("attention", layer), ("ffn", layer)])
        got = []
        for index, operand in enumerate(packed):
            if index > 1:
                operand = after(operand, got[index - 2])
            tiled = operand.shape[0] == held
            got.append(lax.all_gather(operand, "fsdp", axis=0, tiled=tiled))
        w_qkv = w_rest = got[0::2]
        w_ffn = [[both] for both in got[1::2]]
        skip = [3 * col] * layers
        ordered = got[0][:, first_size : first_size + vec_rows.shape[0]].T.astype(F32)
        w_out = got[0][:, 7 * col : first_size].reshape(n, col, layers, col)
        w_out = lax.all_to_all(w_out, "ctx", 0, 0).transpose(2, 1, 0, 3).reshape(layers, col, width)
    else:
        w_out = fetch_out()
        ordered = gather_planes(vec_rows.T).T.astype(F32)
        w_qkv, w_rest, w_ffn, skip = [], [], [], [0] * layers
        for layer in range(layers):
            blocks = [columns(self_qkv, layer, i * width + group * own, own) for i in range(3)]
            w_qkv.append(gather_planes(jnp.concatenate(blocks, axis=1)))
            blocks = [columns(cross_kv, layer, i * width + c * col, col) for i in range(2)]
            blocks += [columns(cross_q, layer, c * col, col), columns(cross_out, layer, c * col, col)]
            w_rest.append(gather_planes(jnp.concatenate(blocks, axis=1)))
            blocks = [
                columns(ffn_in, layer, (n * j + m * high_c + (j + low_c) % m) * piece, piece)
                for j in range(m)
            ]
            down = lax.dynamic_slice(ffn_out, (layer, unit_start, 0), (1, piece, width))[0]
            w_ffn.append([gather_planes(jnp.concatenate(blocks, axis=1)), gather_planes(down)])
    vectors = ordered[:-layers].reshape(layers, -1, width)
    up_bias = ordered[-layers:].reshape(layers, m, held)[:, :, :piece].reshape(layers, units)
    w_sems = pltpu.SemaphoreType.DMA((2 * m,))
    w_scratch = [pltpu.VMEM((width, units), LOW), pltpu.VMEM((units, width), LOW), w_sems]
    qv_bias = lax.dynamic_slice(vectors, (0, 6, group * own), (layers, 2, own))
    ev_bias = lax.dynamic_slice(vectors, (0, 10, c * col), (layers, 1, col))
    ev_bias = jnp.pad(ev_bias, ((0, 0), (0, 0), (col, 0)))

    def own_slots(values):
        if split == 1:
            return values
        shaped = values.reshape((n // split, split, rows) + values.shape[1:])
        return shaped[:, 0].reshape((-1,) + values.shape[1:])

    def share(parts):
        if split == 1:
            return parts[0]
        total = lax.dynamic_index_in_dim(parts, part, 0, False).astype(F32)
        for other in range(1, split):
            term = lax.dynamic_index_in_dim(parts, part ^ other, 0, False)
            total = total + swap(term, other).astype(F32)
        return total

    def half_slots(width_of, kind=LOW):
        return [like((n // 2, rows, width_of), kind)] * 2

    (encoder_all,) = call(
        partial(assemble_kernel, n, rows),
        [here] + first_slots,
        [like((source_length, width), LOW)],
        0,
        smem=1,
    )

    def prepare(layer):
        return call(
            partial(cross_prepare_kernel, col, skip[layer]),
            [w_rest[layer], encoder_all, ev_bias[layer]],
            [like((2 * col, width + source_length), LOW)],
            4 * source_length * width * col,
        )[0]

    x = tokens[0]
    h1_slots = first_slots
    kept = []
    matmul = 2 * length * width
    for layer in range(layers):
        vec = vectors[layer]
        w_t = after(prepared if layer else prepare(0), h1_slots)
        near = gather_near(w_t)
        joined = layer > 0
        h1_all, q, k, v, a, self_lse, *parts = call(
            partial(self_forward_kernel, n, rows, split, layer == 0, joined, head_width),
            h1_slots
            + [vec, after(qv_bias[layer], w_t), w_qkv[layer]]
            + self_bounds
            + [w_out[layer]] * joined,
            [like((length, width), LOW), like((queries, own), LOW)]
            + [like((length, own), LOW)] * 2
            + [like((queries, own), LOW), like((queries, own // head_width), F32)]
            + half_slots(width) * joined,
            matmul * 4 * own + 4 * queries * length * own,
        )
        if not joined:
            parts = call(
                partial(self_out_kernel, n, rows, split),
                [a, w_out[layer]],
                half_slots(width),
                matmul * own,
            )
        even, odd = parts
        near, odd = lax.optimization_barrier((near, odd))
        terms = reduce_slots(even, odd)
        w_slots, where = gather_joined(w_t, near)
        x1, x2, h2, cq, mixed, cross_lse, h3, wq_t, wo_t, ek_t, ev_t = call(
            partial(mid_forward_kernel, n, len(terms), len(w_slots), where, head_width),
            [here, x] + terms + w_slots + [vec] + cross_bounds,
            [like((rows, width), F32)] * 2
            + [like((rows, width), LOW)] * 3
            + [like((rows, HEADS), F32), like((rows, width), LOW)]
            + [like((width, width), LOW)] * 2
            + [like((width, source_length), LOW)] * 2,
            4 * rows * width * (width + source_length),
            smem=1,
        )
        h3_all, g, slope, even, odd = call(
            partial(ffn_forward_kernel, n, len(w_ffn[layer])),
            gather_slots(h3) + [up_bias[layer][None]] + w_ffn[layer],
            [like((length, width), LOW)] + [like((length, units), LOW)] * 2 + half_slots(width),
            2 * matmul * units,
            scratch=w_scratch,
            far=len(w_ffn[layer]),
        )
        last = layer == layers - 1
        if last:
            result_parts = (even, odd)
        else:
            terms = reduce_slots(even, odd)
        kept.append(
            (x, x1, x2, h1_all, q, k, v, a, self_lse, h2, cq, mixed, cross_lse)
            + (h3_all, g, slope, wq_t, wo_t, ek_t, ev_t)
        )
        if last:
            continue
        prepared = prepare(layer + 1)
        outs = call(
            partial(between_kernel, len(terms), False),
            [x2] + terms + [vec, vectors[layer + 1]],
            [like((rows, width), F32), like((rows, width), LOW)],
            rows * width * 20,
        )
        x = outs[0]
        h1_slots = gather_slots(outs[1])

    r = width // (n * m)
    grad_x, e3_slots = grad_out[0], last_slots
    enc_total = jnp.zeros((source_length, width), F32)
    vec_sums = [None] * layers
    moves = [
        (i * m + p, ((n // m) * ((p - i % m) % m) + i // m) * m + p) for i in range(n) for p in range(m)
    ]

    def to_rows(summed):
        return lax.all_to_all(summed.reshape(n, r, summed.shape[1]), "ctx", 0, 0)

    def move_down(sums):
        down = sums[0][n * r :] if units == width else sums[1]
        return lax.ppermute(down, ("ctx", "fsdp"), moves)

    up_rows, down_rows = [None] * layers, [None] * layers
    finish = []
    for layer in reversed(range(layers)):
        x, x1, x2, h1_all, q, k, v, a, self_lse, h2, cq, mixed, cross_lse = kept[layer][:13]
        h3_all, g, slope, wq_t, wo_t, ek_t, ev_t = kept[layer][13:]
        vec = vectors[layer]
        if finish:
            slope = after(slope, cross_grad)
        e3_all, du, fc1_grad, even, odd = call(
            partial(ffn_backward_kernel, n, len(w_ffn[layer])),
            e3_slots + [slope] + w_ffn[layer],
            [like((length, width), LOW), like((length, units), LOW), like((1, units), F32)]
            + half_slots(width),
            2 * matmul * units,
            scratch=w_scratch,
            far=len(w_ffn[layer]),
        )
        terms = reduce_slots(even, odd)
        shapes = [like((m, n * r, units), LOW), like((m, piece + 16, width), LOW)]
        if units == width:
            shapes = [like((m, n * r + piece + 16, width), LOW)]
        ffn_grads = call(
            partial(ffn_weights_kernel, n, m),
            [here, h3_all, after(du, terms[0]), g, e3_all, fc1_grad],
            shapes,
            2 * matmul * units,
            smem=1,
        )
        x1 = after(x1, ffn_grads)
        dx1, e1, e2, dcq, even, odd, sums = call(
            partial(mid_backward_kernel, n, len(terms), head_width),
            [here, grad_x]
            + terms
            + [x1, x2, vec, wq_t, wo_t, ek_t, ev_t, cq, cross_lse]
            + cross_bounds,
            [like((rows, width), F32)]
            + [like((rows, width), LOW)] * 3
            + [like((n // 2, 2 * col, source_length), LOW)] * 2
            + [like((8, width), F32)],
            4 * rows * width * width + 10 * rows * source_length * width,
            scratch=[pltpu.VMEM((width, source_length), LOW)] * 2,
            smem=1,
        )
        ffn_sums = [reduce_planes(grad) for grad in after(ffn_grads, dx1)]
        e1_slots = gather_slots(e1)
        kv_parts = [even, odd]
        even, *odd = call(
            partial(cross_weights_kernel, n),
            [here, h2, dcq, mixed, e2] + kv_parts,
            [like((n // size, 2 * col, width + source_length), LOW) for size in (2, 4, 4)],
            4 * rows * width * width,
            scratch=[pltpu.VMEM((width, width), LOW)] * 2,
            smem=1,
            wait=[entry[2] for entry in finish[-1:]],
        )
        w_terms = reduce_slots(even, list(odd), hold=e1_slots)
        e1_own, dq, dkv, even, odd = call(
            partial(self_backward_kernel, n, split, head_width),
            e1_slots + [w_out[layer], w_qkv[layer], after(q, w_terms[0]), k, v, self_lse] + self_bounds,
            [like((queries, width), LOW), like((queries, own), LOW), like((length, 2 * own), LOW)]
            + half_slots(width),
            matmul * 4 * own + 10 * queries * length * own,
            scratch=[pltpu.VMEM((length, own), F32)] * 2,
        )
        if split > 1:
            shaped = dkv.reshape(n // split, split, rows, 2 * own)
            total = shaped[:, 0].astype(F32)
            for other in range(1, split):
                total = total + swap(shaped[:, other], other).astype(F32)
            dkv = total.astype(LOW).reshape(-1, 2 * own)
            even = dot_t(jnp.concatenate([dq, dkv], axis=1), w_qkv[layer][:, : 3 * own])
            even = even.reshape(n // 2, rows, width)
            odd = jnp.zeros_like(even)
        terms = reduce_slots(even, after(odd, w_terms))
        beside = []
        for done in finish if layer == 0 else ():
            up_rows[done[0]], down_rows[done[0]] = to_rows(done[1][0][: n * r]), move_down(done[1])
            beside += [up_rows[done[0]], down_rows[done[0]]]
        before = []
        if layer == 0:
            up_rows[0], down_rows[0] = to_rows(ffn_sums[0][: n * r]), move_down(ffn_sums)
            *ffn_grads, fc1_own = call(
                partial(place_ffn_kernel, n, m, layers),
                up_rows + down_rows,
                [like((layers, r, hidden), F32), like((layers, piece, width), F32), like((layers, piece), F32)],
                layers * r * hidden,
            )
            before = ffn_grads[:1]
        grad_x, e3, last_sums = call(
            partial(last_backward_kernel, len(terms)),
            [dx1] + terms + [x, vec],
            [like((rows, width), F32), like((rows, width), LOW), like((2, width), F32)],
            rows * width * 20,
            wait=before,
        )

        e3_slots = gather_slots(e3) if layer else None
        hold = (e3_slots[2], e3_slots[4]) if layer else terms[0]
        own_parts = [h1_all, dq, dkv, a, e1_own] if split == 1 else []
        cross_grad, enc_total, ev_sum, *enc_parts = call(
            partial(attention_weights_kernel, n, m, skip[layer], len(terms), split == 1),
            [here]
            + w_terms
            + own_parts
            + [encoder_all, w_rest[layer], after(enc_total, hold)],
            [like((m, n * r, (8 if split == 1 else 4) * col), LOW)]
            + [like((source_length, width), F32), like((2 * col, 1), F32)]
            + [like((n // 2, source_rows, width), F32)] * 2,
            8 * source_length * col * width + matmul * 4 * own,
            smem=1,
            wait=ffn_sums + beside,
        )
        if split > 1:
            qkv_grad = t_dot(own_slots(h1_all), jnp.concatenate([dq, dkv], axis=1)).astype(LOW)
            qkv_grad = share(qkv_grad.reshape(width, 3, split, col).transpose(2, 0, 1, 3))
            qkv_grad = qkv_grad.astype(LOW).reshape(n, m, r, 3 * col).transpose(1, 0, 2, 3)
            o_grad = share(t_dot(a, e1_own).astype(LOW).reshape(split, own // split, width))
            o_grad = o_grad.astype(LOW).reshape(m, r, n, col).transpose(0, 2, 1, 3)
            kv_q = jnp.split(cross_grad, [2 * col], axis=2)
            self_grad = jnp.concatenate([qkv_grad, o_grad], axis=3).reshape(m, n * r, 4 * col)
            parts = [kv_q[0], self_grad[:, :, : 3 * col], kv_q[1], self_grad[:, :, 3 * col :]]
            cross_grad = jnp.concatenate(parts, axis=2)
        both_sum = reduce_planes(cross_grad)
        finish.append((layer, ffn_sums, both_sum))
        zero = jnp.zeros((1, width), F32)
        summed = jnp.concatenate(
            [last_sums[0:1], sums[0:2], last_sums[1:2], sums[2:4], zero, zero]
            + [sums[4:6], zero, sums[6:8]]
        )
        owned_q = share(row_sum(dq).reshape(split, col))
        owned_v = share(row_sum(dkv[:, own:]).reshape(split, col))
        blank = jnp.zeros((col,), F32)
        owned = [blank] * 6 + [owned_q, owned_v, blank, blank, ev_sum[col:, 0], blank, blank]
        vec_sums[layer] = (summed, jnp.stack(owned))

    finish.sort(key=lambda entry: entry[0])
    result_terms = reduce_slots(*result_parts)
    (result,) = call(
        partial(between_kernel, len(result_terms), True),
        [kept[-1][2]] + result_terms + [vectors[-1]],
        [like((rows, width), LOW)],
        rows * width * 20,
    )
    enc_grad = total_of(reduce_slots(*after(enc_parts, grad_x), F32))
    summed = jnp.concatenate([pair[0] for pair in vec_sums])
    owned = jnp.concatenate([pair[1] for pair in vec_sums])
    summed = turn(summed, 1).reshape(-1, n, col).transpose(1, 0, 2)
    vec = total_of(reduce_slots(summed[0::2], summed[1::2], F32)) + owned
    (late,) = call(
        late_kernel,
        [entry[2] for entry in finish],
        [like((n * r, layers * 5 * col), LOW)],
        0,
        wait=[enc_grad],
    )
    late_rows = to_rows(late)
    attention_grads = call(
        partial(place_attention_kernel, n, layers),
        [late_rows] + [entry[2] for entry in finish],
        [like((layers, r, parts * width), F32) for parts in (3, 1, 1, 2, 1)],
        layers * r * 8 * width,
    )
    (vec,) = call(copy_kernel, [vec], [like(vec.shape, F32)], 0, wait=[late])
    vec = sum_planes(vec.reshape(-1, m, col // m).transpose(1, 0, 2))
    vec = vec.reshape(layers, -1, col // m)
    return (
        (result[None], grad_x[None], enc_grad[None])
        + tuple(attention_grads)
        + tuple(ffn_grads)
        + (vec[:, :3], vec[:, 3:], fc1_own)
    )


def solution(mesh):
    tokens = P("fsdp", "ctx", None)
    per_stream = P("fsdp", None)
    weight = P(None, "fsdp", None)
    vector = P(None, None, "fsdp")
    grad = P(None, ("ctx", "fsdp"), None)
    vector_grad = P(None, None, ("ctx", "fsdp"))
    return jax.shard_map(
        on_device,
        mesh=mesh,
        in_specs=(tokens,) * 3 + (per_stream,) * 3 + (weight,) * 7 + (vector,) * 2 + (P(None, "fsdp"),),
        out_specs=(tokens,) * 3 + (grad,) * 7 + (vector_grad,) * 2 + (P(None, ("ctx", "fsdp")),),
        check_vma=False,
    )
```

time: 1110 us -> 676 us (0.61)
  Pallas kernels: 77.1 us -> 235 us
  local copies, waits for them, and re-layouts: 201 us -> 52.1 us
  matrix products: 116 us -> 0 us
  blocking collectives: 95.4 us -> 0 us
  starting transfers between devices: 227 us -> 136 us
  waiting for transfers between devices: 273 us -> 197 us
  other arithmetic: 92 us -> 29.4 us
    pallas_call x8 -> x33, Pallas kernels: 77.1 us -> 235 us  [call(): pl.pallas_call(body, in_specs=[SMEM] * smem + [VMEM] * (count - smem - fa...]
    dot_general x42 -> x0, matrix products: 116 us -> none  [the longest x14 48.7 us: dot(): return jnp.dot(left, right, preferred_element_type=F32)]
    ppermute x214 -> x126, starting transfers between devices: 209 us -> 116 us  [swap(): return lax.ppermute(values, 'ctx', [(i, i ^ bits) for i in range(count)])]
    unnamed x785 -> x279, local copies, waits for them, and re-layouts: 100 us -> 15.8 us
    all_gather x4 -> x0, blocking collectives: 76.8 us -> none  [the longest x2 55.2 us: gather_planes(): return lax.all_gather(values, 'fsdp', axis=0, tiled=True)]
    ppermute x214 -> x126, waiting for transfers between devices: 242 us -> 179 us  [swap(): return lax.ppermute(values, 'ctx', [(i, i ^ bits) for i in range(count)])]
    slice x48 -> x27, local copies, waits for them, and re-layouts: 45.4 us -> 10.5 us  [the longest x3 2.15 us: on_device(): w_out[layer]]
    another operation x56 -> x11, other arithmetic: 49.4 us -> 20.8 us
  transfers between devices with their start and end apart: 238 -> 143, of which waited for: 108 -> 60; matrix products, arithmetic and copies ran while one was open for 33% -> 9% of each run, Pallas kernels for 6% -> 29%
where the time goes in v2:
time: 676 us; the launch traced here: 667 us
  Pallas kernels  235 us (35%)
  waiting for transfers between devices  197 us (29%)
  starting transfers between devices  136 us (20%)
  local copies, waits for them, and re-layouts  52.1 us (8%)
  other arithmetic  29.4 us (4%)
  between operations  16.6 us (2%)
    pallas_call x33, Pallas kernels, call(): pl.pallas_call(body, in_specs=[SMEM] * smem + [VMEM] * (count - smem - fa...  235 us
    ppermute x126, waiting for transfers between devices, swap(): return lax.ppermute(values, 'ctx', [(i, i ^ bits) for i in range(count)])  179 us
    ppermute x126, starting transfers between devices, swap(): return lax.ppermute(values, 'ctx', [(i, i ^ bits) for i in range(count)])  116 us
    another operation x10, other arithmetic  20.2 us
    unnamed x279, local copies, waits for them, and re-layouts  15.8 us
  transfers between devices with their start and end apart: 143, of which 60 were waited for; matrix products, arithmetic and copies ran while one was open for 9% of the time, Pallas kernels for 29%

profile of v2, /device:TPU:0, one launch (start us, length us, event | category | flops | bytes accessed | tf_op | source)
XLA Modules:
  0.0 666.8 jit_solution(9703901301278746387)
XLA Ops:
  34.2 6.3 collective-permute-done.26.refs_2_
  58.8 11.3 %all-gather.7.cloned.1.call-done.refs_0_.refs_10_.refs_9_.refs_11_ = bf16[1024,1280]{1,0:T(8,128)(2,1)} async-done(((bf16[256,1280]{1,0:T(8,128)(2,1)}), bf16[1024,1280]{1,0:T(8,128)(2,1)}) %all-gather.7.cloned.1.call-update) | async-done | bytes 2621456 | tf_op jit(solution)/shard_map/all_gather | solution.py:819
  85.0 13.7 %shard_map.258 = (bf16[1024,1024]{1,0:T(8,128)(2,1)}, bf16[1024,128]{1,0:T(8,128)(2,1)}, bf16[1024,128]{1,0:T(8,128)(2,1)}, bf16[1024,128]{1,0:T(8,128)(2,1)}, b...) custom-call(bf16[160,1024]{1,0:T(8,128)(2,1)} %copy-done.11, bf16[160,1024]{1,0:T(8,128)(2,1)} %copy-done.24, ...), custom_call_target="tpu_custom_call" | custom-call | flops 1610612736 | bytes 8463360 | tf_op jit(solution)/shard_map/pallas_call | solution.py:178
  135.4 6.4 collective-permute-done.12.refs_4_
  142.6 8.0 %shard_map.260 = (f32[128,1024]{1,0:T(8,128)}, f32[128,1024]{1,0:T(8,128)}, bf16[128,1024]{1,0:T(8,128)(2,1)}, bf16[128,1024]{1,0:T(8,128)(2,1)}, bf16[128,1024]...) custom-call(s32[2]{0:T(128)} %pad_add_fusion.refs_0_, ...), custom_call_target="tpu_custom_call" | custom-call | flops 671088640 | bytes 14219272 | tf_op jit(solution)/shard_map/pallas_call | solution.py:178
  166.6 11.9 %shard_map.262 = (bf16[1024,1024]{1,0:T(8,128)(2,1)}, bf16[1024,1024]{1,0:T(8,128)(2,1)}, bf16[1024,1024]{1,0:T(8,128)(2,1)}, bf16[4,128,1024]{2,1,0:T(8,128)(2,1)}, bf16[4,128,1024]{2,1,0:T(8,128)(2,1)}) custom-call(bf16[128,1024]{1,0:T(8,128)(2,1)} %get-tuple-element.168.refs_0_, bf16[128,1024]{1,0:T(8,128)(2,1)} %copy-done.115, ...), custom_call_target="tpu_custom_call" | custom-call | flops 4294967296 | bytes 14684160 | tf_op jit(solution)/shard_map/pallas_call | solution.py:178
  223.7 13.7 %shard_map.266 = (bf16[1024,1024]{1,0:T(8,128)(2,1)}, bf16[1024,128]{1,0:T(8,128)(2,1)}, bf16[1024,128]{1,0:T(8,128)(2,1)}, bf16[1024,128]{1,0:T(8,128)(2,1)}, b...) custom-call(bf16[128,1024]{1,0:T(8,128)(2,1)} %get-tuple-element.173, ...), custom_call_target="tpu_custom_call" | custom-call | flops 1610612736 | bytes 9511936 | tf_op jit(solution)/shard_map/pallas_call | solution.py:178
  241.8 7.5 %collective-permute-done.49 = bf16[128,1280]{1,0:T(8,128)(2,1)S(1)} collective-permute-done((bf16[128,1280]{1,0:T(8,128)(2,1)S(1)}, bf16[128,1280]{1,0:T(8,128)(2,1)S(1)}, u32[]{:S(2)}, u32[]{:S(2)}) %collective-permute-start.49) | collective-permute-done | bytes 327712 | tf_op jit(solution)/shard_map/ppermute | solution.py:23
  267.5 8.2 %shard_map.267 = (f32[128,1024]{1,0:T(8,128)}, f32[128,1024]{1,0:T(8,128)}, bf16[128,1024]{1,0:T(8,128)(2,1)}, bf16[128,1024]{1,0:T(8,128)(2,1)}, bf16[128,1024]...) custom-call(s32[2]{0:T(128)} %pad_add_fusion.refs_0_, ...), custom_call_target="tpu_custom_call" | custom-call | flops 671088640 | bytes 14481416 | tf_op jit(solution)/shard_map/pallas_call | solution.py:178
  291.6 11.9 %shard_map.268 = (bf16[1024,1024]{1,0:T(8,128)(2,1)}, bf16[1024,1024]{1,0:T(8,128)(2,1)}, bf16[1024,1024]{1,0:T(8,128)(2,1)}, bf16[4,128,1024]{2,1,0:T(8,128)(2,1)}, bf16[4,128,1024]{2,1,0:T(8,128)(2,1)}) custom-call(bf16[128,1024]{1,0:T(8,128)(2,1)} %get-tuple-element.184.refs_0_, bf16[128,1024]{1,0:T(8,128)(2,1)} %copy-done.110, ...), custom_call_target="tpu_custom_call" | custom-call | flops 4294967296 | bytes 14684160 | tf_op jit(solution)/shard_map/pallas_call | solution.py:178
  304.3 11.2 %shard_map.270 = (bf16[1024,1024]{1,0:T(8,128)(2,1)}, bf16[1024,1024]{1,0:T(8,128)(2,1)}, f32[1,1024]{1,0:T(1,128)}, bf16[4,128,1024]{2,1,0:T(8,128)(2,1)}, bf16[4,128,1024]{2,1,0:T(8,128)(2,1)}) custom-call(bf16[128,1024]{1,0:T(8,128)(2,1)} %bitcast.246, bf16[128,1024]{1,0:T(8,128)(2,1)} %copy-done.112, bf16[128,1024]{1,0:T(8,128)(2,1)} %copy-done.65, ...), custom_call_target="tpu_custom_call" | custom-call | flops 4294967296 | bytes 14684160 | tf_op jit(solution)/shard_map/pallas_call | solution.py:178
  324.7 10.1 %shard_map.271 = bf16[4,528,1024]{2,1,0:T(8,128)(2,1)} custom-call(s32[2]{0:T(128)} %pad_add_fusion.refs_0_, bf16[1024,1024]{1,0:T(8,128)(2,1)} %get-tuple-element.193.refs_1_, bf16[1024,1024]{1,0:T(8,128)(2,1)} %get-tuple-element.195.refs_2_, bf16[1024,1024]{1,0:T(8,128)(2,1)} %get-tuple-element.196.refs_3_, bf16[1024,1024]{1,0:T(8,128)(2,1)} %get-tuple-element.197.refs_4_, ...), custom_call_target="tpu_custom_call" | custom-call | flops 4294967296 | bytes 12718088 | tf_op jit(solution)/shard_map/pallas_call | solution.py:178
  337.2 10.6 %shard_map.272 = (f32[128,1024]{1,0:T(8,128)}, bf16[128,1024]{1,0:T(8,128)(2,1)}, bf16[128,1024]{1,0:T(8,128)(2,1)}, bf16[128,1024]{1,0:T(8,128)(2,1)}, bf16[4,2...) custom-call(s32[2]{0:T(128)} %pad_add_fusion.refs_0_, bf16[128,1024]{1,0:T(8,128)(2,1)} %bitcast.247, ...), custom_call_target="tpu_custom_call" | custom-call | flops 872415232 | bytes 10582024 | tf_op jit(solution)/shard_map/pallas_call | solution.py:178
  355.7 6.4 collective-permute-done.73.refs_2_
  376.3 16.8 %shard_map.274 = (bf16[1024,1024]{1,0:T(8,128)(2,1)}, bf16[1024,128]{1,0:T(8,128)(2,1)}, bf16[1024,256]{1,0:T(8,128)(2,1)}, bf16[4,128,1024]{2,1,0:T(8,128)(2,1)}, bf16[4,128,1024]{2,1,0:T(8,128)(2,1)}) custom-call(bf16[128,1024]{1,0:T(8,128)(2,1)} %get-tuple-element.207.refs_0_, bf16[128,1024]{1,0:T(8,128)(2,1)} %copy-done.101, ...), custom_call_target="tpu_custom_call" | custom-call | flops 2415919104 | bytes 9981952 | tf_op jit(solution)/shard_map/pallas_call | solution.py:178
  393.1 10.0 %collective-permute-done.84.refs_4_ = bf16[256,1280]{1,0:T(8,128)(2,1)S(1)} collective-permute-done((bf16[256,1280]{1,0:T(8,128)(2,1)S(1)}, bf16[256,1280]{1,0:T(8,128)(2,1)S(1)}, u32[]{:S(2)}, u32[]{:S(2)}) %collective-permute-start.84) | collective-permute-done | bytes 655392 | tf_op jit(solution)/shard_map/ppermute | solution.py:23
  435.8 8.2 %shard_map.276 = (bf16[4,256,1024]{2,1,0:T(8,128)(2,1)}, f32[256,1024]{1,0:T(8,128)}, f32[256,1]{1,0:T(8,128)}, f32[4,32,1024]{2,1,0:T(8,128)}, f32[4,32,1024]{2,1,0:T(8,128)}) custom-call(s32[2]{0:T(128)} %pad_add_fusion.refs_0_, f32[256,1280]{1,0:T(8,128)} %slice_bitcast_fusion.1.refs_1_, bf16[256,1280]{1,0:T(8,128)(2,1)} %copy-done.33, ...), custom_call_target="tpu_custom_call" | custom-call | flops 1342177280 | bytes 16122888 | tf_op jit(solution)/shard_map/pallas_call | solution.py:178
  452.4 11.2 %shard_map.277 = (bf16[1024,1024]{1,0:T(8,128)(2,1)}, bf16[1024,1024]{1,0:T(8,128)(2,1)}, f32[1,1024]{1,0:T(1,128)}, bf16[4,128,1024]{2,1,0:T(8,128)(2,1)}, bf16[4,128,1024]{2,1,0:T(8,128)(2,1)}) custom-call(bf16[128,1024]{1,0:T(8,128)(2,1)} %get-tuple-element.229.refs_0_, bf16[128,1024]{1,0:T(8,128)(2,1)} %copy-done.120, bf16[128,1024]{1,0:T(8,128)(2,1)} %copy-done.73, ...), custom_call_target="tpu_custom_call" | custom-call | flops 4294967296 | bytes 14684160 | tf_op jit(solution)/shard_map/pallas_call | solution.py:178
  472.7 10.1 %shard_map.278 = bf16[4,528,1024]{2,1,0:T(8,128)(2,1)} custom-call(s32[2]{0:T(128)} %pad_add_fusion.refs_0_, bf16[1024,1024]{1,0:T(8,128)(2,1)} %get-tuple-element.243.refs_1_, bf16[1024,1024]{1,0:T(8,128)(2,1)} %get-tuple-element.245.refs_2_, bf16[1024,1024]{1,0:T(8,128)(2,1)} %get-tuple-element.246.refs_3_, bf16[1024,1024]{1,0:T(8,128)(2,1)} %get-tuple-element.247.refs_4_, ...), custom_call_target="tpu_custom_call" | custom-call | flops 4294967296 | bytes 12718088 | tf_op jit(solution)/shard_map/pallas_call | solution.py:178
  484.1 10.7 %shard_map.279 = (f32[128,1024]{1,0:T(8,128)}, bf16[128,1024]{1,0:T(8,128)(2,1)}, bf16[128,1024]{1,0:T(8,128)(2,1)}, bf16[128,1024]{1,0:T(8,128)(2,1)}, bf16[4,2...) custom-call(s32[2]{0:T(128)} %pad_add_fusion.refs_0_, ...), custom_call_target="tpu_custom_call" | custom-call | flops 872415232 | bytes 10844168 | tf_op jit(solution)/shard_map/pallas_call | solution.py:178
  523.6 17.1 %shard_map.281 = (bf16[1024,1024]{1,0:T(8,128)(2,1)}, bf16[1024,128]{1,0:T(8,128)(2,1)}, bf16[1024,256]{1,0:T(8,128)(2,1)}, bf16[4,128,1024]{2,1,0:T(8,128)(2,1)}, bf16[4,128,1024]{2,1,0:T(8,128)(2,1)}) custom-call(bf16[128,1024]{1,0:T(8,128)(2,1)} %get-tuple-element.257.refs_0_, bf16[128,1024]{1,0:T(8,128)(2,1)} %copy-done.102, ...), custom_call_target="tpu_custom_call" | custom-call | flops 2415919104 | bytes 10768384 | tf_op jit(solution)/shard_map/pallas_call | solution.py:178
  540.7 10.2 %collective-permute-done.112.refs_3_ = bf16[256,1280]{1,0:T(8,128)(2,1)} collective-permute-done((bf16[256,1280]{1,0:T(8,128)(2,1)S(1)}, bf16[256,1280]{1,0:T(8,128)(2,1)}, u32[]{:S(2)}, u32[]{:S(2)}) %collective-permute-start.112) | collective-permute-done | bytes 655392 | tf_op jit(solution)/shard_map/ppermute | solution.py:23
  571.5 8.5 %shard_map.284 = (bf16[4,256,1024]{2,1,0:T(8,128)(2,1)}, f32[256,1024]{1,0:T(8,128)}, f32[256,1]{1,0:T(8,128)}, f32[4,32,1024]{2,1,0:T(8,128)}, f32[4,32,1024]{2,1,0:T(8,128)}) custom-call(s32[2]{0:T(128)} %pad_add_fusion.refs_0_, f32[256,1280]{1,0:T(8,128)} %slice_bitcast_fusion.refs_1_, bf16[256,1280]{1,0:T(8,128)(2,1)} %collective-permute-done.111.refs_2_, ...), custom_call_target="tpu_custom_call" | custom-call | flops 1342177280 | bytes 16909320 | tf_op jit(solution)/shard_map/pallas_call | solution.py:178
  599.1 13.9 %collective-permute-start.63 = (bf16[128,1024]{1,0:T(8,128)(2,1)}, bf16[128,1024]{1,0:T(8,128)(2,1)S(1)}, u32[]{:S(2)}, u32[]{:S(2)}) collective-permute-start(bf16[128,1024]{1,0:T(8,128)(2,1)} %get-tuple-element.385), channel_id=1, source_target_pairs={{0,16},{4,20},{8,24},{12,28},{16,0},{20,4},{24,8},{28,12},{1,17},{... | collective-permute-start | bytes 786440 | tf_op jit(solution)/shard_map/ppermute | solution.py:23
  (730 shorter events, 396.4 us)
Async XLA Ops:
  7.2 62.9 %all-gather.7.cloned.1.call-start = ((), (), s32[]{:S(2)}) async-start(), calls=%async_computation.8 | async-start | bytes 3276800 | tf_op jit(solution)/shard_map/all_gather | solution.py:819
  12.4 153.4 %all-gather.11.cloned.1.call-start = ((), (), s32[]{:S(2)}) async-start(), calls=%async_computation.14 | async-start | bytes 5242880 | tf_op jit(solution)/shard_map/all_gather | solution.py:819
  75.2 29.6 %collective-permute-start.8 = (bf16[256,1280]{1,0:T(8,128)(2,1)}, bf16[256,1280]{1,0:T(8,128)(2,1)S(1)}, u32[]{:S(2)}, u32[]{:S(2)}) collective-permute-start(bf16[256,1280]{1,0:T(8,128)(2,1)} %shard_map.257.refs_6_), channel_id=1, source_target_pairs={{0,8},{4,12},{8,0},{12,4},{16,24},{20,28},{24,16},{28,20},{1,9},{5... | collective-permute-start | bytes 1966088 | tf_op jit(solution)/shard_map/ppermute | solution.py:23
  76.6 28.1 %collective-permute-start.9 = (bf16[256,1280]{1,0:T(8,128)(2,1)}, bf16[256,1280]{1,0:T(8,128)(2,1)S(1)}, u32[]{:S(2)}, u32[]{:S(2)}) collective-permute-start(bf16[256,1280]{1,0:T(8,128)(2,1)} %shard_map.257.refs_6_), channel_id=1, source_target_pairs={{0,16},{4,20},{8,24},{12,28},{16,0},{20,4},{24,8},{28,12},{1,17},{... | collective-permute-start | bytes 1966088 | tf_op jit(solution)/shard_map/ppermute | solution.py:23
  82.5 134.7 %all-gather.9.cloned.1.call-start = ((), (), s32[]{:S(2)}) async-start(), calls=%async_computation.9 | async-start | bytes 2293760 | tf_op jit(solution)/shard_map/all_gather | solution.py:819
  106.6 35.2 %collective-permute-start.16 = (bf16[768,1280]{1,0:T(8,128)(2,1)}, bf16[768,1280]{1,0:T(8,128)(2,1)}, u32[]{:S(2)}, u32[]{:S(2)}) collective-permute-start(bf16[768,1280]{1,0:T(8,128)(2,1)} %pad_maximum_fusion), channel_id=1, source_target_pairs={{0,4},{4,0},{8,12},{12,8},{16,20},{20,16},{24,28},{28,24},{1,5},{5... | collective-permute-start | bytes 5898248 | tf_op jit(solution)/shard_map/ppermute | solution.py:23
  114.3 177.0 %all-gather.13.cloned.1.call-start = ((), (), s32[]{:S(2)}) async-start(), calls=%async_computation.15 | async-start | bytes 5242880 | tf_op jit(solution)/shard_map/all_gather | solution.py:819
  178.9 255.8 %reduce-scatter.5.cloned.1.call-start = ((), (), s32[]{:S(2)}) async-start(), calls=%async_computation.10 | async-start | bytes 5406720 | tf_op jit(solution)/shard_map/reduce_scatter | solution.py:132
  238.9 27.1 %collective-permute-start.51 = (bf16[768,1280]{1,0:T(8,128)(2,1)S(1)}, bf16[768,1280]{1,0:T(8,128)(2,1)S(1)}, u32[]{:S(2)}, u32[]{:S(2)}) collective-permute-start(bf16[768,1280]{1,0:T(8,128)(2,1)S(1)} %pad_maximum_fusion.1), channel_id=1, source_target_pairs={{0,4},{4,0},{8,12},{12,8},{16,20},{20,16},{24,28},{28,24},{1,5},{5... | collective-permute-start | bytes 5898248 | tf_op jit(solution)/shard_map/ppermute | solution.py:23
  347.8 147.0 %reduce-scatter.7.cloned.1.call-start = ((), (), s32[]{:S(2)}) async-start(), calls=%async_computation.11 | async-start | bytes 2621440 | tf_op jit(solution)/shard_map/reduce_scatter | solution.py:132
  371.6 21.5 %collective-permute-start.82 = (bf16[256,1280]{1,0:T(8,128)(2,1)S(1)}, bf16[256,1280]{1,0:T(8,128)(2,1)S(1)}, u32[]{:S(2)}, u32[]{:S(2)}) collective-permute-start(bf16[256,1280]{1,0:T(8,128)(2,1)S(1)} %get-tuple-element.224), channel_id=1, source_target_pairs={{0,8},{4,12},{8,0},{12,4},{16,24},{20,28},{24,16},{28,20},{1,9},{5... | collective-permute-start | bytes 1966088 | tf_op jit(solution)/shard_map/ppermute | solution.py:23
  372.7 20.5 %collective-permute-start.83 = (bf16[256,1280]{1,0:T(8,128)(2,1)S(1)}, bf16[256,1280]{1,0:T(8,128)(2,1)S(1)}, u32[]{:S(2)}, u32[]{:S(2)}) collective-permute-start(bf16[256,1280]{1,0:T(8,128)(2,1)S(1)} %get-tuple-element.225), channel_id=1, source_target_pairs={{0,16},{4,20},{8,24},{12,28},{16,0},{20,4},{24,8},{28,12},{1,17},{... | collective-permute-start | bytes 1966088 | tf_op jit(solution)/shard_map/ppermute | solution.py:23
  373.7 29.4 %collective-permute-start.84 = (bf16[256,1280]{1,0:T(8,128)(2,1)S(1)}, bf16[256,1280]{1,0:T(8,128)(2,1)S(1)}, u32[]{:S(2)}, u32[]{:S(2)}) collective-permute-start(bf16[256,1280]{1,0:T(8,128)(2,1)S(1)} %get-tuple-element.226), channel_id=1, source_target_pairs={{0,24},{4,28},{8,16},{12,20},{16,8},{20,12},{24,0},{28,4},{1,25},{... | collective-permute-start | bytes 1966088 | tf_op jit(solution)/shard_map/ppermute | solution.py:23
  444.1 127.4 %reduce-scatter.9.cloned.1.call-start = ((), (), s32[]{:S(2)}) async-start(), calls=%async_computation.12 | async-start | bytes 5406720 | tf_op jit(solution)/shard_map/reduce_scatter | solution.py:132
  511.1 39.8 %collective-permute-start.61 = (bf16[4,128,1024]{2,1,0:T(8,128)(2,1)S(1)}, bf16[4,128,1024]{2,1,0:T(8,128)(2,1)S(1)}, u32[]{:S(2)}, u32[]{:S(2)}) collective-permute-start(bf16[4,128,1024]{2,1,0:T(8,128)(2,1)S(1)} %copy-done.95), channel_id=1, source_target_pairs={{0,4},{4,0},{8,12},{12,8},{16,20},{20,16},{24,28},{28,24},{1,5},{5... | collective-permute-start | bytes 3145736 | tf_op jit(solution)/shard_map/ppermute | solution.py:23
  518.9 21.8 %collective-permute-start.111 = (bf16[256,1280]{1,0:T(8,128)(2,1)S(1)}, bf16[256,1280]{1,0:T(8,128)(2,1)}, u32[]{:S(2)}, u32[]{:S(2)}) collective-permute-start(bf16[256,1280]{1,0:T(8,128)(2,1)S(1)} %get-tuple-element.274), channel_id=1, source_target_pairs={{0,8},{4,12},{8,0},{12,4},{16,24},{20,28},{24,16},{28,20},{1,9},{5... | collective-permute-start | bytes 1966088 | tf_op jit(solution)/shard_map/ppermute | solution.py:23
  519.9 30.9 %collective-permute-start.112 = (bf16[256,1280]{1,0:T(8,128)(2,1)S(1)}, bf16[256,1280]{1,0:T(8,128)(2,1)}, u32[]{:S(2)}, u32[]{:S(2)}) collective-permute-start(bf16[256,1280]{1,0:T(8,128)(2,1)S(1)} %get-tuple-element.275), channel_id=1, source_target_pairs={{0,16},{4,20},{8,24},{12,28},{16,0},{20,4},{24,8},{28,12},{1,17},{... | collective-permute-start | bytes 1966088 | tf_op jit(solution)/shard_map/ppermute | solution.py:23
  521.0 29.9 %collective-permute-start.113 = (bf16[256,1280]{1,0:T(8,128)(2,1)S(1)}, bf16[256,1280]{1,0:T(8,128)(2,1)}, u32[]{:S(2)}, u32[]{:S(2)}) collective-permute-start(bf16[256,1280]{1,0:T(8,128)(2,1)S(1)} %get-tuple-element.276), channel_id=1, source_target_pairs={{0,24},{4,28},{8,16},{12,20},{16,8},{20,12},{24,0},{28,4},{1,25},{... | collective-permute-start | bytes 1966088 | tf_op jit(solution)/shard_map/ppermute | solution.py:23
  559.6 79.7 %reduce-scatter.11.cloned.1.call-start = ((), (), s32[]{:S(2)}) async-start(), calls=%async_computation.13 | async-start | bytes 2621440 | tf_op jit(solution)/shard_map/reduce_scatter | solution.py:132
  581.0 66.4 %collective-permute-start.62 = (bf16[128,1024]{1,0:T(8,128)(2,1)}, bf16[128,1024]{1,0:T(8,128)(2,1)}, u32[]{:S(2)}, u32[]{:S(2)}) collective-permute-start(bf16[128,1024]{1,0:T(8,128)(2,1)} %get-tuple-element.386), channel_id=1, source_target_pairs={{0,8},{4,12},{8,0},{12,4},{16,24},{20,28},{24,16},{28,20},{1,9},{5... | collective-permute-start | bytes 786440 | tf_op jit(solution)/shard_map/ppermute | solution.py:23
  586.4 26.6 %all-to-all-start.1 = ((bf16[8,32,1024]{2,1,0:T(8,128)(2,1)}), bf16[8,32,1024]{2,1,0:T(8,128)(2,1)S(1)}, u32[]{:S(2)}, u32[]{:S(2)}) async-start(bf16[8,32,1024]{2,1,0:T(8,128)(2,1)} %bitcast.67), calls=%async_computation.4 | async-start | bytes 1048576 | tf_op jit(solution)/shard_map/all_to_all | solution.py:965
  592.7 24.8 %collective-permute-start.115 = (bf16[128,1024]{1,0:T(8,128)(2,1)}, bf16[128,1024]{1,0:T(8,128)(2,1)S(1)}, u32[]{:S(2)}, u32[]{:S(2)}) collective-permute-start(bf16[128,1024]{1,0:T(8,128)(2,1)} %get-tuple-element.374), channel_id=1, source_target_pairs={{0,8},{4,12},{8,0},{12,4},{16,24},{20,28},{24,16},{28,20},{1,9},{5... | collective-permute-start | bytes 786440 | tf_op jit(solution)/shard_map/ppermute | solution.py:23
  597.7 20.4 %collective-permute-start.117 = (bf16[128,1024]{1,0:T(8,128)(2,1)}, bf16[128,1024]{1,0:T(8,128)(2,1)S(1)}, u32[]{:S(2)}, u32[]{:S(2)}) collective-permute-start(bf16[128,1024]{1,0:T(8,128)(2,1)} %get-tuple-element.372), channel_id=1, source_target_pairs={{0,24},{4,28},{8,16},{12,20},{16,8},{20,12},{24,0},{28,4},{1,25},{... | collective-permute-start | bytes 786440 | tf_op jit(solution)/shard_map/ppermute | solution.py:23
  599.1 52.1 %collective-permute-start.63 = (bf16[128,1024]{1,0:T(8,128)(2,1)}, bf16[128,1024]{1,0:T(8,128)(2,1)S(1)}, u32[]{:S(2)}, u32[]{:S(2)}) collective-permute-start(bf16[128,1024]{1,0:T(8,128)(2,1)} %get-tuple-element.385), channel_id=1, source_target_pairs={{0,16},{4,20},{8,24},{12,28},{16,0},{20,4},{24,8},{28,12},{1,17},{... | collective-permute-start | bytes 786440 | tf_op jit(solution)/shard_map/ppermute | solution.py:23
  (247 other events, 1803.5 us)
Sparse Core Ops, SparseCore 0:
  12.6 57.4 all-gather.6
  71.7 79.5 all-gather.10
  152.8 39.9 all-gather.8
  194.2 79.6 all-gather.12
  347.9 76.6 reduce-scatter.4
  444.2 41.5 reduce-scatter.6
  494.9 76.5 reduce-scatter.8
  580.2 45.0 reduce-scatter.10

commit v3 on v2

--- a/solution.py
+++ b/solution.py
@@ -15,7 +15,7 @@
 VMEM = pl.BlockSpec(memory_space=pltpu.VMEM)
 SMEM = pl.BlockSpec(memory_space=pltpu.SMEM)
 FAR = pl.BlockSpec(memory_space=pl.ANY)
-VMEM_BYTES = 56 * 2**20
+VMEM_BYTES = 60 * 2**20
 
 
 def swap(values, bits):
@@ -60,29 +60,17 @@
     return gather_slots(rows), [(k, 0) for k in range(count)]
 
 
-def send_chip(chip, kind):
-    count = lax.axis_size("ctx")
-    if count == 8:
-        return [chip[0]] + [swap(chip[i].astype(kind), 2 * i) for i in (1, 2, 3)]
-    bit = count // 4
-    while bit:
-        chip = chip[:bit] + swap(chip[bit : 2 * bit].astype(kind), 2 * bit).astype(F32)
-        bit //= 2
-    return [chip[0]]
-
-
 def reduce_slots(even, odd, kind=LOW, hold=None):
     count = lax.axis_size("ctx")
-    if isinstance(odd, list):
-        odd = jnp.concatenate([swap(block, 1) for block in odd])
-    else:
-        odd = swap(odd.astype(kind), 1)
-    chip = even.astype(F32) + odd.astype(F32)
+    odd = [swap(block.astype(kind), 1) for block in (odd if isinstance(odd, list) else [odd])]
     if count == 8:
+        size = odd[0].shape[0]
+        chip = [even[i].astype(F32) + odd[i // size][i % size].astype(F32) for i in range(4)]
         sent = [chip[i].astype(kind) for i in (1, 2, 3)]
         if hold is not None:
             sent = after(sent, hold)
         return [chip[0]] + [swap(sent[i], 2 * i + 2) for i in range(3)]
+    chip = even.astype(F32) + jnp.concatenate(odd).astype(F32)
     bit = count // 4
     while bit:
         chip = chip[:bit] + swap(chip[bit : 2 * bit].astype(kind), 2 * bit).astype(F32)
@@ -167,8 +155,17 @@
     return lax.dot_general(left, right, (((0,), (0,)), ((), ())), preferred_element_type=F32)
 
 
-def call(kernel, ins, outs, flops, scratch=(), smem=0, far=0, wait=()):
+def call(kernel, ins, outs, flops, scratch=(), smem=0, far=0, wait=(), steps=0, tiles=None):
     count, extra = len(ins), len(wait)
+
+    def spec(index, array):
+        if not steps and not (tiles and index in tiles):
+            return VMEM
+        block, axis = (tiles or {}).get(index, (array.shape, None))
+        dims = len(block)
+        if not steps:
+            return pl.BlockSpec(block, lambda: (0,) * dims)
+        return pl.BlockSpec(block, lambda i: tuple(i if d == axis else 0 for d in range(dims)))
 
     def body(*refs):
         kernel(*refs[:count], *refs[count + extra :])
@@ -177,8 +174,11 @@
     moved += sum(a.size * a.dtype.itemsize for a in outs)
     return pl.pallas_call(
         body,
-        in_specs=[SMEM] * smem + [VMEM] * (count - smem - far) + [FAR] * (far + extra),
-        out_specs=[VMEM] * len(outs),
+        grid=(steps,) if steps else (),
+        in_specs=[SMEM] * smem
+        + [spec(i, ins[i]) for i in range(smem, count - far)]
+        + [FAR] * (far + extra),
+        out_specs=[spec(count + i, array) for i, array in enumerate(outs)],
         out_shape=outs,
         scratch_shapes=list(scratch),
         compiler_params=pltpu.CompilerParams(vmem_limit_bytes=VMEM_BYTES),
@@ -194,10 +194,21 @@
     return pl.ds(pl.multiple_of(rows * size, size), size)
 
 
+def join_rows(blocks, out_ref):
+    rows = blocks[0].shape[0]
+    for k, block in enumerate(blocks):
+        out_ref[k * rows : (k + 1) * rows] = block[...]
+
+
 def put_slots(even_ref, odd_ref, index, values):
     rows = even_ref.shape[1]
-    even_ref[index] = values[:rows].astype(LOW)
-    odd_ref[index] = values[rows:].astype(LOW)
+    for i in range(values.shape[0] // (2 * rows)):
+        even_ref[index + i] = values[2 * i * rows : (2 * i + 1) * rows].astype(LOW)
+        odd_ref[index + i] = values[(2 * i + 1) * rows : (2 * i + 2) * rows].astype(LOW)
+
+
+def pairs_at_once(n, rows, split):
+    return 2 if split == 1 and n % 4 == 0 and n * rows <= 1024 else 1
 
 
 def self_forward_kernel(n, rows, split, raw, joined, head_width, *refs):
@@ -224,9 +235,10 @@
         k_ref[at] = z[:, own : 2 * own].astype(LOW)
         v_ref[at] = (z[:, 2 * own :] + bias_ref[1:2]).astype(LOW)
 
-    step = 2 * rows // split
-
-    @pl.loop(0, n // 2)
+    wide = pairs_at_once(n, rows, split)
+    step = 2 * rows * wide // split
+
+    @pl.loop(0, n // 2 // wide)
     def _(i):
         at = tile_rows(i, step)
         mask = (place_ref[...] >= low_ref[at]) & (place_ref[...] <= high_ref[at])
@@ -243,7 +255,7 @@
         a_ref[at] = a
         lse_ref[at] = jnp.concatenate(masses, axis=1)
         if joined:
-            put_product(split, a, wo_ref, *out_refs, i)
+            put_product(split, a, wo_ref, *out_refs, i * wide)
 
 
 def put_product(split, a, wo_ref, even_ref, odd_ref, i):
@@ -254,11 +266,12 @@
 
 
 def self_out_kernel(n, rows, split, a_ref, wo_ref, even_ref, odd_ref):
-    step = 2 * rows // split
-
-    @pl.loop(0, n // 2)
+    wide = pairs_at_once(n, rows, split)
+    step = 2 * rows * wide // split
+
+    @pl.loop(0, n // 2 // wide)
     def _(i):
-        put_product(split, a_ref[tile_rows(i, step)], wo_ref, even_ref, odd_ref, i)
+        put_product(split, a_ref[tile_rows(i, step)], wo_ref, even_ref, odd_ref, i * wide)
 
 
 def mid_forward_kernel(n, terms, arrays, where, head_width, here_ref, *refs):
@@ -319,49 +332,48 @@
     blocks, refs = refs[:n], refs[n:]
     bias_ref, refs = refs[0], refs[1:]
     sources, refs = refs[:sources], refs[sources:]
-    h_ref, g_ref, slope_ref, even_ref, odd_ref, up_ref, down_ref, sems = refs
-    rows = blocks[0].shape[0]
-    copies = copies_of(sources, up_ref, down_ref, sems)
-    for copy in copies:
-        copy.start()
-    for k in range(n):
-        h_ref[k * rows : (k + 1) * rows] = blocks[k][...]
-    for copy in copies:
-        copy.wait()
-
-    @pl.loop(0, n // 2)
-    def _(i):
-        at = tile_rows(i, 2 * rows)
-        u = dot(h_ref[at], up_ref[...]) + bias_ref[...]
-        share = 0.5 + 0.5 * lax.erf(u * 0.7071067811865476)
-        g = (u * share).astype(LOW)
-        g_ref[at] = g
-        slope_ref[at] = (share + u * (jnp.exp(-0.5 * u * u) * 0.3989422804014327)).astype(LOW)
-        put_slots(even_ref, odd_ref, i, dot(g, down_ref[...]))
+    g_ref, slope_ref, even_ref, odd_ref, h_ref, up_ref, down_ref, sems = refs
+    step = pl.program_id(0)
+
+    @pl.when(step == 0)
+    def _():
+        copies = copies_of(sources, up_ref, down_ref, sems)
+        for copy in copies:
+            copy.start()
+        join_rows(blocks, h_ref)
+        for copy in copies:
+            copy.wait()
+
+    u = dot(h_ref[tile_rows(step, g_ref.shape[0])], up_ref[...]) + bias_ref[...]
+    share = 0.5 + 0.5 * lax.erf(u * 0.7071067811865476)
+    g = (u * share).astype(LOW)
+    g_ref[...] = g
+    slope_ref[...] = (share + u * (jnp.exp(-0.5 * u * u) * 0.3989422804014327)).astype(LOW)
+    put_slots(even_ref, odd_ref, 0, dot(g, down_ref[...]))
 
 
 def ffn_backward_kernel(n, sources, *refs):
     blocks, refs = refs[:n], refs[n:]
     slope_ref, refs = refs[0], refs[1:]
     sources, refs = refs[:sources], refs[sources:]
-    e_ref, du_ref, sum_ref, even_ref, odd_ref, up_ref, down_ref, sems = refs
-    rows = blocks[0].shape[0]
-    copies = copies_of(sources, up_ref, down_ref, sems)
-    for copy in copies:
-        copy.start()
-    for k in range(n):
-        e_ref[k * rows : (k + 1) * rows] = blocks[k][...]
-    sum_ref[...] = jnp.zeros_like(sum_ref)
-    for copy in copies:
-        copy.wait()
-
-    @pl.loop(0, n // 2)
-    def _(i):
-        at = tile_rows(i, 2 * rows)
-        du = (dot_t(e_ref[at], down_ref[...]) * slope_ref[at].astype(F32)).astype(LOW)
-        du_ref[at] = du
-        sum_ref[...] += row_sum(du)
-        put_slots(even_ref, odd_ref, i, dot_t(du, up_ref[...]))
+    du_ref, sum_ref, even_ref, odd_ref, e_ref, up_ref, down_ref, sems = refs
+    step = pl.program_id(0)
+
+    @pl.when(step == 0)
+    def _():
+        copies = copies_of(sources, up_ref, down_ref, sems)
+        for copy in copies:
+            copy.start()
+        join_rows(blocks, e_ref)
+        sum_ref[...] = jnp.zeros_like(sum_ref)
+        for copy in copies:
+            copy.wait()
+
+    grad = dot_t(e_ref[tile_rows(step, du_ref.shape[0])], down_ref[...])
+    du = (grad * slope_ref[...].astype(F32)).astype(LOW)
+    du_ref[...] = du
+    sum_ref[...] += row_sum(du)
+    put_slots(even_ref, odd_ref, 0, dot_t(du, up_ref[...]))
 
 
 def pack_kernel(m, n, jobs, where_ref, *refs):
@@ -423,8 +435,10 @@
         out_ref[:, layer * size : (layer + 1) * size] = ref[:, :size]
 
 
-def copy_kernel(in_ref, out_ref):
-    out_ref[...] = in_ref[...]
+def copy_kernel(*refs):
+    count = len(refs) // 2
+    for in_ref, out_ref in zip(refs[:count], refs[count:]):
+        out_ref[...] = in_ref[...]
 
 
 def assemble_kernel(n, skip, here_ref, *refs):
@@ -500,7 +514,12 @@
         out_ref[plane, device * size : (device + 1) * size, at : at + grad.shape[1]] = part
 
 
-def ffn_weights_kernel(n, m, here_ref, h_ref, du_ref, g_ref, e_ref, sum_ref, up_ref, down_ref=None):
+def ffn_weights_kernel(n, m, here_ref, du_ref, g_ref, sum_ref, *refs):
+    h_blocks, e_blocks, outs = refs[:n], refs[n : 2 * n], refs[2 * n : -2]
+    h_ref, e_ref = refs[-2:]
+    up_ref, down_ref = outs if len(outs) == 2 else (outs[0], None)
+    join_rows(h_blocks, h_ref)
+    join_rows(e_blocks, e_ref)
     piece = g_ref.shape[1] // m
     low = here_ref[0] % m
     first = h_ref.shape[1] // m if down_ref is None else 0
@@ -591,9 +610,10 @@
         e_ref[i * rows : (i + 1) * rows] = blocks[k][...]
     dk_ref[...] = jnp.zeros_like(dk_ref)
     dv_ref[...] = jnp.zeros_like(dv_ref)
-    step = 2 * rows // split
-
-    @pl.loop(0, n // 2)
+    wide = pairs_at_once(n, rows, split)
+    step = 2 * rows * wide // split
+
+    @pl.loop(0, n // 2 // wide)
     def _(i):
         at = tile_rows(i, step)
         mask = (place_ref[...] >= low_ref[at]) & (place_ref[...] <= high_ref[at])
@@ -619,26 +639,26 @@
     if split > 1:
         return
 
-    @pl.loop(0, n // 2)
+    @pl.loop(0, n // 2 // wide)
     def _(i):
-        at = tile_rows(i, 2 * rows)
+        at = tile_rows(i, step)
         put_slots(
-            even_ref, odd_ref, i, dot_t(dq_ref[at], w_ref[:, :own]) + dot_t(dkv_ref[at], w_ref[:, own : 3 * own])
+            even_ref, odd_ref, i * wide, dot_t(dq_ref[at], w_ref[:, :own]) + dot_t(dkv_ref[at], w_ref[:, own : 3 * own])
         )
 
 
 def place_ffn_kernel(n, m, layers, *refs):
-    up_refs, down_refs = refs[:layers], refs[layers : 2 * layers]
-    up_out, down_out, fc1_out = refs[2 * layers :]
+    up_ref, down_ref, up_out, down_out, fc1_out = refs
     piece = fc1_out.shape[1]
     for layer in range(layers):
-        down_out[layer] = down_refs[layer][:piece].astype(F32)
-        fc1_out[layer : layer + 1] = down_refs[layer][piece : piece + 16, :piece].astype(F32)[:1]
+        down_out[layer] = down_ref[layer, :piece].astype(F32)
+        fc1_out[layer : layer + 1] = down_ref[layer, piece : piece + 16, :piece].astype(F32)[:1]
         for device in range(n):
             high, low = device // m, device % m
             for j in range(m):
                 at = (n * j + m * high + (j + low) % m) * piece
-                block = up_refs[layer][device, :, j * piece : (j + 1) * piece]
+                start = (layer * m + j) * piece
+                block = up_ref[device, :, start : start + piece]
                 up_out[layer, :, at : at + piece] = block.astype(F32)
 
 
@@ -873,12 +893,13 @@
         smem=1,
     )
 
-    def prepare(layer):
+    def prepare(layer, wait=()):
         return call(
             partial(cross_prepare_kernel, col, skip[layer]),
             [w_rest[layer], encoder_all, ev_bias[layer]],
             [like((2 * col, width + source_length), LOW)],
             4 * source_length * width * col,
+            wait=wait,
         )[0]
 
     x = tokens[0]
@@ -887,7 +908,7 @@
     matmul = 2 * length * width
     for layer in range(layers):
         vec = vectors[layer]
-        w_t = after(prepared if layer else prepare(0), h1_slots)
+        w_t = after(prepared if layer else prepare(0, packed[2:] if packs else ()), h1_slots)
         near = gather_near(w_t)
         joined = layer > 0
         h1_all, q, k, v, a, self_lse, *parts = call(
@@ -901,6 +922,8 @@
             + [like((queries, own), LOW), like((queries, own // head_width), F32)]
             + half_slots(width) * joined,
             matmul * 4 * own + 4 * queries * length * own,
+            steps=int(packs),
+            tiles={n + 2: ((width, 3 * own), None)} if packs else None,
         )
         if not joined:
             parts = call(
@@ -924,13 +947,20 @@
             4 * rows * width * (width + source_length),
             smem=1,
         )
-        h3_all, g, slope, even, odd = call(
-            partial(ffn_forward_kernel, n, len(w_ffn[layer])),
-            gather_slots(h3) + [up_bias[layer][None]] + w_ffn[layer],
-            [like((length, width), LOW)] + [like((length, units), LOW)] * 2 + half_slots(width),
+        h3_slots = gather_slots(h3)
+        weight_count = len(w_ffn[layer])
+        first = n + 1 + weight_count
+        tile = 4 * rows
+        g, slope, even, odd = call(
+            partial(ffn_forward_kernel, n, weight_count),
+            h3_slots + [up_bias[layer][None]] + w_ffn[layer],
+            [like((length, units), LOW)] * 2 + half_slots(width),
             2 * matmul * units,
-            scratch=w_scratch,
-            far=len(w_ffn[layer]),
+            scratch=[pltpu.VMEM((length, width), LOW)] + w_scratch,
+            far=weight_count,
+            steps=n // 4,
+            tiles={first + i: ((tile, units), 0) for i in range(2)}
+            | {first + 2 + i: ((2, rows, width), 0) for i in range(2)},
         )
         last = layer == layers - 1
         if last:
@@ -939,7 +969,7 @@
             terms = reduce_slots(even, odd)
         kept.append(
             (x, x1, x2, h1_all, q, k, v, a, self_lse, h2, cq, mixed, cross_lse)
-            + (h3_all, g, slope, wq_t, wo_t, ek_t, ev_t)
+            + (h3_slots, g, slope, wq_t, wo_t, ek_t, ev_t)
         )
         if last:
             continue
@@ -964,26 +994,26 @@
     def to_rows(summed):
         return lax.all_to_all(summed.reshape(n, r, summed.shape[1]), "ctx", 0, 0)
 
-    def move_down(sums):
-        down = sums[0][n * r :] if units == width else sums[1]
-        return lax.ppermute(down, ("ctx", "fsdp"), moves)
-
-    up_rows, down_rows = [None] * layers, [None] * layers
     finish = []
     for layer in reversed(range(layers)):
         x, x1, x2, h1_all, q, k, v, a, self_lse, h2, cq, mixed, cross_lse = kept[layer][:13]
-        h3_all, g, slope, wq_t, wo_t, ek_t, ev_t = kept[layer][13:]
+        h3_slots, g, slope, wq_t, wo_t, ek_t, ev_t = kept[layer][13:]
         vec = vectors[layer]
         if finish:
             slope = after(slope, cross_grad)
-        e3_all, du, fc1_grad, even, odd = call(
-            partial(ffn_backward_kernel, n, len(w_ffn[layer])),
+        weight_count = len(w_ffn[layer])
+        first = n + 1 + weight_count
+        tile = 4 * rows
+        du, fc1_grad, even, odd = call(
+            partial(ffn_backward_kernel, n, weight_count),
             e3_slots + [slope] + w_ffn[layer],
-            [like((length, width), LOW), like((length, units), LOW), like((1, units), F32)]
-            + half_slots(width),
+            [like((length, units), LOW), like((1, units), F32)] + half_slots(width),
             2 * matmul * units,
-            scratch=w_scratch,
-            far=len(w_ffn[layer]),
+            scratch=[pltpu.VMEM((length, width), LOW)] + w_scratch,
+            far=weight_count,
+            steps=n // 4,
+            tiles={n: ((tile, units), 0), first: ((tile, units), 0)}
+            | {first + 2 + i: ((2, rows, width), 0) for i in range(2)},
         )
         terms = reduce_slots(even, odd)
         shapes = [like((m, n * r, units), LOW), like((m, piece + 16, width), LOW)]
@@ -991,12 +1021,15 @@
             shapes = [like((m, n * r + piece + 16, width), LOW)]
         ffn_grads = call(
             partial(ffn_weights_kernel, n, m),
-            [here, h3_all, after(du, terms[0]), g, e3_all, fc1_grad],
+            [here, after(du, terms[0]), g, fc1_grad] + h3_slots + e3_slots,
             shapes,
             2 * matmul * units,
+            scratch=[pltpu.VMEM((length, width), LOW)] * 2,
             smem=1,
         )
         x1 = after(x1, ffn_grads)
+        if layer == 0:
+            result_terms = reduce_slots(*result_parts)
         dx1, e1, e2, dcq, even, odd, sums = call(
             partial(mid_backward_kernel, n, len(terms), head_width),
             [here, grad_x]
@@ -1011,7 +1044,7 @@
             scratch=[pltpu.VMEM((width, source_length), LOW)] * 2,
             smem=1,
         )
-        ffn_sums = [reduce_planes(grad) for grad in after(ffn_grads, dx1)]
+        ffn_sums = [reduce_planes(grad) for grad in after(ffn_grads, dx1 if layer else terms)]
         e1_slots = gather_slots(e1)
         kv_parts = [even, odd]
         even, *odd = call(
@@ -1021,7 +1054,7 @@
             4 * rows * width * width,
             scratch=[pltpu.VMEM((width, width), LOW)] * 2,
             smem=1,
-            wait=[entry[2] for entry in finish[-1:]],
+            wait=[entry[2] for entry in finish[-1:]] + ([] if layer else result_terms[1:]),
         )
         w_terms = reduce_slots(even, list(odd), hold=e1_slots)
         e1_own, dq, dkv, even, odd = call(
@@ -1031,6 +1064,8 @@
             + half_slots(width),
             matmul * 4 * own + 10 * queries * length * own,
             scratch=[pltpu.VMEM((length, own), F32)] * 2,
+            steps=int(packs),
+            tiles={n + 1: ((width, 3 * own), None)} if packs else None,
         )
         if split > 1:
             shaped = dkv.reshape(n // split, split, rows, 2 * own)
@@ -1042,20 +1077,19 @@
             even = even.reshape(n // 2, rows, width)
             odd = jnp.zeros_like(even)
         terms = reduce_slots(even, after(odd, w_terms))
-        beside = []
-        for done in finish if layer == 0 else ():
-            up_rows[done[0]], down_rows[done[0]] = to_rows(done[1][0][: n * r]), move_down(done[1])
-            beside += [up_rows[done[0]], down_rows[done[0]]]
         before = []
         if layer == 0:
-            up_rows[0], down_rows[0] = to_rows(ffn_sums[0][: n * r]), move_down(ffn_sums)
+            sums_of = [ffn_sums] + [done[1] for done in reversed(finish)]
+            up_rows = to_rows(jnp.concatenate([sums[0][: n * r] for sums in sums_of], axis=1))
+            down_rows = [sums[0][n * r :] if units == width else sums[1] for sums in sums_of]
+            down_rows = lax.ppermute(jnp.stack(down_rows), ("ctx", "fsdp"), moves)
+            before = [up_rows, down_rows]
             *ffn_grads, fc1_own = call(
                 partial(place_ffn_kernel, n, m, layers),
-                up_rows + down_rows,
+                [up_rows, down_rows],
                 [like((layers, r, hidden), F32), like((layers, piece, width), F32), like((layers, piece), F32)],
                 layers * r * hidden,
             )
-            before = ffn_grads[:1]
         grad_x, e3, last_sums = call(
             partial(last_backward_kernel, len(terms)),
             [dx1] + terms + [x, vec],
@@ -1078,7 +1112,7 @@
             + [like((n // 2, source_rows, width), F32)] * 2,
             8 * source_length * col * width + matmul * 4 * own,
             smem=1,
-            wait=ffn_sums + beside,
+            wait=ffn_sums,
         )
         if split > 1:
             qkv_grad = t_dot(own_slots(h1_all), jnp.concatenate([dq, dkv], axis=1)).astype(LOW)
@@ -1104,16 +1138,15 @@
         vec_sums[layer] = (summed, jnp.stack(owned))
 
     finish.sort(key=lambda entry: entry[0])
-    result_terms = reduce_slots(*result_parts)
     (result,) = call(
         partial(between_kernel, len(result_terms), True),
         [kept[-1][2]] + result_terms + [vectors[-1]],
         [like((rows, width), LOW)],
         rows * width * 20,
     )
-    enc_grad = total_of(reduce_slots(*after(enc_parts, grad_x), F32))
     summed = jnp.concatenate([pair[0] for pair in vec_sums])
     owned = jnp.concatenate([pair[1] for pair in vec_sums])
+    enc_grad = total_of(reduce_slots(*enc_parts, F32))
     summed = turn(summed, 1).reshape(-1, n, col).transpose(1, 0, 2)
     vec = total_of(reduce_slots(summed[0::2], summed[1::2], F32)) + owned
     (late,) = call(
@@ -1121,16 +1154,16 @@
         [entry[2] for entry in finish],
         [like((n * r, layers * 5 * col), LOW)],
         0,
-        wait=[enc_grad],
+        wait=[up_rows, down_rows],
     )
     late_rows = to_rows(late)
+    (vec,) = call(copy_kernel, [vec], [like(vec.shape, F32)], 0, wait=[late])
     attention_grads = call(
         partial(place_attention_kernel, n, layers),
         [late_rows] + [entry[2] for entry in finish],
         [like((layers, r, parts * width), F32) for parts in (3, 1, 1, 2, 1)],
         layers * r * 8 * width,
     )
-    (vec,) = call(copy_kernel, [vec], [like(vec.shape, F32)], 0, wait=[late])
     vec = sum_planes(vec.reshape(-1, m, col // m).transpose(1, 0, 2))
     vec = vec.reshape(layers, -1, col // m)
     return (

time: 676 us -> 665 us (0.984)
  waiting for transfers between devices: 197 us -> 224 us
  starting transfers between devices: 136 us -> 117 us
  local copies, waits for them, and re-layouts: 52.1 us -> 38.8 us
  Pallas kernels: 235 us -> 224 us
    ppermute x126, waiting for transfers between devices: 179 us -> 213 us  [swap(): return lax.ppermute(values, 'ctx', [(i, i ^ bits) for i in range(count)])]
    convert_element_type x0 -> x10, other arithmetic: none -> 24.4 us  [reduce_slots(): sent = [chip[i].astype(kind) for i in (1, 2, 3)]]
    another operation x10 -> x1, other arithmetic: 20.2 us -> 1.09 us  [on_device(): down_rows = lax.ppermute(jnp.stack(down_rows), ('ctx', 'fsdp'), moves)]
    ppermute x126, starting transfers between devices: 116 us -> 97.3 us  [swap(): return lax.ppermute(values, 'ctx', [(i, i ^ bits) for i in range(count)])]
    pallas_call x33, Pallas kernels: 235 us -> 224 us  [call(): pl.pallas_call(body, grid=(steps,) if steps else (), in_specs=[SMEM] * sm...]
    squeeze x12 -> x0, local copies, waits for them, and re-layouts: 10.1 us -> none  [the longest x10 10.1 us: reduce_slots(): return [chip[0]] + [swap(sent[i], 2 * i + 2) for i in range(3)]]
    unnamed x279 -> x301, local copies, waits for them, and re-layouts: 15.8 us -> 19 us
  transfers between devices with their start and end apart: 143 -> 141, of which waited for: 60 -> 61; matrix products, arithmetic and copies ran while one was open for 9% -> 8% of each run, Pallas kernels for 29% -> 28%
where the time goes in v3:
time: 665 us; the launch traced here: 656 us
  Pallas kernels  224 us (34%)
  waiting for transfers between devices  224 us (34%)
  starting transfers between devices  117 us (18%)
  local copies, waits for them, and re-layouts  38.8 us (6%)
  other arithmetic  36 us (5%)
  between operations  16.8 us (3%)
    pallas_call x33, Pallas kernels, call(): pl.pallas_call(body, grid=(steps,) if steps else (), in_specs=[SMEM] * sm...  224 us
    ppermute x126, waiting for transfers between devices, swap(): return lax.ppermute(values, 'ctx', [(i, i ^ bits) for i in range(count)])  213 us
    ppermute x126, starting transfers between devices, swap(): return lax.ppermute(values, 'ctx', [(i, i ^ bits) for i in range(count)])  97.3 us
    convert_element_type x10, other arithmetic, reduce_slots(): sent = [chip[i].astype(kind) for i in (1, 2, 3)]  24.4 us
    unnamed x301, local copies, waits for them, and re-layouts  19 us
  transfers between devices with their start and end apart: 141, of which 61 were waited for; matrix products, arithmetic and copies ran while one was open for 8% of the time, Pallas kernels for 28%

profile of v3, /device:TPU:0, one launch (start us, length us, event | category | flops | bytes accessed | tf_op | source)
XLA Modules:
  0.0 656.1 jit_solution(13126079176250842954)
XLA Ops:
  34.2 6.3 collective-permute-done.26.refs_2_.refs_14_
  62.2 8.0 %all-gather.7.cloned.1.call-done.refs_0_.refs_10_.refs_9_.refs_11_ = bf16[1024,1280]{1,0:T(8,128)(2,1)} async-done(((bf16[256,1280]{1,0:T(8,128)(2,1)}), bf16[1024,1280]{1,0:T(8,128)(2,1)}) %all-gather.7.cloned.1.call-update) | async-done | bytes 2621456 | tf_op jit(solution)/shard_map/all_gather | solution.py:839
  85.0 12.7 %shard_map.259 = (bf16[1024,1024]{1,0:T(8,128)(2,1)}, bf16[1024,128]{1,0:T(8,128)(2,1)}, bf16[1024,128]{1,0:T(8,128)(2,1)}, bf16[1024,128]{1,0:T(8,128)(2,1)}, b...) custom-call(bf16[160,1024]{1,0:T(8,128)(2,1)} %copy-done.12, bf16[160,1024]{1,0:T(8,128)(2,1)} %copy-done.23, ...), custom_call_target="tpu_custom_call" | custom-call | flops 1610612736 | bytes 8463360 | tf_op jit(solution)/shard_map/pallas_call | solution.py:175
  109.1 6.3 collective-permute-done.14
  136.5 8.0 %shard_map.261 = (f32[128,1024]{1,0:T(8,128)}, f32[128,1024]{1,0:T(8,128)}, bf16[128,1024]{1,0:T(8,128)(2,1)}, bf16[128,1024]{1,0:T(8,128)(2,1)}, bf16[128,1024]...) custom-call(s32[2]{0:T(128)} %pad_add_fusion.refs_0_, ...), custom_call_target="tpu_custom_call" | custom-call | flops 671088640 | bytes 14219272 | tf_op jit(solution)/shard_map/pallas_call | solution.py:175
  160.5 9.8 %shard_map.263 = (bf16[1024,1024]{1,0:T(8,128)(2,1)}, bf16[1024,1024]{1,0:T(8,128)(2,1)}, bf16[4,128,1024]{2,1,0:T(8,128)(2,1)}, bf16[4,128,1024]{2,1,0:T(8,128)(2,1)}) custom-call(bf16[128,1024]{1,0:T(8,128)(2,1)} %get-tuple-element.164.refs_0_.refs_4_, bf16[128,1024]{1,0:T(8,128)(2,1)} %copy-done.110, bf16[128,1024]{1,0:T(8,128)(2,1)} %copy-done.68, ...), custom_call_target="tpu_custom_call" | custom-call | flops 4294967296 | bytes 12587008 | tf_op jit(solution)/shard_map/pallas_call | solution.py:175
  215.2 13.4 %shard_map.266 = (bf16[1024,1024]{1,0:T(8,128)(2,1)}, bf16[1024,128]{1,0:T(8,128)(2,1)}, bf16[1024,128]{1,0:T(8,128)(2,1)}, bf16[1024,128]{1,0:T(8,128)(2,1)}, b...) custom-call(bf16[128,1024]{1,0:T(8,128)(2,1)} %get-tuple-element.169, ...), custom_call_target="tpu_custom_call" | custom-call | flops 1610612736 | bytes 9511936 | tf_op jit(solution)/shard_map/pallas_call | solution.py:175
  233.8 8.3 %collective-permute-done.49 = bf16[128,1280]{1,0:T(8,128)(2,1)S(1)} collective-permute-done((bf16[128,1280]{1,0:T(8,128)(2,1)S(1)}, bf16[128,1280]{1,0:T(8,128)(2,1)S(1)}, u32[]{:S(2)}, u32[]{:S(2)}) %collective-permute-start.49) | collective-permute-done | bytes 327712 | tf_op jit(solution)/shard_map/ppermute | solution.py:23
  261.0 8.3 %shard_map.267 = (f32[128,1024]{1,0:T(8,128)}, f32[128,1024]{1,0:T(8,128)}, bf16[128,1024]{1,0:T(8,128)(2,1)}, bf16[128,1024]{1,0:T(8,128)(2,1)}, bf16[128,1024]...) custom-call(s32[2]{0:T(128)} %pad_add_fusion.refs_0_, ...), custom_call_target="tpu_custom_call" | custom-call | flops 671088640 | bytes 14481416 | tf_op jit(solution)/shard_map/pallas_call | solution.py:175
  286.3 9.8 %shard_map.268 = (bf16[1024,1024]{1,0:T(8,128)(2,1)}, bf16[1024,1024]{1,0:T(8,128)(2,1)}, bf16[4,128,1024]{2,1,0:T(8,128)(2,1)}, bf16[4,128,1024]{2,1,0:T(8,128)(2,1)}) custom-call(bf16[128,1024]{1,0:T(8,128)(2,1)} %get-tuple-element.179.refs_0_.refs_4_, bf16[128,1024]{1,0:T(8,128)(2,1)} %copy-done.115, bf16[128,1024]{1,0:T(8,128)(2,1)} %copy-done.76, ...), custom_call_target="tpu_custom_call" | custom-call | flops 4294967296 | bytes 12587008 | tf_op jit(solution)/shard_map/pallas_call | solution.py:175
  296.9 10.1 %shard_map.270 = (bf16[1024,1024]{1,0:T(8,128)(2,1)}, f32[1,1024]{1,0:T(1,128)}, bf16[4,128,1024]{2,1,0:T(8,128)(2,1)}, bf16[4,128,1024]{2,1,0:T(8,128)(2,1)}) custom-call(bf16[128,1024]{1,0:T(8,128)(2,1)} %bitcast.245, bf16[128,1024]{1,0:T(8,128)(2,1)} %collective-permute-done.65.refs_1_.refs_13_, bf16[128,1024]{1,0:T(8,128)(2,1)} %copy-done.70, ...), custom_call_target="tpu_custom_call" | custom-call | flops 4294967296 | bytes 12587008 | tf_op jit(solution)/shard_map/pallas_call | solution.py:175
  315.7 10.0 %shard_map.271 = bf16[4,528,1024]{2,1,0:T(8,128)(2,1)} custom-call(s32[2]{0:T(128)} %pad_add_fusion.refs_0_, bf16[1024,1024]{1,0:T(8,128)(2,1)} %get-tuple-element.188.refs_1_, bf16[1024,1024]{1,0:T(8,128)(2,1)} %get-tuple-element.189.refs_2_, f32[1,1024]{1,0:T(1,128)} %get-tuple-element.190.refs_3_, bf16[128,1024]{1,0:T(8,128)(2,1)} %get-tuple-element.179.refs_0_.refs_4_, ...), custom_call_target="tpu_custom_call" | custom-call | flops 4294967296 | bytes 12718088 | tf_op jit(solution)/shard_map/pallas_call | solution.py:175
  327.6 10.7 %shard_map.272 = (f32[128,1024]{1,0:T(8,128)}, bf16[128,1024]{1,0:T(8,128)(2,1)}, bf16[128,1024]{1,0:T(8,128)(2,1)}, bf16[128,1024]{1,0:T(8,128)(2,1)}, bf16[4,2...) custom-call(s32[2]{0:T(128)} %pad_add_fusion.refs_0_, bf16[128,1024]{1,0:T(8,128)(2,1)} %bitcast.247, ...), custom_call_target="tpu_custom_call" | custom-call | flops 872415232 | bytes 10582024 | tf_op jit(solution)/shard_map/pallas_call | solution.py:175
  368.2 15.0 %shard_map.274 = (bf16[1024,1024]{1,0:T(8,128)(2,1)}, bf16[1024,128]{1,0:T(8,128)(2,1)}, bf16[1024,256]{1,0:T(8,128)(2,1)}, bf16[4,128,1024]{2,1,0:T(8,128)(2,1)}, bf16[4,128,1024]{2,1,0:T(8,128)(2,1)}) custom-call(bf16[128,1024]{1,0:T(8,128)(2,1)} %get-tuple-element.199.refs_0_, bf16[128,1024]{1,0:T(8,128)(2,1)} %copy-done.123, ...), custom_call_target="tpu_custom_call" | custom-call | flops 2415919104 | bytes 9981952 | tf_op jit(solution)/shard_map/pallas_call | solution.py:175
  383.3 13.0 %collective-permute-done.83.refs_3_ = bf16[256,1280]{1,0:T(8,128)(2,1)S(1)} collective-permute-done((bf16[256,1280]{1,0:T(8,128)(2,1)S(1)}, bf16[256,1280]{1,0:T(8,128)(2,1)S(1)}, u32[]{:S(2)}, u32[]{:S(2)}) %collective-permute-start.83) | collective-permute-done | bytes 655392 | tf_op jit(solution)/shard_map/ppermute | solution.py:23
  429.1 8.2 %shard_map.276 = (bf16[4,256,1024]{2,1,0:T(8,128)(2,1)}, f32[256,1024]{1,0:T(8,128)}, f32[256,1]{1,0:T(8,128)}, f32[4,32,1024]{2,1,0:T(8,128)}, f32[4,32,1024]{2,1,0:T(8,128)}) custom-call(s32[2]{0:T(128)} %pad_add_fusion.refs_0_, f32[256,1280]{1,0:T(8,128)} %get-tuple-element.344.refs_1_, bf16[256,1280]{1,0:T(8,128)(2,1)} %copy-done.35, ...), custom_call_target="tpu_custom_call" | custom-call | flops 1342177280 | bytes 16122888 | tf_op jit(solution)/shard_map/pallas_call | solution.py:175
  446.1 10.1 %shard_map.277 = (bf16[1024,1024]{1,0:T(8,128)(2,1)}, f32[1,1024]{1,0:T(1,128)}, bf16[4,128,1024]{2,1,0:T(8,128)(2,1)}, bf16[4,128,1024]{2,1,0:T(8,128)(2,1)}) custom-call(bf16[128,1024]{1,0:T(8,128)(2,1)} %get-tuple-element.221.refs_0_.refs_12_, bf16[128,1024]{1,0:T(8,128)(2,1)} %copy-done.119, bf16[128,1024]{1,0:T(8,128)(2,1)} %copy-done.74, ...), custom_call_target="tpu_custom_call" | custom-call | flops 4294967296 | bytes 12587008 | tf_op jit(solution)/shard_map/pallas_call | solution.py:175
  464.8 10.0 %shard_map.278 = bf16[4,528,1024]{2,1,0:T(8,128)(2,1)} custom-call(s32[2]{0:T(128)} %pad_add_fusion.refs_0_, bf16[1024,1024]{1,0:T(8,128)(2,1)} %get-tuple-element.236.refs_1_, bf16[1024,1024]{1,0:T(8,128)(2,1)} %get-tuple-element.237.refs_2_, f32[1,1024]{1,0:T(1,128)} %get-tuple-element.238.refs_3_, bf16[128,1024]{1,0:T(8,128)(2,1)} %get-tuple-element.164.refs_0_.refs_4_, ...), custom_call_target="tpu_custom_call" | custom-call | flops 4294967296 | bytes 12718088 | tf_op jit(solution)/shard_map/pallas_call | solution.py:175
  485.1 11.5 %shard_map.279 = (f32[128,1024]{1,0:T(8,128)}, bf16[128,1024]{1,0:T(8,128)(2,1)}, bf16[128,1024]{1,0:T(8,128)(2,1)}, bf16[128,1024]{1,0:T(8,128)(2,1)}, bf16[4,2...) custom-call(s32[2]{0:T(128)} %pad_add_fusion.refs_0_, ...), custom_call_target="tpu_custom_call" | custom-call | flops 872415232 | bytes 10844168 | tf_op jit(solution)/shard_map/pallas_call | solution.py:175
  504.5 7.0 %collective-permute-done.102.refs_2_ = bf16[128,1024]{1,0:T(8,128)(2,1)S(1)} collective-permute-done((bf16[128,1024]{1,0:T(8,128)(2,1)S(1)}, bf16[128,1024]{1,0:T(8,128)(2,1)S(1)}, u32[]{:S(2)}, u32[]{:S(2)}) %collective-permute-start.102) | collective-permute-done | bytes 262176 | tf_op jit(solution)/shard_map/ppermute | solution.py:23
  525.1 15.3 %shard_map.281 = (bf16[1024,1024]{1,0:T(8,128)(2,1)}, bf16[1024,128]{1,0:T(8,128)(2,1)}, bf16[1024,256]{1,0:T(8,128)(2,1)}, bf16[4,128,1024]{2,1,0:T(8,128)(2,1)}, bf16[4,128,1024]{2,1,0:T(8,128)(2,1)}) custom-call(bf16[128,1024]{1,0:T(8,128)(2,1)} %get-tuple-element.247.refs_0_, bf16[128,1024]{1,0:T(8,128)(2,1)} %copy-done.121, ...), custom_call_target="tpu_custom_call" | custom-call | flops 2415919104 | bytes 10768384 | tf_op jit(solution)/shard_map/pallas_call | solution.py:175
  540.4 11.4 %collective-permute-done.112.refs_3_ = bf16[256,1280]{1,0:T(8,128)(2,1)S(1)} collective-permute-done((bf16[256,1280]{1,0:T(8,128)(2,1)S(1)}, bf16[256,1280]{1,0:T(8,128)(2,1)S(1)}, u32[]{:S(2)}, u32[]{:S(2)}) %collective-permute-start.112) | collective-permute-done | bytes 655392 | tf_op jit(solution)/shard_map/ppermute | solution.py:23
  560.1 8.5 %shard_map.283 = (bf16[4,256,1024]{2,1,0:T(8,128)(2,1)}, f32[256,1024]{1,0:T(8,128)}, f32[256,1]{1,0:T(8,128)}, f32[4,32,1024]{2,1,0:T(8,128)}, f32[4,32,1024]{2,1,0:T(8,128)}) custom-call(s32[2]{0:T(128)} %pad_add_fusion.refs_0_, f32[256,1280]{1,0:T(8,128)} %get-tuple-element.342.refs_1_, bf16[256,1280]{1,0:T(8,128)(2,1)} %copy-done.39, ...), custom_call_target="tpu_custom_call" | custom-call | flops 1342177280 | bytes 16909320 | tf_op jit(solution)/shard_map/pallas_call | solution.py:175
  588.9 20.7 %collective-permute-done.115.refs_2_ = bf16[128,1024]{1,0:T(8,128)(2,1)S(1)} collective-permute-done((bf16[128,1024]{1,0:T(8,128)(2,1)}, bf16[128,1024]{1,0:T(8,128)(2,1)S(1)}, u32[]{:S(2)}, u32[]{:S(2)}) %collective-permute-start.115) | collective-permute-done | bytes 262176 | tf_op jit(solution)/shard_map/ppermute | solution.py:23
  (728 shorter events, 387.1 us)
Async XLA Ops:
  7.2 62.9 %all-gather.7.cloned.1.call-start = ((), (), s32[]{:S(2)}) async-start(), calls=%async_computation.7 | async-start | bytes 3276800 | tf_op jit(solution)/shard_map/all_gather | solution.py:839
  12.4 147.4 %all-gather.11.cloned.1.call-start = ((), (), s32[]{:S(2)}) async-start(), calls=%async_computation.13 | async-start | bytes 5242880 | tf_op jit(solution)/shard_map/all_gather | solution.py:839
  75.2 28.4 %collective-permute-start.8 = (bf16[256,1280]{1,0:T(8,128)(2,1)}, bf16[256,1280]{1,0:T(8,128)(2,1)S(1)}, u32[]{:S(2)}, u32[]{:S(2)}) collective-permute-start(bf16[256,1280]{1,0:T(8,128)(2,1)} %shard_map.258.refs_6_), channel_id=1, source_target_pairs={{0,8},{4,12},{8,0},{12,4},{16,24},{20,28},{24,16},{28,20},{1,9},{5... | collective-permute-start | bytes 1966088 | tf_op jit(solution)/shard_map/ppermute | solution.py:23
  76.7 27.0 %collective-permute-start.9 = (bf16[256,1280]{1,0:T(8,128)(2,1)}, bf16[256,1280]{1,0:T(8,128)(2,1)S(1)}, u32[]{:S(2)}, u32[]{:S(2)}) collective-permute-start(bf16[256,1280]{1,0:T(8,128)(2,1)} %shard_map.258.refs_6_), channel_id=1, source_target_pairs={{0,16},{4,20},{8,24},{12,28},{16,0},{20,4},{24,8},{28,12},{1,17},{... | collective-permute-start | bytes 1966088 | tf_op jit(solution)/shard_map/ppermute | solution.py:23
  79.0 19.6 %all-to-all-start = ((bf16[8,128,2,128]{3,2,1,0:T(2,128)(2,1)}), bf16[8,128,2,128]{3,2,1,0:T(2,128)(2,1)S(1)}, u32[]{:S(2)}, u32[]{:S(2)}) async-start(bf16[8,128,2,128]{3,2,1,0:T(2,128)(2,1)} %reshape.481), calls=%async_computation | async-start | bytes 1048576 | tf_op jit(solution)/shard_map/all_to_all | solution.py:845
  82.5 125.2 %all-gather.9.cloned.1.call-start = ((), (), s32[]{:S(2)}) async-start(), calls=%async_computation.8 | async-start | bytes 2293760 | tf_op jit(solution)/shard_map/all_gather | solution.py:839
  105.2 30.5 %collective-permute-start.16 = (bf16[768,1280]{1,0:T(8,128)(2,1)}, bf16[768,1280]{1,0:T(8,128)(2,1)}, u32[]{:S(2)}, u32[]{:S(2)}) collective-permute-start(bf16[768,1280]{1,0:T(8,128)(2,1)} %pad_maximum_fusion), channel_id=1, source_target_pairs={{0,4},{4,0},{8,12},{12,8},{16,20},{20,16},{24,28},{28,24},{1,5},{5... | collective-permute-start | bytes 5898248 | tf_op jit(solution)/shard_map/ppermute | solution.py:23
  107.3 178.2 %all-gather.13.cloned.1.call-start = ((), (), s32[]{:S(2)}) async-start(), calls=%async_computation.14 | async-start | bytes 5242880 | tf_op jit(solution)/shard_map/all_gather | solution.py:839
  170.6 257.5 %reduce-scatter.5.cloned.1.call-start = ((), (), s32[]{:S(2)}) async-start(), calls=%async_computation.9 | async-start | bytes 5406720 | tf_op jit(solution)/shard_map/reduce_scatter | solution.py:120
  230.6 28.5 %collective-permute-start.51 = (bf16[768,1280]{1,0:T(8,128)(2,1)S(1)}, bf16[768,1280]{1,0:T(8,128)(2,1)S(1)}, u32[]{:S(2)}, u32[]{:S(2)}) collective-permute-start(bf16[768,1280]{1,0:T(8,128)(2,1)S(1)} %pad_maximum_fusion.1), channel_id=1, source_target_pairs={{0,4},{4,0},{8,12},{12,8},{16,20},{20,16},{24,28},{28,24},{1,5},{5... | collective-permute-start | bytes 5898248 | tf_op jit(solution)/shard_map/ppermute | solution.py:23
  338.3 158.4 %reduce-scatter.7.cloned.1.call-start = ((), (), s32[]{:S(2)}) async-start(), calls=%async_computation.10 | async-start | bytes 2621440 | tf_op jit(solution)/shard_map/reduce_scatter | solution.py:120
  365.8 30.4 %collective-permute-start.83 = (bf16[256,1280]{1,0:T(8,128)(2,1)S(1)}, bf16[256,1280]{1,0:T(8,128)(2,1)S(1)}, u32[]{:S(2)}, u32[]{:S(2)}) collective-permute-start(bf16[256,1280]{1,0:T(8,128)(2,1)S(1)} %get-tuple-element.217), channel_id=1, source_target_pairs={{0,16},{4,20},{8,24},{12,28},{16,0},{20,4},{24,8},{28,12},{1,17},{... | collective-permute-start | bytes 1966088 | tf_op jit(solution)/shard_map/ppermute | solution.py:23
  366.6 29.6 %collective-permute-start.84 = (bf16[256,1280]{1,0:T(8,128)(2,1)S(1)}, bf16[256,1280]{1,0:T(8,128)(2,1)S(1)}, u32[]{:S(2)}, u32[]{:S(2)}) collective-permute-start(bf16[256,1280]{1,0:T(8,128)(2,1)S(1)} %get-tuple-element.218), channel_id=1, source_target_pairs={{0,24},{4,28},{8,16},{12,20},{16,8},{20,12},{24,0},{28,4},{1,25},{... | collective-permute-start | bytes 1966088 | tf_op jit(solution)/shard_map/ppermute | solution.py:23
  437.3 122.8 %reduce-scatter.9.cloned.1.call-start = ((), (), s32[]{:S(2)}) async-start(), calls=%async_computation.11 | async-start | bytes 5406720 | tf_op jit(solution)/shard_map/reduce_scatter | solution.py:120
  476.9 149.8 %reduce-scatter.11.cloned.1.call-start = ((), (), s32[]{:S(2)}) async-start(), calls=%async_computation.12 | async-start | bytes 2621440 | tf_op jit(solution)/shard_map/reduce_scatter | solution.py:120
  521.5 18.9 %collective-permute-start.111 = (bf16[256,1280]{1,0:T(8,128)(2,1)S(1)}, bf16[256,1280]{1,0:T(8,128)(2,1)S(1)}, u32[]{:S(2)}, u32[]{:S(2)}) collective-permute-start(bf16[256,1280]{1,0:T(8,128)(2,1)S(1)} %get-tuple-element.264), channel_id=1, source_target_pairs={{0,8},{4,12},{8,0},{12,4},{16,24},{20,28},{24,16},{28,20},{1,9},{5... | collective-permute-start | bytes 1966088 | tf_op jit(solution)/shard_map/ppermute | solution.py:23
  522.8 29.1 %collective-permute-start.112 = (bf16[256,1280]{1,0:T(8,128)(2,1)S(1)}, bf16[256,1280]{1,0:T(8,128)(2,1)S(1)}, u32[]{:S(2)}, u32[]{:S(2)}) collective-permute-start(bf16[256,1280]{1,0:T(8,128)(2,1)S(1)} %get-tuple-element.265), channel_id=1, source_target_pairs={{0,16},{4,20},{8,24},{12,28},{16,0},{20,4},{24,8},{28,12},{1,17},{... | collective-permute-start | bytes 1966088 | tf_op jit(solution)/shard_map/ppermute | solution.py:23
  523.9 29.4 %collective-permute-start.113 = (bf16[256,1280]{1,0:T(8,128)(2,1)S(1)}, bf16[256,1280]{1,0:T(8,128)(2,1)S(1)}, u32[]{:S(2)}, u32[]{:S(2)}) collective-permute-start(bf16[256,1280]{1,0:T(8,128)(2,1)S(1)} %get-tuple-element.266), channel_id=1, source_target_pairs={{0,24},{4,28},{8,16},{12,20},{16,8},{20,12},{24,0},{28,4},{1,25},{... | collective-permute-start | bytes 1966088 | tf_op jit(solution)/shard_map/ppermute | solution.py:23
  571.3 40.6 %collective-permute-start.118 = (bf16[2,272,1024]{2,1,0:T(8,128)(2,1)}, bf16[2,272,1024]{2,1,0:T(8,128)(2,1)S(1)}, u32[]{:S(2)}, u32[]{:S(2)}) collective-permute-start(bf16[2,272,1024]{2,1,0:T(8,128)(2,1)} %pad_maximum_fusion.2), channel_id=1, source_target_pairs={{0,0},{1,9},{2,18},{3,27},{4,24},{5,1},{6,10},{7,19},{8,16},{9,25}... | collective-permute-start | bytes 3342344 | tf_op jit(solution)/shard_map/ppermute | solution.py:1085
  574.3 37.6 %all-to-all-start.1 = ((bf16[8,32,2048]{2,1,0:T(8,128)(2,1)}), bf16[8,32,2048]{2,1,0:T(8,128)(2,1)S(1)}, u32[]{:S(2)}, u32[]{:S(2)}) async-start(bf16[8,32,2048]{2,1,0:T(8,128)(2,1)} %pad_maximum_fusion.3), calls=%async_computation.4 | async-start | bytes 2097152 | tf_op jit(solution)/shard_map/all_to_all | solution.py:995
  583.1 26.5 %collective-permute-start.115 = (bf16[128,1024]{1,0:T(8,128)(2,1)}, bf16[128,1024]{1,0:T(8,128)(2,1)S(1)}, u32[]{:S(2)}, u32[]{:S(2)}) collective-permute-start(bf16[128,1024]{1,0:T(8,128)(2,1)} %get-tuple-element.348), channel_id=1, source_target_pairs={{0,8},{4,12},{8,0},{12,4},{16,24},{20,28},{24,16},{28,20},{1,9},{5... | collective-permute-start | bytes 786440 | tf_op jit(solution)/shard_map/ppermute | solution.py:23
  585.4 24.2 %collective-permute-start.116 = (bf16[128,1024]{1,0:T(8,128)(2,1)}, bf16[128,1024]{1,0:T(8,128)(2,1)S(1)}, u32[]{:S(2)}, u32[]{:S(2)}) collective-permute-start(bf16[128,1024]{1,0:T(8,128)(2,1)} %get-tuple-element.347), channel_id=1, source_target_pairs={{0,16},{4,20},{8,24},{12,28},{16,0},{20,4},{24,8},{28,12},{1,17},{... | collective-permute-start | bytes 786440 | tf_op jit(solution)/shard_map/ppermute | solution.py:23
  586.6 25.3 %collective-permute-start.117 = (bf16[128,1024]{1,0:T(8,128)(2,1)}, bf16[128,1024]{1,0:T(8,128)(2,1)}, u32[]{:S(2)}, u32[]{:S(2)}) collective-permute-start(bf16[128,1024]{1,0:T(8,128)(2,1)} %get-tuple-element.346), channel_id=1, source_target_pairs={{0,24},{4,28},{8,16},{12,20},{16,8},{20,12},{24,0},{28,4},{1,25},{... | collective-permute-start | bytes 786440 | tf_op jit(solution)/shard_map/ppermute | solution.py:23
  588.1 34.4 %collective-permute-start.119 = (f32[4,32,1024]{2,1,0:T(8,128)}, f32[4,32,1024]{2,1,0:T(8,128)S(1)}, u32[]{:S(2)}, u32[]{:S(2)}) collective-permute-start(f32[4,32,1024]{2,1,0:T(8,128)} %get-tuple-element.277), channel_id=1, source_target_pairs={{0,4},{4,0},{8,12},{12,8},{16,20},{20,16},{24,28},{28,24},{1,5},{5... | collective-permute-start | bytes 1572872 | tf_op jit(solution)/shard_map/ppermute | solution.py:23
  (256 other events, 1883.0 us)
Sparse Core Ops, SparseCore 0:
  12.6 57.4 all-gather.6
  71.7 79.5 all-gather.10
  152.8 39.9 all-gather.8
  194.2 79.6 all-gather.12
  338.4 77.1 reduce-scatter.4
  437.5 41.9 reduce-scatter.6
  481.9 78.2 reduce-scatter.8
  568.8 44.3 reduce-scatter.10

commit v4 on v3

--- a/solution.py
+++ b/solution.py
@@ -528,9 +528,10 @@
         plane = (low + j) % m
         grad = t_dot(g_ref[:, j * piece : (j + 1) * piece], e_ref[...]).astype(LOW)
         down_ref[plane, first : first + piece] = grad
-        part = sum_ref[:, j * piece : (j + 1) * piece].astype(LOW)
+        part = jnp.broadcast_to(sum_ref[:, j * piece : (j + 1) * piece], (16, piece))
+        top = lax.broadcasted_iota(jnp.int32, (16, piece), 0) == 0
         down_ref[plane, first + piece :] = jnp.zeros((16, down_ref.shape[2]), LOW)
-        down_ref[plane, first + piece : first + piece + 1, :piece] = part
+        down_ref[plane, first + piece :, :piece] = jnp.where(top, part, 0.0).astype(LOW)
     step = min(256, h_ref.shape[1])
     for first in range(0, h_ref.shape[1], step):
         grad = t_dot(h_ref[:, first : first + step], du_ref[...]).astype(LOW)

time: 665 us -> 665 us (level)
  no operation moved by 1% of the time
where the time goes in v4:
time: 665 us; the launch traced here: 656 us
  Pallas kernels  224 us (34%)
  waiting for transfers between devices  224 us (34%)
  starting transfers between devices  117 us (18%)
  local copies, waits for them, and re-layouts  38.8 us (6%)
  other arithmetic  36 us (5%)
  between operations  16.8 us (3%)
    pallas_call x33, Pallas kernels, call(): pl.pallas_call(body, grid=(steps,) if steps else (), in_specs=[SMEM] * sm...  224 us
    ppermute x126, waiting for transfers between devices, swap(): return lax.ppermute(values, 'ctx', [(i, i ^ bits) for i in range(count)])  213 us
    ppermute x126, starting transfers between devices, swap(): return lax.ppermute(values, 'ctx', [(i, i ^ bits) for i in range(count)])  97.3 us
    convert_element_type x10, other arithmetic, reduce_slots(): sent = [chip[i].astype(kind) for i in (1, 2, 3)]  24.4 us
    unnamed x301, local copies, waits for them, and re-layouts  19 us
  transfers between devices with their start and end apart: 141, of which 61 were waited for; matrix products, arithmetic and copies ran while one was open for 8% of the time, Pallas kernels for 28%

profile of v4, /device:TPU:0, one launch (start us, length us, event | category | flops | bytes accessed | tf_op | source)
XLA Modules:
  0.0 656.1 jit_solution(5077529049269545584)
XLA Ops:
  34.2 6.3 collective-permute-done.26.refs_2_.refs_14_
  62.2 8.0 %all-gather.7.cloned.1.call-done.refs_0_.refs_10_.refs_9_.refs_11_ = bf16[1024,1280]{1,0:T(8,128)(2,1)} async-done(((bf16[256,1280]{1,0:T(8,128)(2,1)}), bf16[1024,1280]{1,0:T(8,128)(2,1)}) %all-gather.7.cloned.1.call-update) | async-done | bytes 2621456 | tf_op jit(solution)/shard_map/all_gather | solution.py:840
  85.0 12.7 %shard_map.259 = (bf16[1024,1024]{1,0:T(8,128)(2,1)}, bf16[1024,128]{1,0:T(8,128)(2,1)}, bf16[1024,128]{1,0:T(8,128)(2,1)}, bf16[1024,128]{1,0:T(8,128)(2,1)}, b...) custom-call(bf16[160,1024]{1,0:T(8,128)(2,1)} %copy-done.12, bf16[160,1024]{1,0:T(8,128)(2,1)} %copy-done.23, ...), custom_call_target="tpu_custom_call" | custom-call | flops 1610612736 | bytes 8463360 | tf_op jit(solution)/shard_map/pallas_call | solution.py:175
  109.1 6.3 collective-permute-done.14
  136.5 8.0 %shard_map.261 = (f32[128,1024]{1,0:T(8,128)}, f32[128,1024]{1,0:T(8,128)}, bf16[128,1024]{1,0:T(8,128)(2,1)}, bf16[128,1024]{1,0:T(8,128)(2,1)}, bf16[128,1024]...) custom-call(s32[2]{0:T(128)} %pad_add_fusion.refs_0_, ...), custom_call_target="tpu_custom_call" | custom-call | flops 671088640 | bytes 14219272 | tf_op jit(solution)/shard_map/pallas_call | solution.py:175
  160.5 9.8 %shard_map.263 = (bf16[1024,1024]{1,0:T(8,128)(2,1)}, bf16[1024,1024]{1,0:T(8,128)(2,1)}, bf16[4,128,1024]{2,1,0:T(8,128)(2,1)}, bf16[4,128,1024]{2,1,0:T(8,128)(2,1)}) custom-call(bf16[128,1024]{1,0:T(8,128)(2,1)} %get-tuple-element.164.refs_0_.refs_4_, bf16[128,1024]{1,0:T(8,128)(2,1)} %copy-done.110, bf16[128,1024]{1,0:T(8,128)(2,1)} %copy-done.68, ...), custom_call_target="tpu_custom_call" | custom-call | flops 4294967296 | bytes 12587008 | tf_op jit(solution)/shard_map/pallas_call | solution.py:175
  215.2 13.4 %shard_map.266 = (bf16[1024,1024]{1,0:T(8,128)(2,1)}, bf16[1024,128]{1,0:T(8,128)(2,1)}, bf16[1024,128]{1,0:T(8,128)(2,1)}, bf16[1024,128]{1,0:T(8,128)(2,1)}, b...) custom-call(bf16[128,1024]{1,0:T(8,128)(2,1)} %get-tuple-element.169, ...), custom_call_target="tpu_custom_call" | custom-call | flops 1610612736 | bytes 9511936 | tf_op jit(solution)/shard_map/pallas_call | solution.py:175
  233.8 8.3 %collective-permute-done.49 = bf16[128,1280]{1,0:T(8,128)(2,1)S(1)} collective-permute-done((bf16[128,1280]{1,0:T(8,128)(2,1)S(1)}, bf16[128,1280]{1,0:T(8,128)(2,1)S(1)}, u32[]{:S(2)}, u32[]{:S(2)}) %collective-permute-start.49) | collective-permute-done | bytes 327712 | tf_op jit(solution)/shard_map/ppermute | solution.py:23
  261.0 8.3 %shard_map.267 = (f32[128,1024]{1,0:T(8,128)}, f32[128,1024]{1,0:T(8,128)}, bf16[128,1024]{1,0:T(8,128)(2,1)}, bf16[128,1024]{1,0:T(8,128)(2,1)}, bf16[128,1024]...) custom-call(s32[2]{0:T(128)} %pad_add_fusion.refs_0_, ...), custom_call_target="tpu_custom_call" | custom-call | flops 671088640 | bytes 14481416 | tf_op jit(solution)/shard_map/pallas_call | solution.py:175
  286.3 9.8 %shard_map.268 = (bf16[1024,1024]{1,0:T(8,128)(2,1)}, bf16[1024,1024]{1,0:T(8,128)(2,1)}, bf16[4,128,1024]{2,1,0:T(8,128)(2,1)}, bf16[4,128,1024]{2,1,0:T(8,128)(2,1)}) custom-call(bf16[128,1024]{1,0:T(8,128)(2,1)} %get-tuple-element.179.refs_0_.refs_4_, bf16[128,1024]{1,0:T(8,128)(2,1)} %copy-done.115, bf16[128,1024]{1,0:T(8,128)(2,1)} %copy-done.76, ...), custom_call_target="tpu_custom_call" | custom-call | flops 4294967296 | bytes 12587008 | tf_op jit(solution)/shard_map/pallas_call | solution.py:175
  296.9 10.1 %shard_map.270 = (bf16[1024,1024]{1,0:T(8,128)(2,1)}, f32[1,1024]{1,0:T(1,128)}, bf16[4,128,1024]{2,1,0:T(8,128)(2,1)}, bf16[4,128,1024]{2,1,0:T(8,128)(2,1)}) custom-call(bf16[128,1024]{1,0:T(8,128)(2,1)} %bitcast.245, bf16[128,1024]{1,0:T(8,128)(2,1)} %collective-permute-done.65.refs_1_.refs_13_, bf16[128,1024]{1,0:T(8,128)(2,1)} %copy-done.70, ...), custom_call_target="tpu_custom_call" | custom-call | flops 4294967296 | bytes 12587008 | tf_op jit(solution)/shard_map/pallas_call | solution.py:175
  315.7 10.0 %shard_map.271 = bf16[4,528,1024]{2,1,0:T(8,128)(2,1)} custom-call(s32[2]{0:T(128)} %pad_add_fusion.refs_0_, bf16[1024,1024]{1,0:T(8,128)(2,1)} %get-tuple-element.188.refs_1_, bf16[1024,1024]{1,0:T(8,128)(2,1)} %get-tuple-element.189.refs_2_, f32[1,1024]{1,0:T(1,128)} %get-tuple-element.190.refs_3_, bf16[128,1024]{1,0:T(8,128)(2,1)} %get-tuple-element.179.refs_0_.refs_4_, ...), custom_call_target="tpu_custom_call" | custom-call | flops 4294967296 | bytes 12718088 | tf_op jit(solution)/shard_map/pallas_call | solution.py:175
  327.6 10.7 %shard_map.272 = (f32[128,1024]{1,0:T(8,128)}, bf16[128,1024]{1,0:T(8,128)(2,1)}, bf16[128,1024]{1,0:T(8,128)(2,1)}, bf16[128,1024]{1,0:T(8,128)(2,1)}, bf16[4,2...) custom-call(s32[2]{0:T(128)} %pad_add_fusion.refs_0_, bf16[128,1024]{1,0:T(8,128)(2,1)} %bitcast.247, ...), custom_call_target="tpu_custom_call" | custom-call | flops 872415232 | bytes 10582024 | tf_op jit(solution)/shard_map/pallas_call | solution.py:175
  368.2 15.0 %shard_map.274 = (bf16[1024,1024]{1,0:T(8,128)(2,1)}, bf16[1024,128]{1,0:T(8,128)(2,1)}, bf16[1024,256]{1,0:T(8,128)(2,1)}, bf16[4,128,1024]{2,1,0:T(8,128)(2,1)}, bf16[4,128,1024]{2,1,0:T(8,128)(2,1)}) custom-call(bf16[128,1024]{1,0:T(8,128)(2,1)} %get-tuple-element.199.refs_0_, bf16[128,1024]{1,0:T(8,128)(2,1)} %copy-done.123, ...), custom_call_target="tpu_custom_call" | custom-call | flops 2415919104 | bytes 9981952 | tf_op jit(solution)/shard_map/pallas_call | solution.py:175
  383.3 13.0 %collective-permute-done.83.refs_3_ = bf16[256,1280]{1,0:T(8,128)(2,1)S(1)} collective-permute-done((bf16[256,1280]{1,0:T(8,128)(2,1)S(1)}, bf16[256,1280]{1,0:T(8,128)(2,1)S(1)}, u32[]{:S(2)}, u32[]{:S(2)}) %collective-permute-start.83) | collective-permute-done | bytes 655392 | tf_op jit(solution)/shard_map/ppermute | solution.py:23
  429.1 8.2 %shard_map.276 = (bf16[4,256,1024]{2,1,0:T(8,128)(2,1)}, f32[256,1024]{1,0:T(8,128)}, f32[256,1]{1,0:T(8,128)}, f32[4,32,1024]{2,1,0:T(8,128)}, f32[4,32,1024]{2,1,0:T(8,128)}) custom-call(s32[2]{0:T(128)} %pad_add_fusion.refs_0_, f32[256,1280]{1,0:T(8,128)} %get-tuple-element.344.refs_1_, bf16[256,1280]{1,0:T(8,128)(2,1)} %copy-done.35, ...), custom_call_target="tpu_custom_call" | custom-call | flops 1342177280 | bytes 16122888 | tf_op jit(solution)/shard_map/pallas_call | solution.py:175
  446.1 10.1 %shard_map.277 = (bf16[1024,1024]{1,0:T(8,128)(2,1)}, f32[1,1024]{1,0:T(1,128)}, bf16[4,128,1024]{2,1,0:T(8,128)(2,1)}, bf16[4,128,1024]{2,1,0:T(8,128)(2,1)}) custom-call(bf16[128,1024]{1,0:T(8,128)(2,1)} %get-tuple-element.221.refs_0_.refs_12_, bf16[128,1024]{1,0:T(8,128)(2,1)} %copy-done.119, bf16[128,1024]{1,0:T(8,128)(2,1)} %copy-done.74, ...), custom_call_target="tpu_custom_call" | custom-call | flops 4294967296 | bytes 12587008 | tf_op jit(solution)/shard_map/pallas_call | solution.py:175
  464.8 10.0 %shard_map.278 = bf16[4,528,1024]{2,1,0:T(8,128)(2,1)} custom-call(s32[2]{0:T(128)} %pad_add_fusion.refs_0_, bf16[1024,1024]{1,0:T(8,128)(2,1)} %get-tuple-element.236.refs_1_, bf16[1024,1024]{1,0:T(8,128)(2,1)} %get-tuple-element.237.refs_2_, f32[1,1024]{1,0:T(1,128)} %get-tuple-element.238.refs_3_, bf16[128,1024]{1,0:T(8,128)(2,1)} %get-tuple-element.164.refs_0_.refs_4_, ...), custom_call_target="tpu_custom_call" | custom-call | flops 4294967296 | bytes 12718088 | tf_op jit(solution)/shard_map/pallas_call | solution.py:175
  485.1 11.5 %shard_map.279 = (f32[128,1024]{1,0:T(8,128)}, bf16[128,1024]{1,0:T(8,128)(2,1)}, bf16[128,1024]{1,0:T(8,128)(2,1)}, bf16[128,1024]{1,0:T(8,128)(2,1)}, bf16[4,2...) custom-call(s32[2]{0:T(128)} %pad_add_fusion.refs_0_, ...), custom_call_target="tpu_custom_call" | custom-call | flops 872415232 | bytes 10844168 | tf_op jit(solution)/shard_map/pallas_call | solution.py:175
  504.5 7.0 %collective-permute-done.102.refs_2_ = bf16[128,1024]{1,0:T(8,128)(2,1)S(1)} collective-permute-done((bf16[128,1024]{1,0:T(8,128)(2,1)S(1)}, bf16[128,1024]{1,0:T(8,128)(2,1)S(1)}, u32[]{:S(2)}, u32[]{:S(2)}) %collective-permute-start.102) | collective-permute-done | bytes 262176 | tf_op jit(solution)/shard_map/ppermute | solution.py:23
  525.1 15.3 %shard_map.281 = (bf16[1024,1024]{1,0:T(8,128)(2,1)}, bf16[1024,128]{1,0:T(8,128)(2,1)}, bf16[1024,256]{1,0:T(8,128)(2,1)}, bf16[4,128,1024]{2,1,0:T(8,128)(2,1)}, bf16[4,128,1024]{2,1,0:T(8,128)(2,1)}) custom-call(bf16[128,1024]{1,0:T(8,128)(2,1)} %get-tuple-element.247.refs_0_, bf16[128,1024]{1,0:T(8,128)(2,1)} %copy-done.121, ...), custom_call_target="tpu_custom_call" | custom-call | flops 2415919104 | bytes 10768384 | tf_op jit(solution)/shard_map/pallas_call | solution.py:175
  540.4 11.4 %collective-permute-done.112.refs_3_ = bf16[256,1280]{1,0:T(8,128)(2,1)S(1)} collective-permute-done((bf16[256,1280]{1,0:T(8,128)(2,1)S(1)}, bf16[256,1280]{1,0:T(8,128)(2,1)S(1)}, u32[]{:S(2)}, u32[]{:S(2)}) %collective-permute-start.112) | collective-permute-done | bytes 655392 | tf_op jit(solution)/shard_map/ppermute | solution.py:23
  560.1 8.5 %shard_map.283 = (bf16[4,256,1024]{2,1,0:T(8,128)(2,1)}, f32[256,1024]{1,0:T(8,128)}, f32[256,1]{1,0:T(8,128)}, f32[4,32,1024]{2,1,0:T(8,128)}, f32[4,32,1024]{2,1,0:T(8,128)}) custom-call(s32[2]{0:T(128)} %pad_add_fusion.refs_0_, f32[256,1280]{1,0:T(8,128)} %get-tuple-element.342.refs_1_, bf16[256,1280]{1,0:T(8,128)(2,1)} %copy-done.39, ...), custom_call_target="tpu_custom_call" | custom-call | flops 1342177280 | bytes 16909320 | tf_op jit(solution)/shard_map/pallas_call | solution.py:175
  588.9 20.7 %collective-permute-done.115.refs_2_ = bf16[128,1024]{1,0:T(8,128)(2,1)S(1)} collective-permute-done((bf16[128,1024]{1,0:T(8,128)(2,1)}, bf16[128,1024]{1,0:T(8,128)(2,1)S(1)}, u32[]{:S(2)}, u32[]{:S(2)}) %collective-permute-start.115) | collective-permute-done | bytes 262176 | tf_op jit(solution)/shard_map/ppermute | solution.py:23
  (728 shorter events, 387.1 us)
Async XLA Ops:
  7.2 62.9 %all-gather.7.cloned.1.call-start = ((), (), s32[]{:S(2)}) async-start(), calls=%async_computation.7 | async-start | bytes 3276800 | tf_op jit(solution)/shard_map/all_gather | solution.py:840
  12.4 147.4 %all-gather.11.cloned.1.call-start = ((), (), s32[]{:S(2)}) async-start(), calls=%async_computation.13 | async-start | bytes 5242880 | tf_op jit(solution)/shard_map/all_gather | solution.py:840
  75.2 28.4 %collective-permute-start.8 = (bf16[256,1280]{1,0:T(8,128)(2,1)}, bf16[256,1280]{1,0:T(8,128)(2,1)S(1)}, u32[]{:S(2)}, u32[]{:S(2)}) collective-permute-start(bf16[256,1280]{1,0:T(8,128)(2,1)} %shard_map.258.refs_6_), channel_id=1, source_target_pairs={{0,8},{4,12},{8,0},{12,4},{16,24},{20,28},{24,16},{28,20},{1,9},{5... | collective-permute-start | bytes 1966088 | tf_op jit(solution)/shard_map/ppermute | solution.py:23
  76.7 27.0 %collective-permute-start.9 = (bf16[256,1280]{1,0:T(8,128)(2,1)}, bf16[256,1280]{1,0:T(8,128)(2,1)S(1)}, u32[]{:S(2)}, u32[]{:S(2)}) collective-permute-start(bf16[256,1280]{1,0:T(8,128)(2,1)} %shard_map.258.refs_6_), channel_id=1, source_target_pairs={{0,16},{4,20},{8,24},{12,28},{16,0},{20,4},{24,8},{28,12},{1,17},{... | collective-permute-start | bytes 1966088 | tf_op jit(solution)/shard_map/ppermute | solution.py:23
  79.0 19.6 %all-to-all-start = ((bf16[8,128,2,128]{3,2,1,0:T(2,128)(2,1)}), bf16[8,128,2,128]{3,2,1,0:T(2,128)(2,1)S(1)}, u32[]{:S(2)}, u32[]{:S(2)}) async-start(bf16[8,128,2,128]{3,2,1,0:T(2,128)(2,1)} %reshape.481), calls=%async_computation | async-start | bytes 1048576 | tf_op jit(solution)/shard_map/all_to_all | solution.py:846
  82.5 125.2 %all-gather.9.cloned.1.call-start = ((), (), s32[]{:S(2)}) async-start(), calls=%async_computation.8 | async-start | bytes 2293760 | tf_op jit(solution)/shard_map/all_gather | solution.py:840
  105.2 30.5 %collective-permute-start.16 = (bf16[768,1280]{1,0:T(8,128)(2,1)}, bf16[768,1280]{1,0:T(8,128)(2,1)}, u32[]{:S(2)}, u32[]{:S(2)}) collective-permute-start(bf16[768,1280]{1,0:T(8,128)(2,1)} %pad_maximum_fusion), channel_id=1, source_target_pairs={{0,4},{4,0},{8,12},{12,8},{16,20},{20,16},{24,28},{28,24},{1,5},{5... | collective-permute-start | bytes 5898248 | tf_op jit(solution)/shard_map/ppermute | solution.py:23
  107.3 178.2 %all-gather.13.cloned.1.call-start = ((), (), s32[]{:S(2)}) async-start(), calls=%async_computation.14 | async-start | bytes 5242880 | tf_op jit(solution)/shard_map/all_gather | solution.py:840
  170.6 257.5 %reduce-scatter.5.cloned.1.call-start = ((), (), s32[]{:S(2)}) async-start(), calls=%async_computation.9 | async-start | bytes 5406720 | tf_op jit(solution)/shard_map/reduce_scatter | solution.py:120
  230.6 28.5 %collective-permute-start.51 = (bf16[768,1280]{1,0:T(8,128)(2,1)S(1)}, bf16[768,1280]{1,0:T(8,128)(2,1)S(1)}, u32[]{:S(2)}, u32[]{:S(2)}) collective-permute-start(bf16[768,1280]{1,0:T(8,128)(2,1)S(1)} %pad_maximum_fusion.1), channel_id=1, source_target_pairs={{0,4},{4,0},{8,12},{12,8},{16,20},{20,16},{24,28},{28,24},{1,5},{5... | collective-permute-start | bytes 5898248 | tf_op jit(solution)/shard_map/ppermute | solution.py:23
  338.3 158.4 %reduce-scatter.7.cloned.1.call-start = ((), (), s32[]{:S(2)}) async-start(), calls=%async_computation.10 | async-start | bytes 2621440 | tf_op jit(solution)/shard_map/reduce_scatter | solution.py:120
  365.8 30.4 %collective-permute-start.83 = (bf16[256,1280]{1,0:T(8,128)(2,1)S(1)}, bf16[256,1280]{1,0:T(8,128)(2,1)S(1)}, u32[]{:S(2)}, u32[]{:S(2)}) collective-permute-start(bf16[256,1280]{1,0:T(8,128)(2,1)S(1)} %get-tuple-element.217), channel_id=1, source_target_pairs={{0,16},{4,20},{8,24},{12,28},{16,0},{20,4},{24,8},{28,12},{1,17},{... | collective-permute-start | bytes 1966088 | tf_op jit(solution)/shard_map/ppermute | solution.py:23
  366.6 29.6 %collective-permute-start.84 = (bf16[256,1280]{1,0:T(8,128)(2,1)S(1)}, bf16[256,1280]{1,0:T(8,128)(2,1)S(1)}, u32[]{:S(2)}, u32[]{:S(2)}) collective-permute-start(bf16[256,1280]{1,0:T(8,128)(2,1)S(1)} %get-tuple-element.218), channel_id=1, source_target_pairs={{0,24},{4,28},{8,16},{12,20},{16,8},{20,12},{24,0},{28,4},{1,25},{... | collective-permute-start | bytes 1966088 | tf_op jit(solution)/shard_map/ppermute | solution.py:23
  437.3 122.8 %reduce-scatter.9.cloned.1.call-start = ((), (), s32[]{:S(2)}) async-start(), calls=%async_computation.11 | async-start | bytes 5406720 | tf_op jit(solution)/shard_map/reduce_scatter | solution.py:120
  476.9 149.8 %reduce-scatter.11.cloned.1.call-start = ((), (), s32[]{:S(2)}) async-start(), calls=%async_computation.12 | async-start | bytes 2621440 | tf_op jit(solution)/shard_map/reduce_scatter | solution.py:120
  521.5 18.9 %collective-permute-start.111 = (bf16[256,1280]{1,0:T(8,128)(2,1)S(1)}, bf16[256,1280]{1,0:T(8,128)(2,1)S(1)}, u32[]{:S(2)}, u32[]{:S(2)}) collective-permute-start(bf16[256,1280]{1,0:T(8,128)(2,1)S(1)} %get-tuple-element.264), channel_id=1, source_target_pairs={{0,8},{4,12},{8,0},{12,4},{16,24},{20,28},{24,16},{28,20},{1,9},{5... | collective-permute-start | bytes 1966088 | tf_op jit(solution)/shard_map/ppermute | solution.py:23
  522.8 29.1 %collective-permute-start.112 = (bf16[256,1280]{1,0:T(8,128)(2,1)S(1)}, bf16[256,1280]{1,0:T(8,128)(2,1)S(1)}, u32[]{:S(2)}, u32[]{:S(2)}) collective-permute-start(bf16[256,1280]{1,0:T(8,128)(2,1)S(1)} %get-tuple-element.265), channel_id=1, source_target_pairs={{0,16},{4,20},{8,24},{12,28},{16,0},{20,4},{24,8},{28,12},{1,17},{... | collective-permute-start | bytes 1966088 | tf_op jit(solution)/shard_map/ppermute | solution.py:23
  523.9 29.4 %collective-permute-start.113 = (bf16[256,1280]{1,0:T(8,128)(2,1)S(1)}, bf16[256,1280]{1,0:T(8,128)(2,1)S(1)}, u32[]{:S(2)}, u32[]{:S(2)}) collective-permute-start(bf16[256,1280]{1,0:T(8,128)(2,1)S(1)} %get-tuple-element.266), channel_id=1, source_target_pairs={{0,24},{4,28},{8,16},{12,20},{16,8},{20,12},{24,0},{28,4},{1,25},{... | collective-permute-start | bytes 1966088 | tf_op jit(solution)/shard_map/ppermute | solution.py:23
  571.3 40.6 %collective-permute-start.118 = (bf16[2,272,1024]{2,1,0:T(8,128)(2,1)}, bf16[2,272,1024]{2,1,0:T(8,128)(2,1)S(1)}, u32[]{:S(2)}, u32[]{:S(2)}) collective-permute-start(bf16[2,272,1024]{2,1,0:T(8,128)(2,1)} %pad_maximum_fusion.2), channel_id=1, source_target_pairs={{0,0},{1,9},{2,18},{3,27},{4,24},{5,1},{6,10},{7,19},{8,16},{9,25}... | collective-permute-start | bytes 3342344 | tf_op jit(solution)/shard_map/ppermute | solution.py:1086
  574.3 37.6 %all-to-all-start.1 = ((bf16[8,32,2048]{2,1,0:T(8,128)(2,1)}), bf16[8,32,2048]{2,1,0:T(8,128)(2,1)S(1)}, u32[]{:S(2)}, u32[]{:S(2)}) async-start(bf16[8,32,2048]{2,1,0:T(8,128)(2,1)} %pad_maximum_fusion.3), calls=%async_computation.4 | async-start | bytes 2097152 | tf_op jit(solution)/shard_map/all_to_all | solution.py:996
  583.1 26.5 %collective-permute-start.115 = (bf16[128,1024]{1,0:T(8,128)(2,1)}, bf16[128,1024]{1,0:T(8,128)(2,1)S(1)}, u32[]{:S(2)}, u32[]{:S(2)}) collective-permute-start(bf16[128,1024]{1,0:T(8,128)(2,1)} %get-tuple-element.348), channel_id=1, source_target_pairs={{0,8},{4,12},{8,0},{12,4},{16,24},{20,28},{24,16},{28,20},{1,9},{5... | collective-permute-start | bytes 786440 | tf_op jit(solution)/shard_map/ppermute | solution.py:23
  585.4 24.2 %collective-permute-start.116 = (bf16[128,1024]{1,0:T(8,128)(2,1)}, bf16[128,1024]{1,0:T(8,128)(2,1)S(1)}, u32[]{:S(2)}, u32[]{:S(2)}) collective-permute-start(bf16[128,1024]{1,0:T(8,128)(2,1)} %get-tuple-element.347), channel_id=1, source_target_pairs={{0,16},{4,20},{8,24},{12,28},{16,0},{20,4},{24,8},{28,12},{1,17},{... | collective-permute-start | bytes 786440 | tf_op jit(solution)/shard_map/ppermute | solution.py:23
  586.6 25.3 %collective-permute-start.117 = (bf16[128,1024]{1,0:T(8,128)(2,1)}, bf16[128,1024]{1,0:T(8,128)(2,1)}, u32[]{:S(2)}, u32[]{:S(2)}) collective-permute-start(bf16[128,1024]{1,0:T(8,128)(2,1)} %get-tuple-element.346), channel_id=1, source_target_pairs={{0,24},{4,28},{8,16},{12,20},{16,8},{20,12},{24,0},{28,4},{1,25},{... | collective-permute-start | bytes 786440 | tf_op jit(solution)/shard_map/ppermute | solution.py:23
  588.1 34.4 %collective-permute-start.119 = (f32[4,32,1024]{2,1,0:T(8,128)}, f32[4,32,1024]{2,1,0:T(8,128)S(1)}, u32[]{:S(2)}, u32[]{:S(2)}) collective-permute-start(f32[4,32,1024]{2,1,0:T(8,128)} %get-tuple-element.277), channel_id=1, source_target_pairs={{0,4},{4,0},{8,12},{12,8},{16,20},{20,16},{24,28},{28,24},{1,5},{5... | collective-permute-start | bytes 1572872 | tf_op jit(solution)/shard_map/ppermute | solution.py:23
  (256 other events, 1883.1 us)
Sparse Core Ops, SparseCore 0:
  12.6 57.4 all-gather.6
  71.7 79.5 all-gather.10
  152.8 39.9 all-gather.8
  194.2 79.6 all-gather.12
  338.4 77.1 reduce-scatter.4
  437.5 41.9 reduce-scatter.6
  481.9 78.2 reduce-scatter.8
  568.8 44.3 reduce-scatter.10

commit v5 on v4

--- a/solution.py
+++ b/solution.py
@@ -475,10 +475,12 @@
             out_ref[p, i * size : (i + 1) * size, at : at + width] = block
 
 
-def attention_weights_kernel(n, m, skip, terms, full, here_ref, *refs):
+def attention_weights_kernel(n, m, skip, terms, full, first, last, here_ref, *refs):
     w_refs, refs = refs[:terms], refs[terms:]
     own_refs, refs = (refs[:5], refs[5:]) if full else ((), refs)
-    enc_ref, w_kv_ref, before_ref, out_ref, total_ref, sum_ref, even_ref, odd_ref = refs
+    enc_ref, w_kv_ref, *refs = refs
+    before = 0.0 if first else refs.pop(0)[...]
+    out_ref, total_ref, sum_ref, *halves = refs
     col = w_refs[0].shape[0] // 2
     width = w_kv_ref.shape[0]
     grad = total_of([t[:, :width] for t in w_refs]).astype(LOW)
@@ -488,11 +490,11 @@
     dkv_t = total_of([t[:, width:] for t in w_refs])
     sum_ref[...] = jnp.sum(dkv_t.astype(LOW).astype(F32), axis=1, keepdims=True)
     dkv = dkv_t.T.astype(LOW)
-    total_ref[...] = before_ref[...] + dot_t(dkv, w_kv_ref[:, skip : skip + 2 * col])
+    total_ref[...] = before + dot_t(dkv, w_kv_ref[:, skip : skip + 2 * col])
     put_by_rows(out_ref, t_dot(enc_ref[...], dkv).astype(LOW), 0, width, n, m)
-    for k in range(n):
-        part = total_ref[tile_rows(here_ref[0] ^ k, even_ref.shape[1])]
-        (odd_ref if k % 2 else even_ref)[k // 2] = part
+    for k in range(n if last else 0):
+        half = halves[k % 2]
+        half[k // 2] = total_ref[tile_rows(here_ref[0] ^ k, half.shape[1])]
     if not full:
         return
     h_ref, dq_ref, dkv_ref, a_ref, e_ref = own_refs
@@ -986,7 +988,7 @@
 
     r = width // (n * m)
     grad_x, e3_slots = grad_out[0], last_slots
-    enc_total = jnp.zeros((source_length, width), F32)
+    enc_total = None
     vec_sums = [None] * layers
     moves = [
         (i * m + p, ((n // m) * ((p - i % m) % m) + i // m) * m + p) for i in range(n) for p in range(m)
@@ -1103,14 +1105,24 @@
         hold = (e3_slots[2], e3_slots[4]) if layer else terms[0]
         own_parts = [h1_all, dq, dkv, a, e1_own] if split == 1 else []
         cross_grad, enc_total, ev_sum, *enc_parts = call(
-            partial(attention_weights_kernel, n, m, skip[layer], len(terms), split == 1),
+            partial(
+                attention_weights_kernel,
+                n,
+                m,
+                skip[layer],
+                len(terms),
+                split == 1,
+                layer == layers - 1,
+                layer == 0,
+            ),
             [here]
             + w_terms
             + own_parts
-            + [encoder_all, w_rest[layer], after(enc_total, hold)],
+            + [after(encoder_all, hold), w_rest[layer]]
+            + ([] if enc_total is None else [enc_total]),
             [like((m, n * r, (8 if split == 1 else 4) * col), LOW)]
             + [like((source_length, width), F32), like((2 * col, 1), F32)]
-            + [like((n // 2, source_rows, width), F32)] * 2,
+            + [like((n // 2, source_rows, width), F32)] * (0 if layer else 2),
             8 * source_length * col * width + matmul * 4 * own,
             smem=1,
             wait=ffn_sums,

time: 665 us -> 664 us (level)
  no operation moved by 1% of the time
where the time goes in v5:
time: 664 us; the launch traced here: 655 us
  Pallas kernels  224 us (34%)
  waiting for transfers between devices  224 us (34%)
  starting transfers between devices  117 us (18%)
  local copies, waits for them, and re-layouts  37.6 us (6%)
  other arithmetic  36 us (5%)
  between operations  16.8 us (3%)
    pallas_call x33, Pallas kernels, call(): pl.pallas_call(body, grid=(steps,) if steps else (), in_specs=[SMEM] * sm...  224 us
    ppermute x126, waiting for transfers between devices, swap(): return lax.ppermute(values, 'ctx', [(i, i ^ bits) for i in range(count)])  213 us
    ppermute x126, starting transfers between devices, swap(): return lax.ppermute(values, 'ctx', [(i, i ^ bits) for i in range(count)])  97.3 us
    convert_element_type x10, other arithmetic, reduce_slots(): sent = [chip[i].astype(kind) for i in (1, 2, 3)]  24.4 us
    unnamed x301, local copies, waits for them, and re-layouts  18.9 us
  transfers between devices with their start and end apart: 141, of which 61 were waited for; matrix products, arithmetic and copies ran while one was open for 8% of the time, Pallas kernels for 28%

profile of v5, /device:TPU:0, one launch (start us, length us, event | category | flops | bytes accessed | tf_op | source)
XLA Modules:
  0.0 654.7 jit_solution(11955898298334954913)
XLA Ops:
  34.2 6.3 collective-permute-done.26.refs_2_.refs_14_
  62.2 8.0 %all-gather.7.cloned.1.call-done.refs_0_.refs_10_.refs_9_.refs_11_ = bf16[1024,1280]{1,0:T(8,128)(2,1)} async-done(((bf16[256,1280]{1,0:T(8,128)(2,1)}), bf16[1024,1280]{1,0:T(8,128)(2,1)}) %all-gather.7.cloned.1.call-update) | async-done | bytes 2621456 | tf_op jit(solution)/shard_map/all_gather | solution.py:842
  85.0 12.7 %shard_map.259 = (bf16[1024,1024]{1,0:T(8,128)(2,1)}, bf16[1024,128]{1,0:T(8,128)(2,1)}, bf16[1024,128]{1,0:T(8,128)(2,1)}, bf16[1024,128]{1,0:T(8,128)(2,1)}, b...) custom-call(bf16[160,1024]{1,0:T(8,128)(2,1)} %copy-done.12, bf16[160,1024]{1,0:T(8,128)(2,1)} %copy-done.23, ...), custom_call_target="tpu_custom_call" | custom-call | flops 1610612736 | bytes 8463360 | tf_op jit(solution)/shard_map/pallas_call | solution.py:175
  109.1 6.3 collective-permute-done.14
  136.5 8.0 %shard_map.261 = (f32[128,1024]{1,0:T(8,128)}, f32[128,1024]{1,0:T(8,128)}, bf16[128,1024]{1,0:T(8,128)(2,1)}, bf16[128,1024]{1,0:T(8,128)(2,1)}, bf16[128,1024]...) custom-call(s32[2]{0:T(128)} %pad_add_fusion.refs_0_, ...), custom_call_target="tpu_custom_call" | custom-call | flops 671088640 | bytes 14219272 | tf_op jit(solution)/shard_map/pallas_call | solution.py:175
  160.5 9.8 %shard_map.263 = (bf16[1024,1024]{1,0:T(8,128)(2,1)}, bf16[1024,1024]{1,0:T(8,128)(2,1)}, bf16[4,128,1024]{2,1,0:T(8,128)(2,1)}, bf16[4,128,1024]{2,1,0:T(8,128)(2,1)}) custom-call(bf16[128,1024]{1,0:T(8,128)(2,1)} %get-tuple-element.164.refs_0_.refs_4_, bf16[128,1024]{1,0:T(8,128)(2,1)} %copy-done.110, bf16[128,1024]{1,0:T(8,128)(2,1)} %copy-done.68, ...), custom_call_target="tpu_custom_call" | custom-call | flops 4294967296 | bytes 12587008 | tf_op jit(solution)/shard_map/pallas_call | solution.py:175
  215.2 13.4 %shard_map.266 = (bf16[1024,1024]{1,0:T(8,128)(2,1)}, bf16[1024,128]{1,0:T(8,128)(2,1)}, bf16[1024,128]{1,0:T(8,128)(2,1)}, bf16[1024,128]{1,0:T(8,128)(2,1)}, b...) custom-call(bf16[128,1024]{1,0:T(8,128)(2,1)} %get-tuple-element.169, ...), custom_call_target="tpu_custom_call" | custom-call | flops 1610612736 | bytes 9511936 | tf_op jit(solution)/shard_map/pallas_call | solution.py:175
  233.8 8.3 %collective-permute-done.49 = bf16[128,1280]{1,0:T(8,128)(2,1)S(1)} collective-permute-done((bf16[128,1280]{1,0:T(8,128)(2,1)S(1)}, bf16[128,1280]{1,0:T(8,128)(2,1)S(1)}, u32[]{:S(2)}, u32[]{:S(2)}) %collective-permute-start.49) | collective-permute-done | bytes 327712 | tf_op jit(solution)/shard_map/ppermute | solution.py:23
  261.0 8.3 %shard_map.267 = (f32[128,1024]{1,0:T(8,128)}, f32[128,1024]{1,0:T(8,128)}, bf16[128,1024]{1,0:T(8,128)(2,1)}, bf16[128,1024]{1,0:T(8,128)(2,1)}, bf16[128,1024]...) custom-call(s32[2]{0:T(128)} %pad_add_fusion.refs_0_, ...), custom_call_target="tpu_custom_call" | custom-call | flops 671088640 | bytes 14481416 | tf_op jit(solution)/shard_map/pallas_call | solution.py:175
  286.3 9.8 %shard_map.268 = (bf16[1024,1024]{1,0:T(8,128)(2,1)}, bf16[1024,1024]{1,0:T(8,128)(2,1)}, bf16[4,128,1024]{2,1,0:T(8,128)(2,1)}, bf16[4,128,1024]{2,1,0:T(8,128)(2,1)}) custom-call(bf16[128,1024]{1,0:T(8,128)(2,1)} %get-tuple-element.179.refs_0_.refs_4_, bf16[128,1024]{1,0:T(8,128)(2,1)} %copy-done.115, bf16[128,1024]{1,0:T(8,128)(2,1)} %copy-done.74, ...), custom_call_target="tpu_custom_call" | custom-call | flops 4294967296 | bytes 12587008 | tf_op jit(solution)/shard_map/pallas_call | solution.py:175
  296.9 10.1 %shard_map.270 = (bf16[1024,1024]{1,0:T(8,128)(2,1)}, f32[1,1024]{1,0:T(1,128)}, bf16[4,128,1024]{2,1,0:T(8,128)(2,1)}, bf16[4,128,1024]{2,1,0:T(8,128)(2,1)}) custom-call(bf16[128,1024]{1,0:T(8,128)(2,1)} %bitcast.245, bf16[128,1024]{1,0:T(8,128)(2,1)} %collective-permute-done.65.refs_1_.refs_13_, bf16[128,1024]{1,0:T(8,128)(2,1)} %copy-done.70, ...), custom_call_target="tpu_custom_call" | custom-call | flops 4294967296 | bytes 12587008 | tf_op jit(solution)/shard_map/pallas_call | solution.py:175
  315.7 10.0 %shard_map.271 = bf16[4,528,1024]{2,1,0:T(8,128)(2,1)} custom-call(s32[2]{0:T(128)} %pad_add_fusion.refs_0_, bf16[1024,1024]{1,0:T(8,128)(2,1)} %get-tuple-element.188.refs_1_, bf16[1024,1024]{1,0:T(8,128)(2,1)} %get-tuple-element.189.refs_2_, f32[1,1024]{1,0:T(1,128)} %get-tuple-element.190.refs_3_, bf16[128,1024]{1,0:T(8,128)(2,1)} %get-tuple-element.179.refs_0_.refs_4_, ...), custom_call_target="tpu_custom_call" | custom-call | flops 4294967296 | bytes 12718088 | tf_op jit(solution)/shard_map/pallas_call | solution.py:175
  327.6 10.6 %shard_map.272 = (f32[128,1024]{1,0:T(8,128)}, bf16[128,1024]{1,0:T(8,128)(2,1)}, bf16[128,1024]{1,0:T(8,128)(2,1)}, bf16[128,1024]{1,0:T(8,128)(2,1)}, bf16[4,2...) custom-call(s32[2]{0:T(128)} %pad_add_fusion.refs_0_, bf16[128,1024]{1,0:T(8,128)(2,1)} %bitcast.247, ...), custom_call_target="tpu_custom_call" | custom-call | flops 872415232 | bytes 10582024 | tf_op jit(solution)/shard_map/pallas_call | solution.py:175
  368.2 15.1 %shard_map.274 = (bf16[1024,1024]{1,0:T(8,128)(2,1)}, bf16[1024,128]{1,0:T(8,128)(2,1)}, bf16[1024,256]{1,0:T(8,128)(2,1)}, bf16[4,128,1024]{2,1,0:T(8,128)(2,1)}, bf16[4,128,1024]{2,1,0:T(8,128)(2,1)}) custom-call(bf16[128,1024]{1,0:T(8,128)(2,1)} %get-tuple-element.199.refs_0_, bf16[128,1024]{1,0:T(8,128)(2,1)} %copy-done.123, ...), custom_call_target="tpu_custom_call" | custom-call | flops 2415919104 | bytes 9981952 | tf_op jit(solution)/shard_map/pallas_call | solution.py:175
  383.2 12.9 %collective-permute-done.83.refs_3_ = bf16[256,1280]{1,0:T(8,128)(2,1)S(1)} collective-permute-done((bf16[256,1280]{1,0:T(8,128)(2,1)S(1)}, bf16[256,1280]{1,0:T(8,128)(2,1)S(1)}, u32[]{:S(2)}, u32[]{:S(2)}) %collective-permute-start.83) | collective-permute-done | bytes 655392 | tf_op jit(solution)/shard_map/ppermute | solution.py:23
  427.9 7.9 %shard_map.276 = (bf16[4,256,1024]{2,1,0:T(8,128)(2,1)}, f32[256,1024]{1,0:T(8,128)}, f32[256,1]{1,0:T(8,128)}) custom-call(s32[2]{0:T(128)} %pad_add_fusion.refs_0_, f32[256,1280]{1,0:T(8,128)} %get-tuple-element.344.refs_1_, bf16[256,1280]{1,0:T(8,128)(2,1)} %copy-done.35, bf16[256,1280]{1,0:T(8,128)(2,1)} %copy-done.36, bf16[256,1280]{1,0:T(8,128)(2,1)} %copy-done.37, ...), custom_call_target="tpu_custom_call" | custom-call | flops 1342177280 | bytes 14025736 | tf_op jit(solution)/shard_map/pallas_call | solution.py:175
  444.6 10.1 %shard_map.277 = (bf16[1024,1024]{1,0:T(8,128)(2,1)}, f32[1,1024]{1,0:T(1,128)}, bf16[4,128,1024]{2,1,0:T(8,128)(2,1)}, bf16[4,128,1024]{2,1,0:T(8,128)(2,1)}) custom-call(bf16[128,1024]{1,0:T(8,128)(2,1)} %get-tuple-element.221.refs_0_.refs_12_, bf16[128,1024]{1,0:T(8,128)(2,1)} %copy-done.119, bf16[128,1024]{1,0:T(8,128)(2,1)} %copy-done.75, ...), custom_call_target="tpu_custom_call" | custom-call | flops 4294967296 | bytes 12587008 | tf_op jit(solution)/shard_map/pallas_call | solution.py:175
  463.4 10.0 %shard_map.278 = bf16[4,528,1024]{2,1,0:T(8,128)(2,1)} custom-call(s32[2]{0:T(128)} %pad_add_fusion.refs_0_, bf16[1024,1024]{1,0:T(8,128)(2,1)} %get-tuple-element.236.refs_1_, bf16[1024,1024]{1,0:T(8,128)(2,1)} %get-tuple-element.237.refs_2_, f32[1,1024]{1,0:T(1,128)} %get-tuple-element.238.refs_3_, bf16[128,1024]{1,0:T(8,128)(2,1)} %get-tuple-element.164.refs_0_.refs_4_, ...), custom_call_target="tpu_custom_call" | custom-call | flops 4294967296 | bytes 12718088 | tf_op jit(solution)/shard_map/pallas_call | solution.py:175
  483.6 11.5 %shard_map.279 = (f32[128,1024]{1,0:T(8,128)}, bf16[128,1024]{1,0:T(8,128)(2,1)}, bf16[128,1024]{1,0:T(8,128)(2,1)}, bf16[128,1024]{1,0:T(8,128)(2,1)}, bf16[4,2...) custom-call(s32[2]{0:T(128)} %pad_add_fusion.refs_0_, ...), custom_call_target="tpu_custom_call" | custom-call | flops 872415232 | bytes 10844168 | tf_op jit(solution)/shard_map/pallas_call | solution.py:175
  503.0 7.0 %collective-permute-done.102.refs_2_ = bf16[128,1024]{1,0:T(8,128)(2,1)S(1)} collective-permute-done((bf16[128,1024]{1,0:T(8,128)(2,1)S(1)}, bf16[128,1024]{1,0:T(8,128)(2,1)S(1)}, u32[]{:S(2)}, u32[]{:S(2)}) %collective-permute-start.102) | collective-permute-done | bytes 262176 | tf_op jit(solution)/shard_map/ppermute | solution.py:23
  523.5 15.3 %shard_map.281 = (bf16[1024,1024]{1,0:T(8,128)(2,1)}, bf16[1024,128]{1,0:T(8,128)(2,1)}, bf16[1024,256]{1,0:T(8,128)(2,1)}, bf16[4,128,1024]{2,1,0:T(8,128)(2,1)}, bf16[4,128,1024]{2,1,0:T(8,128)(2,1)}) custom-call(bf16[128,1024]{1,0:T(8,128)(2,1)} %get-tuple-element.247.refs_0_, bf16[128,1024]{1,0:T(8,128)(2,1)} %copy-done.121, ...), custom_call_target="tpu_custom_call" | custom-call | flops 2415919104 | bytes 10768384 | tf_op jit(solution)/shard_map/pallas_call | solution.py:175
  538.8 11.5 %collective-permute-done.112.refs_3_ = bf16[256,1280]{1,0:T(8,128)(2,1)S(1)} collective-permute-done((bf16[256,1280]{1,0:T(8,128)(2,1)S(1)}, bf16[256,1280]{1,0:T(8,128)(2,1)S(1)}, u32[]{:S(2)}, u32[]{:S(2)}) %collective-permute-start.112) | collective-permute-done | bytes 655392 | tf_op jit(solution)/shard_map/ppermute | solution.py:23
  558.7 8.5 %shard_map.283 = (bf16[4,256,1024]{2,1,0:T(8,128)(2,1)}, f32[256,1024]{1,0:T(8,128)}, f32[256,1]{1,0:T(8,128)}, f32[4,32,1024]{2,1,0:T(8,128)}, f32[4,32,1024]{2,1,0:T(8,128)}) custom-call(s32[2]{0:T(128)} %pad_add_fusion.refs_0_, f32[256,1280]{1,0:T(8,128)} %get-tuple-element.342.refs_1_, bf16[256,1280]{1,0:T(8,128)(2,1)} %copy-done.39, ...), custom_call_target="tpu_custom_call" | custom-call | flops 1342177280 | bytes 16909320 | tf_op jit(solution)/shard_map/pallas_call | solution.py:175
  587.4 20.8 %collective-permute-done.115.refs_2_ = bf16[128,1024]{1,0:T(8,128)(2,1)S(1)} collective-permute-done((bf16[128,1024]{1,0:T(8,128)(2,1)}, bf16[128,1024]{1,0:T(8,128)(2,1)S(1)}, u32[]{:S(2)}, u32[]{:S(2)}) %collective-permute-start.115) | collective-permute-done | bytes 262176 | tf_op jit(solution)/shard_map/ppermute | solution.py:23
  (727 shorter events, 385.9 us)
Async XLA Ops:
  7.2 62.9 %all-gather.7.cloned.1.call-start = ((), (), s32[]{:S(2)}) async-start(), calls=%async_computation.7 | async-start | bytes 3276800 | tf_op jit(solution)/shard_map/all_gather | solution.py:842
  12.4 147.4 %all-gather.11.cloned.1.call-start = ((), (), s32[]{:S(2)}) async-start(), calls=%async_computation.13 | async-start | bytes 5242880 | tf_op jit(solution)/shard_map/all_gather | solution.py:842
  75.2 28.4 %collective-permute-start.8 = (bf16[256,1280]{1,0:T(8,128)(2,1)}, bf16[256,1280]{1,0:T(8,128)(2,1)S(1)}, u32[]{:S(2)}, u32[]{:S(2)}) collective-permute-start(bf16[256,1280]{1,0:T(8,128)(2,1)} %shard_map.258.refs_6_), channel_id=1, source_target_pairs={{0,8},{4,12},{8,0},{12,4},{16,24},{20,28},{24,16},{28,20},{1,9},{5... | collective-permute-start | bytes 1966088 | tf_op jit(solution)/shard_map/ppermute | solution.py:23
  76.7 27.0 %collective-permute-start.9 = (bf16[256,1280]{1,0:T(8,128)(2,1)}, bf16[256,1280]{1,0:T(8,128)(2,1)S(1)}, u32[]{:S(2)}, u32[]{:S(2)}) collective-permute-start(bf16[256,1280]{1,0:T(8,128)(2,1)} %shard_map.258.refs_6_), channel_id=1, source_target_pairs={{0,16},{4,20},{8,24},{12,28},{16,0},{20,4},{24,8},{28,12},{1,17},{... | collective-permute-start | bytes 1966088 | tf_op jit(solution)/shard_map/ppermute | solution.py:23
  79.0 19.6 %all-to-all-start = ((bf16[8,128,2,128]{3,2,1,0:T(2,128)(2,1)}), bf16[8,128,2,128]{3,2,1,0:T(2,128)(2,1)S(1)}, u32[]{:S(2)}, u32[]{:S(2)}) async-start(bf16[8,128,2,128]{3,2,1,0:T(2,128)(2,1)} %reshape.481), calls=%async_computation | async-start | bytes 1048576 | tf_op jit(solution)/shard_map/all_to_all | solution.py:848
  82.5 125.2 %all-gather.9.cloned.1.call-start = ((), (), s32[]{:S(2)}) async-start(), calls=%async_computation.8 | async-start | bytes 2293760 | tf_op jit(solution)/shard_map/all_gather | solution.py:842
  105.2 30.5 %collective-permute-start.16 = (bf16[768,1280]{1,0:T(8,128)(2,1)}, bf16[768,1280]{1,0:T(8,128)(2,1)}, u32[]{:S(2)}, u32[]{:S(2)}) collective-permute-start(bf16[768,1280]{1,0:T(8,128)(2,1)} %pad_maximum_fusion), channel_id=1, source_target_pairs={{0,4},{4,0},{8,12},{12,8},{16,20},{20,16},{24,28},{28,24},{1,5},{5... | collective-permute-start | bytes 5898248 | tf_op jit(solution)/shard_map/ppermute | solution.py:23
  107.3 178.2 %all-gather.13.cloned.1.call-start = ((), (), s32[]{:S(2)}) async-start(), calls=%async_computation.14 | async-start | bytes 5242880 | tf_op jit(solution)/shard_map/all_gather | solution.py:842
  170.6 257.4 %reduce-scatter.5.cloned.1.call-start = ((), (), s32[]{:S(2)}) async-start(), calls=%async_computation.9 | async-start | bytes 5406720 | tf_op jit(solution)/shard_map/reduce_scatter | solution.py:120
  230.6 28.5 %collective-permute-start.51 = (bf16[768,1280]{1,0:T(8,128)(2,1)S(1)}, bf16[768,1280]{1,0:T(8,128)(2,1)S(1)}, u32[]{:S(2)}, u32[]{:S(2)}) collective-permute-start(bf16[768,1280]{1,0:T(8,128)(2,1)S(1)} %pad_maximum_fusion.1), channel_id=1, source_target_pairs={{0,4},{4,0},{8,12},{12,8},{16,20},{20,16},{24,28},{28,24},{1,5},{5... | collective-permute-start | bytes 5898248 | tf_op jit(solution)/shard_map/ppermute | solution.py:23
  338.2 157.0 %reduce-scatter.7.cloned.1.call-start = ((), (), s32[]{:S(2)}) async-start(), calls=%async_computation.10 | async-start | bytes 2621440 | tf_op jit(solution)/shard_map/reduce_scatter | solution.py:120
  365.7 30.4 %collective-permute-start.83 = (bf16[256,1280]{1,0:T(8,128)(2,1)S(1)}, bf16[256,1280]{1,0:T(8,128)(2,1)S(1)}, u32[]{:S(2)}, u32[]{:S(2)}) collective-permute-start(bf16[256,1280]{1,0:T(8,128)(2,1)S(1)} %get-tuple-element.217), channel_id=1, source_target_pairs={{0,16},{4,20},{8,24},{12,28},{16,0},{20,4},{24,8},{28,12},{1,17},{... | collective-permute-start | bytes 1966088 | tf_op jit(solution)/shard_map/ppermute | solution.py:23
  366.6 29.6 %collective-permute-start.84 = (bf16[256,1280]{1,0:T(8,128)(2,1)S(1)}, bf16[256,1280]{1,0:T(8,128)(2,1)S(1)}, u32[]{:S(2)}, u32[]{:S(2)}) collective-permute-start(bf16[256,1280]{1,0:T(8,128)(2,1)S(1)} %get-tuple-element.218), channel_id=1, source_target_pairs={{0,24},{4,28},{8,16},{12,20},{16,8},{20,12},{24,0},{28,4},{1,25},{... | collective-permute-start | bytes 1966088 | tf_op jit(solution)/shard_map/ppermute | solution.py:23
  435.9 122.7 %reduce-scatter.9.cloned.1.call-start = ((), (), s32[]{:S(2)}) async-start(), calls=%async_computation.11 | async-start | bytes 5406720 | tf_op jit(solution)/shard_map/reduce_scatter | solution.py:120
  475.4 149.9 %reduce-scatter.11.cloned.1.call-start = ((), (), s32[]{:S(2)}) async-start(), calls=%async_computation.12 | async-start | bytes 2621440 | tf_op jit(solution)/shard_map/reduce_scatter | solution.py:120
  519.9 18.9 %collective-permute-start.111 = (bf16[256,1280]{1,0:T(8,128)(2,1)S(1)}, bf16[256,1280]{1,0:T(8,128)(2,1)S(1)}, u32[]{:S(2)}, u32[]{:S(2)}) collective-permute-start(bf16[256,1280]{1,0:T(8,128)(2,1)S(1)} %get-tuple-element.264), channel_id=1, source_target_pairs={{0,8},{4,12},{8,0},{12,4},{16,24},{20,28},{24,16},{28,20},{1,9},{5... | collective-permute-start | bytes 1966088 | tf_op jit(solution)/shard_map/ppermute | solution.py:23
  521.3 29.0 %collective-permute-start.112 = (bf16[256,1280]{1,0:T(8,128)(2,1)S(1)}, bf16[256,1280]{1,0:T(8,128)(2,1)S(1)}, u32[]{:S(2)}, u32[]{:S(2)}) collective-permute-start(bf16[256,1280]{1,0:T(8,128)(2,1)S(1)} %get-tuple-element.265), channel_id=1, source_target_pairs={{0,16},{4,20},{8,24},{12,28},{16,0},{20,4},{24,8},{28,12},{1,17},{... | collective-permute-start | bytes 1966088 | tf_op jit(solution)/shard_map/ppermute | solution.py:23
  522.3 29.4 %collective-permute-start.113 = (bf16[256,1280]{1,0:T(8,128)(2,1)S(1)}, bf16[256,1280]{1,0:T(8,128)(2,1)S(1)}, u32[]{:S(2)}, u32[]{:S(2)}) collective-permute-start(bf16[256,1280]{1,0:T(8,128)(2,1)S(1)} %get-tuple-element.266), channel_id=1, source_target_pairs={{0,24},{4,28},{8,16},{12,20},{16,8},{20,12},{24,0},{28,4},{1,25},{... | collective-permute-start | bytes 1966088 | tf_op jit(solution)/shard_map/ppermute | solution.py:23
  569.8 40.7 %collective-permute-start.118 = (bf16[2,272,1024]{2,1,0:T(8,128)(2,1)}, bf16[2,272,1024]{2,1,0:T(8,128)(2,1)S(1)}, u32[]{:S(2)}, u32[]{:S(2)}) collective-permute-start(bf16[2,272,1024]{2,1,0:T(8,128)(2,1)} %pad_maximum_fusion.2), channel_id=1, source_target_pairs={{0,0},{1,9},{2,18},{3,27},{4,24},{5,1},{6,10},{7,19},{8,16},{9,25}... | collective-permute-start | bytes 3342344 | tf_op jit(solution)/shard_map/ppermute | solution.py:1088
  572.9 37.7 %all-to-all-start.1 = ((bf16[8,32,2048]{2,1,0:T(8,128)(2,1)}), bf16[8,32,2048]{2,1,0:T(8,128)(2,1)S(1)}, u32[]{:S(2)}, u32[]{:S(2)}) async-start(bf16[8,32,2048]{2,1,0:T(8,128)(2,1)} %pad_maximum_fusion.3), calls=%async_computation.4 | async-start | bytes 2097152 | tf_op jit(solution)/shard_map/all_to_all | solution.py:998
  581.6 26.5 %collective-permute-start.115 = (bf16[128,1024]{1,0:T(8,128)(2,1)}, bf16[128,1024]{1,0:T(8,128)(2,1)S(1)}, u32[]{:S(2)}, u32[]{:S(2)}) collective-permute-start(bf16[128,1024]{1,0:T(8,128)(2,1)} %get-tuple-element.348), channel_id=1, source_target_pairs={{0,8},{4,12},{8,0},{12,4},{16,24},{20,28},{24,16},{28,20},{1,9},{5... | collective-permute-start | bytes 786440 | tf_op jit(solution)/shard_map/ppermute | solution.py:23
  583.9 24.3 %collective-permute-start.116 = (bf16[128,1024]{1,0:T(8,128)(2,1)}, bf16[128,1024]{1,0:T(8,128)(2,1)S(1)}, u32[]{:S(2)}, u32[]{:S(2)}) collective-permute-start(bf16[128,1024]{1,0:T(8,128)(2,1)} %get-tuple-element.347), channel_id=1, source_target_pairs={{0,16},{4,20},{8,24},{12,28},{16,0},{20,4},{24,8},{28,12},{1,17},{... | collective-permute-start | bytes 786440 | tf_op jit(solution)/shard_map/ppermute | solution.py:23
  585.1 25.4 %collective-permute-start.117 = (bf16[128,1024]{1,0:T(8,128)(2,1)}, bf16[128,1024]{1,0:T(8,128)(2,1)}, u32[]{:S(2)}, u32[]{:S(2)}) collective-permute-start(bf16[128,1024]{1,0:T(8,128)(2,1)} %get-tuple-element.346), channel_id=1, source_target_pairs={{0,24},{4,28},{8,16},{12,20},{16,8},{20,12},{24,0},{28,4},{1,25},{... | collective-permute-start | bytes 786440 | tf_op jit(solution)/shard_map/ppermute | solution.py:23
  586.6 34.5 %collective-permute-start.119 = (f32[4,32,1024]{2,1,0:T(8,128)}, f32[4,32,1024]{2,1,0:T(8,128)S(1)}, u32[]{:S(2)}, u32[]{:S(2)}) collective-permute-start(f32[4,32,1024]{2,1,0:T(8,128)} %get-tuple-element.277), channel_id=1, source_target_pairs={{0,4},{4,0},{8,12},{12,8},{16,20},{20,16},{24,28},{28,24},{1,5},{5... | collective-permute-start | bytes 1572872 | tf_op jit(solution)/shard_map/ppermute | solution.py:23
  (256 other events, 1879.8 us)
Sparse Core Ops, SparseCore 0:
  12.6 57.4 all-gather.6
  71.7 79.5 all-gather.10
  152.8 39.9 all-gather.8
  194.2 79.6 all-gather.12
  338.3 77.1 reduce-scatter.4
  436.0 41.9 reduce-scatter.6
  480.4 78.1 reduce-scatter.8
  567.3 44.3 reduce-scatter.10
